TPU v7x, 256 devices: a whole 4x4x8 slice. The times are simulated.
256 devices in a mesh: prow: 16 (over y, x), pcol: 16 (over z, core).
Axes of the slice: x: 4, y: 4, z: 8, core: 2. Of those that a mesh axis runs over, the one named last changes fastest.
Arguments:
- right_side: float32 [19, 16, 32768], P(None, 'pcol', 'prow'), may hold values from -6 to 6
- inverse_rows: float32 [19, 16, 512, 512], P(None, 'pcol', 'prow'), may hold values from -0.25 to 0.25
- panels: float32 [19, 16, 7, 512, 512], P(None, 'pcol', None, 'prow'), may hold values from -0.0625 to 0.0625
- pattern: int32 [19, 16, 7], P(None, 'pcol'), may hold values 0 or 1
- node_sizes: int32 [19, 16], P(None, 'pcol'), may hold values from 256 to 512
- parent: int32 [254], replicated, may hold values from 128 to 254, as said below
Outputs:
- solution: float32 [19, 16, 32768], P(None, 'pcol', 'prow')
Inputs may be any that keep to these rules, and one draw needn't show every extreme that they name: Nodes are numbered level by level from the leaves (128 of them, halving up to one root); entry g is the number of node g's parent, which lies on the next level up, and every node above the leaves has exactly two children.
All inputs are finite; a program needn't handle non-finite values. No bound on the sum of `pattern` on one device may be relied on, other than what follows from the above.
Results may differ from a plain program's by a relative error of at most 0.0001.
Values sent between devices are 32-bit elements; how exact they have to be, the bound alone decides.
No kernel may reach another device: no remote copies, remote signals or barrier semaphores. Data moves between devices by JAX's collectives and lax.ppermute only.
A program may use at most 128 MiB of HBM per device.

v0:
```python
import jax
import jax.numpy as jnp
from jax import lax
from jax.sharding import PartitionSpec as P

LEVELS = 8
LEAVES = 128


def collect_updates(pending, level_slots, col_count):
    shaped = pending.reshape(level_slots, col_count, pending.shape[1])
    return lax.psum_scatter(shaped, "pcol", scatter_dimension=1, tiled=True)[:, 0]


def on_device(right_side, inverse_rows, panels, pattern, node_sizes, parent):
    col_count = lax.axis_size("pcol")
    col_index = lax.axis_index("pcol")
    row_index = lax.axis_index("prow")
    part_rows = panels.shape[3]
    full_rows = panels.shape[4]
    rhs_count = right_side.shape[2] // part_rows
    piece_len = part_rows * rhs_count
    node_counts = [LEAVES >> height for height in range(LEVELS)]
    slot_counts = [max(1, count_here // col_count) for count_here in node_counts]
    pending = {}
    for height in range(1, LEVELS):
        pending[height] = jnp.zeros((slot_counts[height] * col_count, piece_len), jnp.float32)
    row_ids = row_index * part_rows + jnp.arange(part_rows, dtype=jnp.int32)
    full_ids = jnp.arange(full_rows, dtype=jnp.int32)
    outputs = []
    node_base = 0
    slot_base = 0
    for height in range(LEVELS):
        level_nodes = node_counts[height]
        level_slots = slot_counts[height]
        local_nodes = jnp.arange(level_slots, dtype=jnp.int32) * col_count + col_index
        is_real = local_nodes < level_nodes
        node_ids = node_base + jnp.minimum(local_nodes, level_nodes - 1)
        residue = right_side[slot_base : slot_base + level_slots, 0]
        if height > 0:
            residue = residue - collect_updates(pending[height], level_slots, col_count)
        live_limit = node_sizes[slot_base : slot_base + level_slots, 0]
        keep_rows = ((row_ids[None, :] < live_limit[:, None]) & is_real[:, None]).astype(
            jnp.float32
        )
        keep_full = ((full_ids[None, :] < live_limit[:, None]) & is_real[:, None]).astype(
            jnp.float32
        )
        scaled = residue.reshape(level_slots, part_rows, rhs_count) * keep_rows[:, :, None]
        inverse = inverse_rows[slot_base : slot_base + level_slots, 0]
        partial_term = jnp.einsum("nvw,nvq->nwq", inverse, scaled, precision=lax.Precision.HIGHEST)
        partial_term = partial_term.reshape(level_slots, full_rows * rhs_count)
        solved = None
        summed = lax.psum(partial_term, "prow")
        solved = summed.reshape(level_slots, full_rows, rhs_count) * keep_full[:, :, None]
        own_rows = lax.dynamic_slice_in_dim(solved, row_index * part_rows, part_rows, 1)
        outputs.append(own_rows.reshape(level_slots, piece_len))
        reach = LEVELS - 1 - height
        if reach > 0:
            panel_rows = panels[slot_base : slot_base + level_slots, 0, :reach]
            contrib = jnp.einsum(
                "napw,nwq->napq", panel_rows, solved, precision=lax.Precision.HIGHEST
            )
            block_mask = pattern[slot_base : slot_base + level_slots, 0, :reach].astype(
                jnp.float32
            ) * is_real[:, None].astype(jnp.float32)
            contrib = contrib * block_mask[:, :, None, None]
            ancestor = node_ids
            target_base = node_base + level_nodes
            for distance in range(reach):
                ancestor = parent[ancestor]
                target = height + 1 + distance
                target_rows = slot_counts[target] * col_count
                onehot = (
                    (ancestor - target_base)[:, None]
                    == jnp.arange(target_rows, dtype=jnp.int32)[None, :]
                ).astype(jnp.float32)
                addition = jnp.einsum(
                    "nt,nx->tx",
                    onehot,
                    contrib[:, distance].reshape(level_slots, piece_len),
                    precision=lax.Precision.HIGHEST,
                )
                pending[target] = pending[target] + addition
                target_base = target_base + node_counts[target]
        node_base = node_base + level_nodes
        slot_base = slot_base + level_slots
    return jnp.concatenate(outputs, 0)[:, None, :]


def solution(mesh):
    in_specs = (
        P(None, "pcol", "prow"),
        P(None, "pcol", "prow", None),
        P(None, "pcol", None, "prow", None),
        P(None, "pcol", None),
        P(None, "pcol"),
        P(),
    )
    out_specs = P(None, "pcol", "prow")
    return jax.shard_map(
        on_device, mesh=mesh, in_specs=in_specs, out_specs=out_specs, check_vma=False
    )
```

profile of v0, /device:TPU:1, one launch (start us, length us, event | category | flops | bytes accessed | tf_op | source)
XLA Modules:
  0.0 1603.2 jit_solution(3799345065621271661)
XLA Ops:
  8.4 3.2 convolution_bitcast_fusion
  70.3 41.0 %all-reduce.23.cloned.1.call-done = f32[8,512,64]{1,2,0:T(8,128)} async-done(((f32[8,512,64]{1,2,0:T(8,128)}), f32[8,512,64]{1,2,0:T(8,128)}) %all-reduce.23.cloned.1.call-update) | async-done | bytes 1048592 | tf_op jit(solution)/shard_map/psum | solution.py:54
  112.6 5.1 fusion.18
  129.2 100.8 %all-reduce.39.cloned.1.call-done = f32[4,16,2048]{2,0,1:T(4,128)} async-done(((f32[4,16,2048]{2,0,1:T(4,128)}), f32[4,16,2048]{2,0,1:T(4,128)}) %all-reduce.39.cloned.1.call-update) | async-done | bytes 524304
  236.5 91.3 %all-reduce.25.cloned.1.call-done = f32[4,512,64]{1,2,0:T(8,128)} async-done(((f32[4,512,64]{1,2,0:T(8,128)}), f32[4,512,64]{1,2,0:T(8,128)}) %all-reduce.25.cloned.1.call-update) | async-done | bytes 524304 | tf_op jit(solution)/shard_map/psum | solution.py:54
  328.9 2.8 fusion.20
  337.6 107.9 %all-reduce.41.cloned.1.call-done = f32[2,16,2048]{2,0,1:T(2,128)} async-done(((f32[2,16,2048]{2,0,1:T(2,128)}), f32[2,16,2048]{2,0,1:T(2,128)}) %all-reduce.41.cloned.1.call-update) | async-done | bytes 262160
  450.4 92.1 %all-reduce.27.cloned.1.call-done = f32[2,512,64]{1,2,0:T(8,128)} async-done(((f32[2,512,64]{1,2,0:T(8,128)}), f32[2,512,64]{1,2,0:T(8,128)}) %all-reduce.27.cloned.1.call-update) | async-done | bytes 262160 | tf_op jit(solution)/shard_map/psum | solution.py:54
  551.6 105.1 %all-reduce.43.cloned.1.call-done = f32[1,16,2048]{2,1,0:T(8,128)} async-done(((f32[1,16,2048]{2,1,0:T(8,128)}), f32[1,16,2048]{2,1,0:T(8,128)}) %all-reduce.43.cloned.1.call-update) | async-done | bytes 131088
  661.9 1.9 convolution_add_fusion.8
  664.6 88.5 %all-reduce.29.cloned.1.call-done = f32[1,32768]{1,0:T(1,128)} async-done(((f32[1,32768]{1,0:T(1,128)}), f32[1,32768]{1,0:T(1,128)}) %all-reduce.29.cloned.1.call-update) | async-done | bytes 131088 | tf_op jit(solution)/shard_map/psum | solution.py:54
  753.7 2.9 multiply_reduce_fusion.3
  764.2 106.0 %all-reduce.45.cloned.1.call-done = f32[1,16,2048]{2,1,0:T(8,128)} async-done(((f32[1,16,2048]{2,1,0:T(8,128)}), f32[1,16,2048]{2,1,0:T(8,128)}) %all-reduce.45.cloned.1.call-update) | async-done | bytes 131088
  878.8 87.9 %all-reduce.31.cloned.1.call-done = f32[1,32768]{1,0:T(1,128)} async-done(((f32[1,32768]{1,0:T(1,128)}), f32[1,32768]{1,0:T(1,128)}) %all-reduce.31.cloned.1.call-update) | async-done | bytes 131088 | tf_op jit(solution)/shard_map/psum | solution.py:54
  966.6 2.9 multiply_reduce_fusion.2
  976.6 106.5 %all-reduce.47.cloned.1.call-done = f32[1,16,2048]{2,1,0:T(8,128)} async-done(((f32[1,16,2048]{2,1,0:T(8,128)}), f32[1,16,2048]{2,1,0:T(8,128)}) %all-reduce.47.cloned.1.call-update) | async-done | bytes 131088
  1089.7 88.3 %all-reduce.33.cloned.1.call-done = f32[1,32768]{1,0:T(1,128)} async-done(((f32[1,32768]{1,0:T(1,128)}), f32[1,32768]{1,0:T(1,128)}) %all-reduce.33.cloned.1.call-update) | async-done | bytes 131088 | tf_op jit(solution)/shard_map/psum | solution.py:54
  1178.0 2.2 multiply_reduce_fusion.1
  1183.8 107.6 %all-reduce.49.cloned.1.call-done = f32[1,16,2048]{2,1,0:T(8,128)} async-done(((f32[1,16,2048]{2,1,0:T(8,128)}), f32[1,16,2048]{2,1,0:T(8,128)}) %all-reduce.49.cloned.1.call-update) | async-done | bytes 131088
  1295.6 90.5 %all-reduce.35.cloned.1.call-done = f32[1,32768]{1,0:T(1,128)} async-done(((f32[1,32768]{1,0:T(1,128)}), f32[1,32768]{1,0:T(1,128)}) %all-reduce.35.cloned.1.call-update) | async-done | bytes 131088 | tf_op jit(solution)/shard_map/psum | solution.py:54
  1386.1 2.2 multiply_reduce_fusion
  1389.6 1.9 fusion.5
  1392.1 108.1 %all-reduce.51.cloned.1.call-done = f32[1,16,2048]{2,1,0:T(8,128)} async-done(((f32[1,16,2048]{2,1,0:T(8,128)}), f32[1,16,2048]{2,1,0:T(8,128)}) %all-reduce.51.cloned.1.call-update) | async-done | bytes 131088
  1503.1 91.6 %all-reduce.37.cloned.1.call-done = f32[1,512,64]{1,2,0:T(8,128)} async-done(((f32[1,512,64]{1,2,0:T(8,128)}), f32[1,512,64]{1,2,0:T(8,128)}) %all-reduce.37.cloned.1.call-update) | async-done | bytes 131088 | tf_op jit(solution)/shard_map/psum | solution.py:54
  (373 shorter events, 132.5 us)
Async XLA Ops:
  6.5 104.8 %all-reduce.23.cloned.1.call-start = ((), (), s32[]{:S(2)}) async-start(), calls=%async_computation | async-start | bytes 2097152 | tf_op jit(solution)/shard_map/psum | solution.py:54
  11.6 218.3 %all-reduce.39.cloned.1.call-start = ((), (), s32[]{:S(2)}) async-start(), calls=%async_computation.8 | async-start | bytes 1048576
  119.6 208.2 %all-reduce.25.cloned.1.call-start = ((), (), s32[]{:S(2)}) async-start(), calls=%async_computation.1 | async-start | bytes 1048576 | tf_op jit(solution)/shard_map/psum | solution.py:54
  232.9 212.6 %all-reduce.41.cloned.1.call-start = ((), (), s32[]{:S(2)}) async-start(), calls=%async_computation.9 | async-start | bytes 524288
  336.2 206.2 %all-reduce.27.cloned.1.call-start = ((), (), s32[]{:S(2)}) async-start(), calls=%async_computation.2 | async-start | bytes 524288 | tf_op jit(solution)/shard_map/psum | solution.py:54
  448.8 207.8 %all-reduce.43.cloned.1.call-start = ((), (), s32[]{:S(2)}) async-start(), calls=%async_computation.10 | async-start | bytes 262144
  548.3 204.8 %all-reduce.29.cloned.1.call-start = ((), (), s32[]{:S(2)}) async-start(), calls=%async_computation.3 | async-start | bytes 262144 | tf_op jit(solution)/shard_map/psum | solution.py:54
  661.8 208.4 %all-reduce.45.cloned.1.call-start = ((), (), s32[]{:S(2)}) async-start(), calls=%async_computation.11 | async-start | bytes 262144
  761.6 205.1 %all-reduce.31.cloned.1.call-start = ((), (), s32[]{:S(2)}) async-start(), calls=%async_computation.4 | async-start | bytes 262144 | tf_op jit(solution)/shard_map/psum | solution.py:54
  875.4 207.7 %all-reduce.47.cloned.1.call-start = ((), (), s32[]{:S(2)}) async-start(), calls=%async_computation.12 | async-start | bytes 262144
  974.5 203.5 %all-reduce.33.cloned.1.call-start = ((), (), s32[]{:S(2)}) async-start(), calls=%async_computation.5 | async-start | bytes 262144 | tf_op jit(solution)/shard_map/psum | solution.py:54
  974.7 205.7 %copy-start.19 = (f32[2]{0:T(128)S(1)}, f32[2]{0:T(128)}, u32[]{:S(2)}) copy-start(f32[2]{0:T(128)} %multiply_reduce_fusion.6) | copy-start | bytes 28
  976.4 205.2 %copy-start.21 = (s32[2]{0:T(128)S(1)}, s32[2]{0:T(128)}, u32[]{:S(2)}) copy-start(s32[2]{0:T(128)} %broadcast_add_fusion.3) | copy-start | bytes 28
  1085.8 205.6 %copy-start.8 = (f32[19,1,2048]{2,1,0:T(1,128)S(1)}, f32[19,1,2048]{2,1,0:T(1,128)}, u32[]{:S(2)}) copy-start(f32[19,1,2048]{2,1,0:T(1,128)} %param.6) | copy-start | bytes 466948
  1085.8 207.1 %copy-start.18 = (f32[32]{0:T(128)S(1)}, f32[32]{0:T(128)}, u32[]{:S(2)}) copy-start(f32[32]{0:T(128)} %and_convert_fusion.3) | copy-start | bytes 388
  1086.7 204.7 %all-reduce.49.cloned.1.call-start = ((), (), s32[]{:S(2)}) async-start(), calls=%async_computation.13 | async-start | bytes 262144
  1182.8 203.3 %all-reduce.35.cloned.1.call-start = ((), (), s32[]{:S(2)}) async-start(), calls=%async_computation.6 | async-start | bytes 262144 | tf_op jit(solution)/shard_map/psum | solution.py:54
  1294.4 205.8 %all-reduce.51.cloned.1.call-start = ((), (), s32[]{:S(2)}) async-start(), calls=%async_computation.14 | async-start | bytes 262144
  1295.3 206.5 %copy-start.17 = (f32[32]{0:T(128)S(1)}, f32[32]{0:T(128)}, u32[]{:S(2)}) copy-start(f32[32]{0:T(128)} %and_convert_fusion.2) | copy-start | bytes 388
  1295.4 207.4 %copy-start.23 = (f32[32]{0:T(128)S(1)}, f32[32]{0:T(128)}, u32[]{:S(2)}) copy-start(f32[32]{0:T(128)} %dynamic-slice.46) | copy-start | bytes 388
  1295.4 207.4 %copy-start.24 = (f32[32]{0:T(128)S(1)}, f32[32]{0:T(128)}, u32[]{:S(2)}) copy-start(f32[32]{0:T(128)} %dynamic-slice.47) | copy-start | bytes 388
  1295.6 299.2 %copy-start.22 = (f32[32]{0:T(128)S(1)}, f32[32]{0:T(128)}, u32[]{:S(2)}) copy-start(f32[32]{0:T(128)} %dynamic-slice.48) | copy-start | bytes 388
  1295.6 300.2 %copy-start.7 = (f32[8,2048]{1,0:T(8,128)S(1)}, f32[8,2048]{1,0:T(8,128)}, u32[]{:S(2)}) copy-start(f32[8,2048]{1,0:T(8,128)} %reshape.1921) | copy-start | bytes 196612
  1391.6 203.2 %all-reduce.37.cloned.1.call-start = ((), (), s32[]{:S(2)}) async-start(), calls=%async_computation.7 | async-start | bytes 262144 | tf_op jit(solution)/shard_map/psum | solution.py:54
  (33 other events, 3533.6 us)
Sparse Core Ops, SparseCore 0:
  11.8 99.4 all-reduce.22
  119.7 110.1 all-reduce.38
  233.4 94.3 all-reduce.24
  336.3 109.1 all-reduce.40
  448.9 93.4 all-reduce.26
  548.5 108.1 all-reduce.42
  661.9 91.1 all-reduce.28
  761.7 108.4 all-reduce.44
  875.5 91.1 all-reduce.30
  974.6 108.4 all-reduce.46
  1086.8 91.1 all-reduce.32
  1182.9 108.4 all-reduce.48
  1294.9 91.1 all-reduce.34
  1391.7 108.4 all-reduce.50
  1503.6 91.1 all-reduce.36
where the time goes:
time: 1610 us; the launch traced here: 1600 us
  waiting for transfers between devices  1410 us (88%)
  local copies, waits for them, and re-layouts  54.2 us (3%)
  other arithmetic  51.9 us (3%)
  matrix products  50.7 us (3%)
  between operations  32.3 us (2%)
    unnamed x22, waiting for transfers between devices  742 us
    psum x8, waiting for transfers between devices, on_device(): summed = lax.psum(partial_term, 'prow')  671 us
  transfers between devices with their start and end apart: 15, of which 15 were waited for; matrix products, arithmetic and copies ran while one was open for 5% of the time, Pallas kernels for 0%

commit v1 on v0

v1 whole, which is shorter than its diff:
```python
import functools

import jax
import jax.numpy as jnp
from jax import lax
from jax.experimental import pallas as pl
from jax.experimental.pallas import tpu as pltpu
from jax.sharding import PartitionSpec as P

LEVELS = 8
LEAVES = 128
GATHER_FROM = 1
VMEM_LIMIT = 24 * 1024 * 1024

NODES = [LEAVES >> h for h in range(LEVELS)]
NODE_BASE = [2 * LEAVES - 2 * (LEAVES >> h) for h in range(LEVELS)]


def split(x):
    high = x.astype(jnp.bfloat16)
    low = (x - high.astype(jnp.float32)).astype(jnp.bfloat16)
    return high, low


def dot3(a, b, dims):
    ah, al = split(a)
    bh, bl = split(b)
    dot = functools.partial(
        lax.dot_general, dimension_numbers=(dims, ((), ())), preferred_element_type=jnp.float32
    )
    return dot(ah, bh) + (dot(ah, bl) + dot(al, bh))


def unfold(x, scratch):
    n = x.shape[0]
    scratch[pl.ds(0, n, stride=2), :] = x
    scratch[pl.ds(1, n, stride=2), :] = pltpu.roll(x, 64, 1)
    return scratch[pl.ds(0, 2 * n), :][:, :64]


def fold(x, scratch):
    n = x.shape[0] // 2
    scratch[pl.ds(0, 2 * n), :] = jnp.concatenate([x, x], 1)
    even = scratch[pl.ds(0, n, stride=2), :]
    odd = scratch[pl.ds(1, n, stride=2), :]
    lane = lax.broadcasted_iota(jnp.int32, (n, 128), 1)
    return jnp.where(lane < 64, even, odd)


def own_mask(pos, sizes, slot, local, nodes):
    row = lax.broadcasted_iota(jnp.int32, (16, 128), 0)
    lane = lax.broadcasted_iota(jnp.int32, (16, 128), 1)
    row_id = pos[0] * 32 + 2 * row + (lane >= 64).astype(jnp.int32)
    limit = jnp.where(local * 16 + pos[1] < nodes, sizes[slot], 0)
    return row_id < limit


def residue_kernel(height, slots, slot_base, pos, parent, pattern, sizes, recv, rhs, out):
    for s in range(slots):
        total = recv[0, s]
        for i in range(1, 16):
            total = total + recv[i, s]
        keep = own_mask(pos, sizes, slot_base + s, s, NODES[height])
        z = jnp.where(keep, rhs[s] - total, 0.0)
        for i in range(16):
            out[i, s] = z


def partial_kernel(height, slots, slot_base, pos, parent, pattern, sizes, *refs):
    recv = None
    if height > 0:
        recv, *refs = refs
    rhs, inverse, out, scratch = refs
    s = pl.program_id(0)
    z = rhs[0]
    if recv is not None:
        total = recv[0, 0]
        for i in range(1, 16):
            total = total + recv[i, 0]
        z = z - total
    keep = own_mask(pos, sizes, slot_base + s, s, NODES[height])
    z = jnp.where(keep, z, 0.0)
    z = unfold(z, scratch)
    part = dot3(inverse[0, 0], z, ((0,), (0,)))
    out[:, 0] = fold(part, scratch).reshape(16, 16, 128)


def solved_kernel(height, slots, slot_base, pos, parent, pattern, sizes, recv, out, sol):
    for s in range(slots):
        total = recv[0, s]
        for i in range(1, 16):
            total = total + recv[i, s]
        keep = own_mask(pos, sizes, slot_base + s, s, NODES[height])
        y = jnp.where(keep, total, 0.0)
        sol[s] = y
        for i in range(16):
            out[i, s] = y


def spread_kernel(height, slots, slot_base, whole, pos, parent, pattern, sizes, *refs):
    reach = LEVELS - 1 - height
    refs = list(refs)
    gathered = refs.pop(0)
    inverse = refs.pop(0) if whole else None
    panels = refs.pop(0) if reach else None
    before = [refs.pop(0) for _ in range(reach)] if height > 0 else []
    sol = refs.pop(0) if whole else None
    after = [refs.pop(0) for _ in range(reach)]
    scratch = refs.pop(0)
    s = pl.program_id(0)

    @pl.when(s == 0)
    def _():
        for i, ref in enumerate(after):
            ref[...] = before[i][...] if before else jnp.zeros_like(ref)

    x = unfold(gathered[:, 0].reshape(256, 128), scratch)
    slot = slot_base + s
    if whole:
        y_t = dot3(x.T, inverse[:, 0].reshape(512, 512), ((1,), (0,)))
        limit = sizes[slot]
        y_t = jnp.where(lax.broadcasted_iota(jnp.int32, (64, 512), 1) < limit, y_t, 0.0)
        y = y_t.T
        scratch[...] = jnp.concatenate([y, y], 1)
        own = scratch[pl.ds(pl.multiple_of(pos[0] * 32, 32), 32), :]
        sol[0] = fold(own[:, :64], scratch)
    else:
        y_t = x.T
    if reach:
        block = panels[0, 0].reshape(reach * 32, 512)
        update = fold(dot3(block, y_t, ((1,), (1,))), scratch)
        node = NODE_BASE[height] + jnp.minimum(s * 16 + pos[1], NODES[height] - 1)
        for d in range(reach):
            node = parent[node]
            target = height + 1 + d
            j = node - NODE_BASE[target]
            where = (j % 16) * max(1, NODES[target] // 16) + j // 16
            scale = pattern[slot * 7 + d].astype(jnp.float32)
            after[d][where] += scale * update[d * 16 : (d + 1) * 16]


def on_device(right_side, inverse_rows, panels, pattern, node_sizes, parent):
    pos = jnp.stack([lax.axis_index("prow"), lax.axis_index("pcol")]).astype(jnp.int32)
    rhs = right_side.reshape(19, 16, 128)
    scalars = (pos, parent, pattern.reshape(-1), node_sizes.reshape(-1))
    slot_counts = [max(1, n // 16) for n in NODES]
    bases = [sum(slot_counts[:h]) for h in range(LEVELS)]
    first = bases[GATHER_FROM]
    cuts = [first, bases[min(GATHER_FROM + 1, LEVELS - 1)], 19]
    inverses = []
    for lo, hi in zip(cuts[:-1], cuts[1:]):
        inverses.append((lo, lax.all_gather(inverse_rows[lo:hi, 0], "prow", axis=0)))

    def call(kernel, scratch, grid, in_specs, out_specs, out_shape, aliases, *args):
        return pl.pallas_call(
            kernel,
            grid_spec=pltpu.PrefetchScalarGridSpec(
                num_scalar_prefetch=4,
                grid=grid,
                in_specs=in_specs,
                out_specs=out_specs,
                scratch_shapes=[pltpu.VMEM((512, 128), jnp.float32)] if scratch else [],
            ),
            out_shape=out_shape,
            input_output_aliases={k + 4: v for k, v in aliases.items()},
            compiler_params=pltpu.CompilerParams(vmem_limit_bytes=VMEM_LIMIT),
        )(*scalars, *args)

    def exchange(x, axis):
        return lax.all_to_all(x, axis, 0, 0, tiled=True)

    f32 = jnp.float32
    pending = []
    recv = None
    outputs = []
    for height in range(LEVELS):
        count = slot_counts[height]
        base = bases[height]
        reach = LEVELS - 1 - height
        info = (height, count, base)
        whole = height >= GATHER_FROM
        piece = jax.ShapeDtypeStruct((16, count, 16, 128), f32)
        own = jax.ShapeDtypeStruct((count, 16, 128), f32)
        every = pl.BlockSpec((16, count, 16, 128), lambda *_: (0, 0, 0, 0))
        every_own = pl.BlockSpec((count, 16, 128), lambda *_: (0, 0, 0))
        one = pl.BlockSpec((16, 1, 16, 128), lambda s, *_: (0, s, 0, 0))
        rhs_all = pl.BlockSpec((count, 16, 128), lambda *_, b=base // count: (b, 0, 0))
        if whole:
            z = call(
                functools.partial(residue_kernel, *info), False, (1,), [every, rhs_all], every, piece, {}, recv, rhs
            )
            gathered = exchange(z, "prow")
        else:
            in_specs = [
                pl.BlockSpec((1, 16, 128), lambda s, *_, b=base: (b + s, 0, 0)),
                pl.BlockSpec((1, 1, 32, 512), lambda s, *_, b=base: (b + s, 0, 0, 0)),
            ]
            args = [rhs, inverse_rows]
            if height > 0:
                in_specs, args = [one] + in_specs, [recv] + args
            parts = call(functools.partial(partial_kernel, *info), True, (count,), in_specs, one, piece, {}, *args)
            parts = exchange(parts, "prow")
            y, sol = call(
                functools.partial(solved_kernel, *info), False, (1,), [every], [every, every_own], [piece, own], {}, parts
            )
            outputs.append(sol)
            gathered = exchange(y, "prow")
        in_specs, args = [one], [gathered]
        out_specs, out_shape = [], []
        if whole:
            lo, inverse = [pair for pair in inverses if pair[0] <= base][-1]
            in_specs.append(pl.BlockSpec((16, 1, 32, 512), lambda s, *_, b=base - lo: (0, b + s, 0, 0)))
            args.append(inverse)
            out_specs.append(pl.BlockSpec((1, 16, 128), lambda s, *_: (s, 0, 0)))
            out_shape.append(own)
        if reach:
            in_specs.append(
                pl.BlockSpec((1, 1, reach, 32, 512), lambda s, *_, b=base: (b + s, 0, 0, 0, 0))
            )
            args.append(panels)
        aliases = {}
        for d in range(reach):
            shape = (16 * slot_counts[height + 1 + d], 16, 128)
            spec = pl.BlockSpec(shape, lambda *_: (0, 0, 0))
            if height > 0:
                aliases[len(in_specs)] = len(out_specs)
                in_specs.append(spec)
                args.append(pending[d])
            out_specs.append(spec)
            out_shape.append(jax.ShapeDtypeStruct(shape, f32))
        results = call(
            functools.partial(spread_kernel, *info, whole), True, (count,), in_specs, out_specs, out_shape, aliases, *args
        )
        results = list(results)
        if whole:
            outputs.append(results.pop(0))
        if reach:
            following = slot_counts[height + 1]
            recv = exchange(results[0].reshape(16, following, 16, 128), "pcol")
            pending = results[1:]
    return jnp.concatenate(outputs, 0).reshape(19, 1, 2048)


def solution(mesh):
    in_specs = (
        P(None, "pcol", "prow"),
        P(None, "pcol", "prow", None),
        P(None, "pcol", None, "prow", None),
        P(None, "pcol", None),
        P(None, "pcol"),
        P(),
    )
    out_specs = P(None, "pcol", "prow")
    return jax.shard_map(
        on_device, mesh=mesh, in_specs=in_specs, out_specs=out_specs, check_vma=False
    )
```

time: 1610 us -> 329 us (0.20)
  waiting for transfers between devices: 1410 us -> 24 us
  blocking collectives: 0 us -> 205 us
  other arithmetic: 51.9 us -> 0.08 us
  matrix products: 50.7 us -> 0 us
  Pallas kernels: 0 us -> 40 us
  local copies, waits for them, and re-layouts: 54.2 us -> 33.9 us
  between operations: 32.3 us -> 13.6 us
    unnamed x22 -> x2, waiting for transfers between devices: 742 us -> 0.03 us
    psum x8 -> x0, waiting for transfers between devices: 671 us -> none  [on_device(): summed = lax.psum(partial_term, 'prow')]
    all_to_all x0 -> x13, blocking collectives: none -> 205 us  [exchange(): return lax.all_to_all(x, axis, 0, 0, tiled=True)]
    dot_general x33 -> x0, matrix products: 50.7 us -> none  [the longest x18 23.6 us: on_device(): jnp.einsum('nt,nx->tx', onehot, contrib[:, distance].reshape(level_slots,...]
    pallas_call x0 -> x16, Pallas kernels: none -> 40 us  [call(): pl.pallas_call(kernel, grid_spec=pltpu.PrefetchScalarGridSpec(num_scalar_...]
    unnamed x84 -> x44, local copies, waits for them, and re-layouts: 1.09 us -> 27.7 us
    all_to_all x0 -> x3, waiting for transfers between devices: none -> 23.9 us  [exchange(): return lax.all_to_all(x, axis, 0, 0, tiled=True)]
    sub x25 -> x0, other arithmetic: 19 us -> none  [the longest x7 10.2 us: on_device(): residue = residue - collect_updates(pending[height], level_slots, col_count)]
  transfers between devices with their start and end apart: 15 -> 5, of which waited for: 15 -> 3; matrix products, arithmetic and copies ran while one was open for 5% -> 1% of each run, Pallas kernels for 0% -> 6%
where the time goes in v1:
time: 329 us; the launch traced here: 327 us
  blocking collectives  205 us (62%)
  Pallas kernels  40 us (12%)
  local copies, waits for them, and re-layouts  33.9 us (10%)
  waiting for transfers between devices  24 us (7%)
  between operations  13.6 us (4%)
  starting transfers between devices  11.2 us (3%)
    all_to_all x13, blocking collectives, exchange(): return lax.all_to_all(x, axis, 0, 0, tiled=True)  205 us
    pallas_call x16, Pallas kernels, call(): pl.pallas_call(kernel, grid_spec=pltpu.PrefetchScalarGridSpec(num_scalar_...  40 us
    unnamed x44, local copies, waits for them, and re-layouts  27.7 us
    all_to_all x3, waiting for transfers between devices, exchange(): return lax.all_to_all(x, axis, 0, 0, tiled=True)  23.9 us
    all_to_all x3, starting transfers between devices, exchange(): return lax.all_to_all(x, axis, 0, 0, tiled=True)  11.1 us
  transfers between devices with their start and end apart: 5, of which 3 were waited for; matrix products, arithmetic and copies ran while one was open for 1% of the time, Pallas kernels for 6%

profile of v1, /device:TPU:1, one launch (start us, length us, event | category | flops | bytes accessed | tf_op | source)
XLA Modules:
  0.0 327.3 jit_solution(7374438920710513252)
XLA Ops:
  14.7 4.1 %shard_map.64 = f32[16,8,16,128]{3,2,1,0:T(8,128)S(1)} custom-call(s32[2]{0:T(128)S(1)} %pad_add_fusion.pos, s32[254]{0:T(256)S(1)} %copy-done.10, s32[133]{0:T(256)S(1)} %reshape.33.pattern, s32[19]{0:T(128)S(1)} %bitcast.39, f32[19,16,128]{2,1,0:T(8,128)S(1)} %bitcast.24, f32[19,1,32,512]{3,2,1,0:T(8,128)S(1)} %copy-done.9), custom_call_target="tpu_custom_call" | custom-call | tf_op jit(solution)/shard_map/pallas_call | solution.py:155
  18.8 28.6 %all_to_all.80.recv = f32[16,8,16,128]{3,2,1,0:T(8,128)S(1)} all-to-all(f32[16,8,16,128]{3,2,1,0:T(8,128)S(1)} %shard_map.64), channel_id=1, replica_groups=mesh['prow'=16,'pcol'=16] {'prow'}, dimensions={0} | all-to-all | bytes 2097152 | tf_op jit(solution)/shard_map/all_to_all | solution.py:170
  48.1 22.5 %all_to_all.81.refs_0_ = f32[16,8,16,128]{3,2,1,0:T(8,128)S(1)} all-to-all(f32[16,8,16,128]{3,2,1,0:T(8,128)S(1)} %get-tuple-element.42), channel_id=1, replica_groups=mesh['prow'=16,'pcol'=16] {'prow'}, dimensions={0} | all-to-all | bytes 2097152 | tf_op jit(solution)/shard_map/all_to_all | solution.py:170
  70.6 3.6 %copy-done = f32[19,1,7,32,512]{4,3,2,1,0:T(8,128)S(1)} copy-done((f32[19,1,7,32,512]{4,3,2,1,0:T(8,128)S(1)}, f32[19,1,7,32,512]{4,3,2,1,0:T(8,128)}, u32[]{:S(2)}) %copy-start) | copy-done | bytes 8716312
  74.2 6.4 %shard_map.66 = (f32[64,16,128]{2,1,0:T(8,128)S(1)}, f32[32,16,128]{2,1,0:T(8,128)S(1)}, f32[16,16,128]{2,1,0:T(8,128)S(1)}, f32[16,16,128]{2,1,0:T(8,128)S(1)},...) custom-call(s32[2]{0:T(128)S(1)} %pad_add_fusion.pos, s32[254]{0:T(256)S(1)} %copy-done.11, ...), custom_call_target="tpu_custom_call" | custom-call | tf_op jit(solution)/shard_map/pallas_call | solution.py:155
  80.5 30.4 %all_to_all.82.recv = f32[16,4,16,128]{3,2,1,0:T(8,128)S(1)} all-to-all(f32[16,4,16,128]{3,2,1,0:T(8,128)S(1)} %bitcast.38), channel_id=1, replica_groups=mesh['prow'=16,'pcol'=16] {'pcol'}, dimensions={0} | all-to-all | bytes 1048576 | tf_op jit(solution)/shard_map/all_to_all | solution.py:170
  111.6 13.8 %all_to_all.83.refs_0_ = f32[16,4,16,128]{3,2,1,0:T(8,128)S(1)} all-to-all(f32[16,4,16,128]{3,2,1,0:T(8,128)S(1)} %shard_map.67), channel_id=1, replica_groups=mesh['prow'=16,'pcol'=16] {'prow'}, dimensions={0} | all-to-all | bytes 1048576 | tf_op jit(solution)/shard_map/all_to_all | solution.py:170
  125.4 3.7 %copy-done.1 = f32[19,1,7,32,512]{4,3,2,1,0:T(8,128)S(1)} copy-done((f32[19,1,7,32,512]{4,3,2,1,0:T(8,128)S(1)}, f32[19,1,7,32,512]{4,3,2,1,0:T(8,128)}, u32[]{:S(2)}) %copy-start.1) | copy-done | bytes 8716312
  131.3 6.2 %shard_map.68 = (f32[4,16,128]{2,1,0:T(8,128)S(1)}, f32[32,16,128]{2,1,0:T(8,128)S(1)}, f32[16,16,128]{2,1,0:T(8,128)S(1)}, f32[16,16,128]{2,1,0:T(8,128)S(1)}, ...) custom-call(s32[2]{0:T(128)S(1)} %pad_add_fusion.pos, ...), custom_call_target="tpu_custom_call", output_to_operand_aliasing={{1}: (7, {}), {2}: (8, {}), {3}: (9, {}), {4}: (10, {}), {5... | custom-call | tf_op jit(solution)/shard_map/pallas_call | solution.py:155
  137.5 15.8 %all_to_all.84.recv = f32[16,2,16,128]{3,2,1,0:T(8,128)S(1)} all-to-all(f32[16,2,16,128]{3,2,1,0:T(8,128)S(1)} %bitcast.37), channel_id=1, replica_groups=mesh['prow'=16,'pcol'=16] {'pcol'}, dimensions={0} | all-to-all | bytes 524288 | tf_op jit(solution)/shard_map/all_to_all | solution.py:170
  153.9 11.9 %all_to_all.85.refs_0_ = f32[16,2,16,128]{3,2,1,0:T(8,128)S(1)} all-to-all(f32[16,2,16,128]{3,2,1,0:T(8,128)S(1)} %shard_map.69), channel_id=1, replica_groups=mesh['prow'=16,'pcol'=16] {'prow'}, dimensions={0} | all-to-all | bytes 524288 | tf_op jit(solution)/shard_map/all_to_all | solution.py:170
  172.3 4.4 %shard_map.70 = (f32[2,16,128]{2,1,0:T(8,128)S(1)}, f32[16,16,128]{2,1,0:T(8,128)S(1)}, f32[16,16,128]{2,1,0:T(8,128)S(1)}, f32[16,16,128]{2,1,0:T(8,128)S(1)}, ...) custom-call(s32[2]{0:T(128)S(1)} %pad_add_fusion.pos, ...), custom_call_target="tpu_custom_call", output_to_operand_aliasing={{1}: (7, {}), {2}: (8, {}), {3}: (9, {}), {4}: (10, {}), {5... | custom-call | tf_op jit(solution)/shard_map/pallas_call | solution.py:155
  176.7 13.9 %all_to_all.86.recv = f32[16,1,16,128]{3,2,1,0:T(8,128)S(1)} all-to-all(f32[16,1,16,128]{3,2,1,0:T(8,128)S(1)} %bitcast.36), channel_id=1, replica_groups=mesh['prow'=16,'pcol'=16] {'pcol'}, dimensions={0} | all-to-all | bytes 262144 | tf_op jit(solution)/shard_map/all_to_all | solution.py:170
  191.2 10.0 %all_to_all.87.refs_0_ = f32[16,1,16,128]{3,2,1,0:T(8,128)S(1)} all-to-all(f32[16,1,16,128]{3,2,1,0:T(8,128)S(1)} %shard_map.71), channel_id=1, replica_groups=mesh['prow'=16,'pcol'=16] {'prow'}, dimensions={0} | all-to-all | bytes 262144 | tf_op jit(solution)/shard_map/all_to_all | solution.py:170
  204.5 12.5 %all_to_all.88.recv = f32[16,1,16,128]{3,2,1,0:T(8,128)S(1)} all-to-all(f32[16,1,16,128]{3,2,1,0:T(8,128)S(1)} %bitcast.35), channel_id=1, replica_groups=mesh['prow'=16,'pcol'=16] {'pcol'}, dimensions={0} | all-to-all | bytes 262144 | tf_op jit(solution)/shard_map/all_to_all | solution.py:170
  217.6 10.2 %all_to_all.89.refs_0_ = f32[16,1,16,128]{3,2,1,0:T(8,128)S(1)} all-to-all(f32[16,1,16,128]{3,2,1,0:T(8,128)S(1)} %shard_map.73), channel_id=1, replica_groups=mesh['prow'=16,'pcol'=16] {'prow'}, dimensions={0} | all-to-all | bytes 262144 | tf_op jit(solution)/shard_map/all_to_all | solution.py:170
  230.9 12.5 %all_to_all.90.recv = f32[16,1,16,128]{3,2,1,0:T(8,128)S(1)} all-to-all(f32[16,1,16,128]{3,2,1,0:T(8,128)S(1)} %bitcast.34), channel_id=1, replica_groups=mesh['prow'=16,'pcol'=16] {'pcol'}, dimensions={0} | all-to-all | bytes 262144 | tf_op jit(solution)/shard_map/all_to_all | solution.py:170
  244.0 10.2 %all_to_all.91.refs_0_ = f32[16,1,16,128]{3,2,1,0:T(8,128)S(1)} all-to-all(f32[16,1,16,128]{3,2,1,0:T(8,128)S(1)} %shard_map.75), channel_id=1, replica_groups=mesh['prow'=16,'pcol'=16] {'prow'}, dimensions={0} | all-to-all | bytes 262144 | tf_op jit(solution)/shard_map/all_to_all | solution.py:170
  257.3 12.5 %all_to_all.92.recv = f32[16,1,16,128]{3,2,1,0:T(8,128)S(1)} all-to-all(f32[16,1,16,128]{3,2,1,0:T(8,128)S(1)} %bitcast.32), channel_id=1, replica_groups=mesh['prow'=16,'pcol'=16] {'pcol'}, dimensions={0} | all-to-all | bytes 262144 | tf_op jit(solution)/shard_map/all_to_all | solution.py:170
  274.6 7.4 %all-to-all-done.13.refs_0_ = f32[16,1,16,128]{3,2,1,0:T(8,128)S(1)} async-done(((f32[16,1,16,128]{3,2,1,0:T(8,128)}), f32[16,1,16,128]{3,2,1,0:T(8,128)S(1)}, u32[]{:S(2)}, u32[]{:S(2)}) %all-to-all-start.13) | async-done | bytes 131104 | tf_op jit(solution)/shard_map/all_to_all | solution.py:170
  291.7 4.1 %all-to-all-start.14 = ((f32[16,1,16,128]{3,2,1,0:T(8,128)}), f32[16,1,16,128]{3,2,1,0:T(8,128)S(1)}, u32[]{:S(2)}, u32[]{:S(2)}) async-start(f32[16,1,16,128]{3,2,1,0:T(8,128)} %bitcast.12), calls=%async_computation.14 | async-start | bytes 262144 | tf_op jit(solution)/shard_map/all_to_all | solution.py:170
  295.8 9.2 %all-to-all-done.14.recv = f32[16,1,16,128]{3,2,1,0:T(8,128)S(1)} async-done(((f32[16,1,16,128]{3,2,1,0:T(8,128)}), f32[16,1,16,128]{3,2,1,0:T(8,128)S(1)}, u32[]{:S(2)}, u32[]{:S(2)}) %all-to-all-start.14) | async-done | bytes 131104 | tf_op jit(solution)/shard_map/all_to_all | solution.py:170
  306.2 3.5 %all-to-all-start.15 = ((f32[16,1,16,128]{3,2,1,0:T(8,128)}), f32[16,1,16,128]{3,2,1,0:T(8,128)S(1)}, u32[]{:S(2)}, u32[]{:S(2)}) async-start(f32[16,1,16,128]{3,2,1,0:T(8,128)} %shard_map.79), calls=%async_computation.15 | async-start | bytes 262144 | tf_op jit(solution)/shard_map/all_to_all | solution.py:170
  309.8 7.4 %all-to-all-done.15 = f32[16,1,16,128]{3,2,1,0:T(8,128)S(1)} async-done(((f32[16,1,16,128]{3,2,1,0:T(8,128)}), f32[16,1,16,128]{3,2,1,0:T(8,128)S(1)}, u32[]{:S(2)}, u32[]{:S(2)}) %all-to-all-start.15) | async-done | bytes 131104 | tf_op jit(solution)/shard_map/all_to_all | solution.py:170
  (67 shorter events, 49.2 us)
Async XLA Ops:
  6.5 64.0 %copy-start.13 = (s32[19,1]{0,1:T(1,128)S(1)}, s32[19,1]{0,1:T(1,128)}, u32[]{:S(2)}) copy-start(s32[19,1]{0,1:T(1,128)} %param.10) | copy-start | bytes 232
  6.5 64.0 %copy-start.11 = (s32[254]{0:T(256)S(1)}, s32[254]{0:T(256)}, u32[]{:S(2)}) copy-start(s32[254]{0:T(256)} %parent.32) | copy-start | bytes 3052
  6.5 118.8 %all-gather.5.cloned.1.call-start = ((), (), s32[]{:S(2)}) async-start(), calls=%async_computation.16 | async-start | bytes 4456448 | tf_op jit(solution)/shard_map/all_gather | solution.py:152
  8.3 157.4 %all-gather.7.cloned.1.call-start = ((), (), s32[]{:S(2)}) async-start(), calls=%async_computation.17 | async-start | bytes 7798784 | tf_op jit(solution)/shard_map/all_gather | solution.py:152
  11.1 0.9 copy-start.6
  12.0 1.3 copy-start.9
  13.3 0.7 copy-start.10
  14.0 0.7 copy-start.12
  47.4 63.5 %copy-start.7 = (f32[19,1,2048]{2,1,0:T(1,128)S(1)}, f32[19,1,2048]{2,1,0:T(1,128)}, u32[]{:S(2)}) copy-start(f32[19,1,2048]{2,1,0:T(1,128)} %param.6) | copy-start | bytes 466948
  70.6 3.6 %copy-start = (f32[19,1,7,32,512]{4,3,2,1,0:T(8,128)S(1)}, f32[19,1,7,32,512]{4,3,2,1,0:T(8,128)}, u32[]{:S(2)}) copy-start(f32[19,1,7,32,512]{4,3,2,1,0:T(8,128)} %refs_2_.11) | copy-start | bytes 26148868
  125.4 3.7 %copy-start.1 = (f32[19,1,7,32,512]{4,3,2,1,0:T(8,128)S(1)}, f32[19,1,7,32,512]{4,3,2,1,0:T(8,128)}, u32[]{:S(2)}) copy-start(f32[19,1,7,32,512]{4,3,2,1,0:T(8,128)} %refs_2_.11) | copy-start | bytes 26148868
  129.1 2.2 copy-start.8
  153.2 48.0 %slice-start = ((s8[8716288]{0:T(1024)(128)(4,1)}), s8[327680]{0:T(1024)(128)(4,1)S(1)}, s32[]{:S(2)}) async-start(s8[8716288]{0:T(1024)(128)(4,1)} %bitcast.16), calls=%async_computation.18 | async-start | bytes 655360
  165.7 3.5 %copy-start.2 = (f32[19,1,7,32,512]{4,3,2,1,0:T(8,128)S(1)}, f32[19,1,7,32,512]{4,3,2,1,0:T(8,128)}, u32[]{:S(2)}) copy-start(f32[19,1,7,32,512]{4,3,2,1,0:T(8,128)} %refs_2_.11) | copy-start | bytes 26148868
  169.2 3.1 copy-start.4
  172.3 29.0 %slice-start.1 = ((s8[8716288]{0:T(1024)(128)(4,1)}), s8[4194304]{0:T(1024)(128)(4,1)S(1)}, s32[]{:S(2)}) async-start(s8[8716288]{0:T(1024)(128)(4,1)} %bitcast.16), calls=%async_computation.19 | async-start | bytes 8388608
  172.3 29.0 %slice-start.2 = ((s8[8716288]{0:T(1024)(128)(4,1)}), s8[4194304]{0:T(1024)(128)(4,1)S(1)}, s32[]{:S(2)}) async-start(s8[8716288]{0:T(1024)(128)(4,1)} %bitcast.16), calls=%async_computation.20 | async-start | bytes 8388608
  271.1 10.9 %all-to-all-start.13 = ((f32[16,1,16,128]{3,2,1,0:T(8,128)}), f32[16,1,16,128]{3,2,1,0:T(8,128)S(1)}, u32[]{:S(2)}, u32[]{:S(2)}) async-start(f32[16,1,16,128]{3,2,1,0:T(8,128)} %shard_map.77), calls=%async_computation.13 | async-start | bytes 262144 | tf_op jit(solution)/shard_map/all_to_all | solution.py:170
  282.0 3.5 %copy-start.3 = (f32[19,1,7,32,512]{4,3,2,1,0:T(8,128)S(1)}, f32[19,1,7,32,512]{4,3,2,1,0:T(8,128)}, u32[]{:S(2)}) copy-start(f32[19,1,7,32,512]{4,3,2,1,0:T(8,128)} %refs_2_.11) | copy-start | bytes 26148868
  285.4 3.1 copy-start.5
  291.7 13.3 %all-to-all-start.14 = ((f32[16,1,16,128]{3,2,1,0:T(8,128)}), f32[16,1,16,128]{3,2,1,0:T(8,128)S(1)}, u32[]{:S(2)}, u32[]{:S(2)}) async-start(f32[16,1,16,128]{3,2,1,0:T(8,128)} %bitcast.12), calls=%async_computation.14 | async-start | bytes 262144 | tf_op jit(solution)/shard_map/all_to_all | solution.py:170
  306.2 10.9 %all-to-all-start.15 = ((f32[16,1,16,128]{3,2,1,0:T(8,128)}), f32[16,1,16,128]{3,2,1,0:T(8,128)S(1)}, u32[]{:S(2)}, u32[]{:S(2)}) async-start(f32[16,1,16,128]{3,2,1,0:T(8,128)} %shard_map.79), calls=%async_computation.15 | async-start | bytes 262144 | tf_op jit(solution)/shard_map/all_to_all | solution.py:170
  319.8 0.7 copy-start.14
Sparse Core Ops, SparseCore 0:
  9.8 73.7 all-gather.4
  86.0 72.2 all-gather.6

commit v2 on v1

--- a/solution.py
+++ b/solution.py
@@ -10,10 +10,25 @@
 LEVELS = 8
 LEAVES = 128
 GATHER_FROM = 1
+CUTS = (1, 5)
+SCRATCH = [pltpu.VMEM((512, 128), jnp.float32)]
+TOP = 5
 VMEM_LIMIT = 24 * 1024 * 1024
 
 NODES = [LEAVES >> h for h in range(LEVELS)]
 NODE_BASE = [2 * LEAVES - 2 * (LEAVES >> h) for h in range(LEVELS)]
+
+
+class Part:
+    def __init__(self, ref, start):
+        self.ref, self.start = ref, start
+
+    def __getitem__(self, index):
+        return self.ref[index + self.start]
+
+
+def with_parts(kernel, *refs):
+    return kernel(*[Part(refs[0], start) for start in (0, 2, 256, 389)], *refs[1:])
 
 
 def split(x):
@@ -23,8 +38,18 @@
 
 
 def dot3(a, b, dims):
+    bh, bl = split(b)
+    n = a.shape[0]
+    if n <= 64 and dims[0] == (1,):
+        high = a.astype(jnp.bfloat16).astype(jnp.float32)
+        both = jnp.concatenate([high, a - high], 0).astype(jnp.bfloat16)
+        dot = functools.partial(
+            lax.dot_general, dimension_numbers=(dims, ((), ())), preferred_element_type=jnp.float32
+        )
+        first = dot(both, bh)
+        second = dot(high.astype(jnp.bfloat16), bl)
+        return first[:n] + (first[n:] + second)
     ah, al = split(a)
-    bh, bl = split(b)
     dot = functools.partial(
         lax.dot_general, dimension_numbers=(dims, ((), ())), preferred_element_type=jnp.float32
     )
@@ -139,32 +164,155 @@
             after[d][where] += scale * update[d * 16 : (d + 1) * 16]
 
 
+def pack_kernel(pos, parent, pattern, sizes, inv5, inv6, inv7, panel5, panel6, *refs):
+    half = len(refs) // 2
+    for source, target in zip(refs[:half], refs[half + 1 :]):
+        target[...] = source[:, 0]
+    out = refs[half]
+    for level, inv, panel, at in ((0, inv5, panel5, 3), (1, inv6, panel6, 0), (2, inv7, None, 2)):
+        slot = 16 + level
+        size = sizes[slot]
+        row = pos[0] * 32 + lax.broadcasted_iota(jnp.int32, (32, 512), 0)
+        column = lax.broadcasted_iota(jnp.int32, (32, 512), 1)
+        out[at] = jnp.where((row < size) & (column < size), inv[0, 0], 0.0)
+        for d in range(2 - level):
+            out[at + 1 + d] = panel[0, 0, d] * pattern[slot * 7 + d].astype(jnp.float32)
+
+
+def choose_kernel(pos, parent, pattern, sizes, low, middle, high, out):
+    for c in range(4):
+        out[3 * c : 3 * c + 3] = low[c]
+    for c in range(2):
+        out[12 + 2 * c : 14 + 2 * c] = middle[c]
+    out[16:17] = high[0]
+
+
+def turn_kernel(pos, parent, pattern, sizes, p5, p6, p7, rhs, out, scratch):
+    at = 0
+    for level, ref in enumerate((p5, p6, p7)):
+        for j in range(4 >> level):
+            piece = ref[j] - jnp.where(pos[1] == j, rhs[16 + level], 0.0)
+            scratch[pl.ds(at * 32, 16, stride=2), :] = piece
+            scratch[pl.ds(at * 32 + 1, 16, stride=2), :] = pltpu.roll(piece, 64, 1)
+            at += 1
+    scratch[pl.ds(224, 32), :] = jnp.zeros((32, 128), jnp.float32)
+    turned = scratch[pl.ds(0, 256), :].T
+    for z in range(8):
+        out[2 * z] = turned[8 * z : 8 * z + 8]
+        out[2 * z + 1] = turned[8 * z : 8 * z + 8]
+
+
+def sum_kernel(pos, parent, pattern, sizes, recv, out):
+    total = recv[0]
+    for i in range(1, 16):
+        total = total + recv[i]
+    for i in range(16):
+        out[i] = total
+
+
+def place(own, y, level, pos):
+    lanes = pltpu.roll(y, (256 - (pos[0] % 8) * 32) % 256, 1)[:, :128]
+    lane = lax.broadcasted_iota(jnp.int32, (8, 128), 1) // 32
+    return jnp.where(lane == level, pltpu.roll(lanes, level * 32, 1), own)
+
+
+def low_kernel(pos, parent, pattern, sizes, recv, block, out, left, z, y):
+    step = pl.program_id(0)
+
+    @pl.when(step == 0)
+    def _():
+        lane = lax.broadcasted_iota(jnp.int32, (8, 128), 1) // 32
+        for n in range(7):
+            for g in range(4):
+                whole = jnp.zeros((8, 128), jnp.float32)
+                for i in range(4):
+                    piece = recv[4 * g + i][:, (n // 4) * 128 : (n // 4 + 1) * 128]
+                    turned = pltpu.roll(piece, ((i - n % 4) * 32) % 128, 1)
+                    whole = jnp.where(lane == i, turned, whole)
+                if n < 4:
+                    z[n, :, g * 128 : (g + 1) * 128] = -whole
+                else:
+                    left[n - 4, :, g * 128 : (g + 1) * 128] = jnp.where(pos[1] % 2 == 0, -whole, 0.0)
+        out[...] = jnp.zeros_like(out)
+
+    node, kind = step // 3, step % 3
+    matrix = block[:, 0].reshape(512, 256)
+
+    @pl.when(kind == 0)
+    def _():
+        solved = dot3(z[node], matrix, ((1,), (0,)))
+        y[...] = solved
+        out[node] = place(out[node], solved, 0, pos)
+
+    @pl.when(kind > 0)
+    def _():
+        update = dot3(y[...], matrix, ((1,), (1,)))
+        target = jnp.where(kind == 1, parent[NODE_BASE[TOP] + node] - NODE_BASE[TOP + 1], 2)
+        left[target] = left[target] - update
+
+
+def middle_kernel(pos, parent, pattern, sizes, left, other, before, block, out, after, y):
+    step = pl.program_id(0)
+
+    @pl.when(step == 0)
+    def _():
+        out[...] = before[...]
+        after[...] = left[2]
+
+    node, kind = step // 2, step % 2
+    matrix = block[:, 0].reshape(512, 256)
+
+    @pl.when(kind == 0)
+    def _():
+        solved = dot3(left[node] + other[node], matrix, ((1,), (0,)))
+        y[...] = solved
+        out[node] = place(out[node], solved, 1, pos)
+
+    @pl.when(kind > 0)
+    def _():
+        after[...] = after[...] - dot3(y[...], matrix, ((1,), (1,)))
+
+
+def root_kernel(pos, parent, pattern, sizes, left, other, before, block, out):
+    solved = dot3(left[...] + other[...], block[:, 0].reshape(512, 256), ((1,), (0,)))
+    out[...] = before[...]
+    out[0] = place(before[0], solved, 2, pos)
+
+
+def last_kernel(pos, parent, pattern, sizes, recv, out, scratch):
+    columns = jnp.concatenate([recv[2 * i + pos[0] // 8] for i in range(8)], 0)
+    scratch[pl.ds(0, 64), :] = columns
+    scratch[pl.ds(64, 64), :] = columns
+    turned = scratch[pl.ds(0, 128), :].T
+    scratch[pl.ds(128, 128), :] = turned
+    lane = lax.broadcasted_iota(jnp.int32, (16, 128), 1)
+    for level in range(3):
+        even = scratch[pl.ds(128 + level * 32, 16, stride=2), :]
+        odd = scratch[pl.ds(129 + level * 32, 16, stride=2), :]
+        out[level] = jnp.where(lane < 64, even, odd)
+
+
 def on_device(right_side, inverse_rows, panels, pattern, node_sizes, parent):
     pos = jnp.stack([lax.axis_index("prow"), lax.axis_index("pcol")]).astype(jnp.int32)
     rhs = right_side.reshape(19, 16, 128)
-    scalars = (pos, parent, pattern.reshape(-1), node_sizes.reshape(-1))
+    scalars = jnp.concatenate([pos, parent, pattern.reshape(-1), node_sizes.reshape(-1)])
     slot_counts = [max(1, n // 16) for n in NODES]
     bases = [sum(slot_counts[:h]) for h in range(LEVELS)]
-    first = bases[GATHER_FROM]
-    cuts = [first, bases[min(GATHER_FROM + 1, LEVELS - 1)], 19]
-    inverses = []
-    for lo, hi in zip(cuts[:-1], cuts[1:]):
-        inverses.append((lo, lax.all_gather(inverse_rows[lo:hi, 0], "prow", axis=0)))
-
     def call(kernel, scratch, grid, in_specs, out_specs, out_shape, aliases, *args):
+        args = [pltpu.with_memory_space_constraint(a, pltpu.HBM) if a.size > 1 << 18 else a for a in args]
         return pl.pallas_call(
-            kernel,
+            functools.partial(with_parts, kernel),
             grid_spec=pltpu.PrefetchScalarGridSpec(
-                num_scalar_prefetch=4,
+                num_scalar_prefetch=1,
                 grid=grid,
                 in_specs=in_specs,
                 out_specs=out_specs,
-                scratch_shapes=[pltpu.VMEM((512, 128), jnp.float32)] if scratch else [],
+                scratch_shapes=scratch,
             ),
             out_shape=out_shape,
-            input_output_aliases={k + 4: v for k, v in aliases.items()},
+            input_output_aliases={k + 1: v for k, v in aliases.items()},
             compiler_params=pltpu.CompilerParams(vmem_limit_bytes=VMEM_LIMIT),
-        )(*scalars, *args)
+        )(scalars, *args)
 
     def exchange(x, axis):
         return lax.all_to_all(x, axis, 0, 0, tiled=True)
@@ -173,7 +321,32 @@
     pending = []
     recv = None
     outputs = []
-    for height in range(LEVELS):
+    cuts = [bases[h] for h in CUTS]
+    rows = pl.BlockSpec((6, 32, 512), lambda *_: (0, 0, 0))
+
+    def block(*lead):
+        def spec(n, slot):
+            return pl.BlockSpec((1, 1) + (n,) * len(lead) + (32, 512), lambda *_: (slot, 0) + lead + (0, 0))
+
+        return spec
+
+    spans = list(zip(cuts[:-1], cuts[1:]))
+    top, *wholes = call(
+        pack_kernel,
+        [],
+        (1,),
+        [block()(0, 16), block()(0, 17), block()(0, 18), block(0)(2, 16), block(0)(1, 17)]
+        + [pl.BlockSpec((hi - lo, 1, 32, 512), lambda *_, i=lo // (hi - lo): (i, 0, 0, 0)) for lo, hi in spans],
+        [rows] + [pl.BlockSpec((hi - lo, 32, 512), lambda *_: (0, 0, 0)) for lo, hi in spans],
+        [jax.ShapeDtypeStruct((6, 32, 512), f32)]
+        + [jax.ShapeDtypeStruct((hi - lo, 32, 512), f32) for lo, hi in spans],
+        {},
+        *[inverse_rows] * 3,
+        *[panels] * 2,
+        *[inverse_rows] * len(spans),
+    )
+    inverses = [(lo, lax.all_gather(part, "prow", axis=0)) for lo, part in zip(cuts[:-1], wholes)]
+    for height in range(TOP):
         count = slot_counts[height]
         base = bases[height]
         reach = LEVELS - 1 - height
@@ -187,7 +360,7 @@
         rhs_all = pl.BlockSpec((count, 16, 128), lambda *_, b=base // count: (b, 0, 0))
         if whole:
             z = call(
-                functools.partial(residue_kernel, *info), False, (1,), [every, rhs_all], every, piece, {}, recv, rhs
+                functools.partial(residue_kernel, *info), [], (1,), [every, rhs_all], every, piece, {}, recv, rhs
             )
             gathered = exchange(z, "prow")
         else:
@@ -198,10 +371,13 @@
             args = [rhs, inverse_rows]
             if height > 0:
                 in_specs, args = [one] + in_specs, [recv] + args
-            parts = call(functools.partial(partial_kernel, *info), True, (count,), in_specs, one, piece, {}, *args)
+            parts = call(functools.partial(partial_kernel, *info), SCRATCH, (count,), in_specs, one, piece, {}, *args)
             parts = exchange(parts, "prow")
+            if height == 0:
+                top, parts = lax.optimization_barrier((top, parts))
+                top = lax.all_gather(top, "pcol", axis=0)
             y, sol = call(
-                functools.partial(solved_kernel, *info), False, (1,), [every], [every, every_own], [piece, own], {}, parts
+                functools.partial(solved_kernel, *info), [], (1,), [every], [every, every_own], [piece, own], {}, parts
             )
             outputs.append(sol)
             gathered = exchange(y, "prow")
@@ -229,15 +405,110 @@
             out_specs.append(spec)
             out_shape.append(jax.ShapeDtypeStruct(shape, f32))
         results = call(
-            functools.partial(spread_kernel, *info, whole), True, (count,), in_specs, out_specs, out_shape, aliases, *args
+            functools.partial(spread_kernel, *info, whole), SCRATCH, (count,), in_specs, out_specs, out_shape, aliases, *args
         )
         results = list(results)
         if whole:
             outputs.append(results.pop(0))
-        if reach:
+        if height + 1 < TOP:
             following = slot_counts[height + 1]
             recv = exchange(results[0].reshape(16, following, 16, 128), "pcol")
             pending = results[1:]
+        if height == 1:
+            top, recv = lax.optimization_barrier((top, recv))
+            halves = [(4, 3, 0, 1), (2, 2, 0, 0), (1, 1, 0, 2)]
+            chosen = call(
+                choose_kernel,
+                [],
+                (1,),
+                [
+                    pl.BlockSpec((m, n, 32, 256), lambda _, info, a=a, b=b: (a, b, 0, info[1] % 2))
+                    for m, n, a, b in halves
+                ],
+                pl.BlockSpec((17, 32, 256), lambda *_: (0, 0, 0)),
+                jax.ShapeDtypeStruct((17, 32, 256), f32),
+                {},
+                *[top] * 3,
+            )
+            top = lax.all_gather(chosen, "prow", axis=0)
+    many = pl.BlockSpec((16, 16, 128), lambda *_: (0, 0, 0))
+    sides = pl.BlockSpec((16, 8, 256), lambda *_: (0, 0, 0))
+    sides_shape = jax.ShapeDtypeStruct((16, 8, 256), f32)
+    turned = call(
+        turn_kernel,
+        SCRATCH,
+        (1,),
+        [many] * 3 + [pl.BlockSpec((19, 16, 128), lambda *_: (0, 0, 0))],
+        sides,
+        sides_shape,
+        {},
+        *results,
+        rhs,
+    )
+    total = call(sum_kernel, [], (1,), [sides], sides, sides_shape, {}, exchange(turned, "pcol"))
+    gathered = exchange(total, "prow")
+    def halves_from(start):
+        return pl.BlockSpec((16, 1, 32, 256), lambda s, *_: (0, start + s, 0, 0))
+
+    def whole_of(*shape):
+        return pl.BlockSpec(shape, lambda *_: (0,) * len(shape)), jax.ShapeDtypeStruct(shape, f32)
+
+    def other_core(x):
+        return lax.ppermute(x, "pcol", [(i, i ^ 1) for i in range(16)])
+
+    found, found_shape = whole_of(16, 8, 128)
+    three, three_shape = whole_of(3, 8, 512)
+    single, single_shape = whole_of(8, 512)
+    half_y = pltpu.VMEM((8, 256), f32)
+    solved, left = call(
+        low_kernel,
+        [pltpu.VMEM((4, 8, 512), f32), half_y],
+        (12,),
+        [sides, halves_from(0)],
+        [found, three],
+        [found_shape, three_shape],
+        {},
+        gathered,
+        top,
+    )
+    solved, left = call(
+        middle_kernel,
+        [half_y],
+        (4,),
+        [three, three, found, halves_from(12)],
+        [found, single],
+        [found_shape, single_shape],
+        {},
+        left,
+        other_core(left),
+        solved,
+        top,
+    )
+    solved = call(
+        root_kernel,
+        [],
+        (1,),
+        [single, single, found, halves_from(16)],
+        found,
+        found_shape,
+        {},
+        left,
+        other_core(left),
+        solved,
+        top,
+    )
+    outputs.append(
+        call(
+            last_kernel,
+            SCRATCH,
+            (1,),
+            [pl.BlockSpec((16, 8, 128), lambda *_: (0, 0, 0))],
+            pl.BlockSpec((3, 16, 128), lambda *_: (0, 0, 0)),
+            jax.ShapeDtypeStruct((3, 16, 128), f32),
+            {},
+            exchange(solved, "pcol"),
+        )
+    )
     return jnp.concatenate(outputs, 0).reshape(19, 1, 2048)
 
 

time: 329 us -> 298 us (0.906)
  local copies, waits for them, and re-layouts: 33.9 us -> 2.31 us
  blocking collectives: 205 us -> 176 us
  Pallas kernels: 40 us -> 56.7 us
  waiting for transfers between devices: 24 us -> 35.7 us
    all_to_all x13 -> x10, blocking collectives: 205 us -> 176 us  [exchange(): return lax.all_to_all(x, axis, 0, 0, tiled=True)]
    unnamed x44 -> x10, local copies, waits for them, and re-layouts: 27.7 us -> 1.45 us
    all_gather x2 -> x3, waiting for transfers between devices: 0.01 us -> 18.7 us  [the longest x1 18.7 us: on_device(): top = lax.all_gather(top, 'pcol', axis=0)]
    pallas_call x16 -> x19, Pallas kernels: 40 us -> 56.7 us  [call(): pl.pallas_call(functools.partial(with_parts, kernel), grid_spec=pltpu.Pre...]
    all_to_all x3, waiting for transfers between devices: 23.9 us -> 15.2 us  [exchange(): return lax.all_to_all(x, axis, 0, 0, tiled=True)]
    slice x2 -> x0, local copies, waits for them, and re-layouts: 3.53 us -> none  [on_device(): inverse_rows[lo:hi, 0]]
  transfers between devices with their start and end apart: 5 -> 8, of which waited for: 3 -> 5; matrix products, arithmetic and copies ran while one was open for 1% -> 0% of each run, Pallas kernels for 6% -> 12%
where the time goes in v2:
time: 298 us; the launch traced here: 296 us
  blocking collectives  176 us (59%)
  Pallas kernels  56.7 us (19%)
  waiting for transfers between devices  35.7 us (12%)
  between operations  13.2 us (4%)
  starting transfers between devices  12.5 us (4%)
    all_to_all x10, blocking collectives, exchange(): return lax.all_to_all(x, axis, 0, 0, tiled=True)  176 us
    pallas_call x19, Pallas kernels, call(): pl.pallas_call(functools.partial(with_parts, kernel), grid_spec=pltpu.Pre...  56.7 us
    all_gather x1, waiting for transfers between devices, on_device(): top = lax.all_gather(top, 'pcol', axis=0)  18.7 us
    all_to_all x3, waiting for transfers between devices, exchange(): return lax.all_to_all(x, axis, 0, 0, tiled=True)  15.2 us
    all_to_all x3, starting transfers between devices, exchange(): return lax.all_to_all(x, axis, 0, 0, tiled=True)  11.1 us
  transfers between devices with their start and end apart: 8, of which 5 were waited for; matrix products, arithmetic and copies ran while one was open for 0% of the time, Pallas kernels for 12%

profile of v2, /device:TPU:1, one launch (start us, length us, event | category | flops | bytes accessed | tf_op | source)
XLA Modules:
  0.0 296.4 jit_solution(17997726307961215379)
XLA Ops:
  8.2 2.8 shard_map.64
  11.0 6.2 %shard_map.65 = f32[16,8,16,128]{3,2,1,0:T(8,128)S(1)} custom-call(s32[408]{0:T(512)S(1)} %concatenate.6.refs_0_, f32[19,16,128]{2,1,0:T(8,128)S(1)} %bitcast.14, f32[19,1,32,512]{3,2,1,0:T(8,128)} %refs_2_.4), custom_call_target="tpu_custom_call" | custom-call | tf_op jit(solution)/shard_map/pallas_call | solution.py:303
  17.2 29.0 %all_to_all.65.refs_1_ = f32[16,8,16,128]{3,2,1,0:T(8,128)S(1)} all-to-all(f32[16,8,16,128]{3,2,1,0:T(8,128)S(1)} %shard_map.65), channel_id=1, replica_groups=mesh['prow'=16,'pcol'=16] {'prow'}, dimensions={0} | all-to-all | bytes 2097152 | tf_op jit(solution)/shard_map/all_to_all | solution.py:318
  46.9 15.9 %all_to_all.66.refs_1_ = f32[16,8,16,128]{3,2,1,0:T(8,128)S(1)} all-to-all(f32[16,8,16,128]{3,2,1,0:T(8,128)S(1)} %get-tuple-element.49), channel_id=1, replica_groups=mesh['prow'=16,'pcol'=16] {'prow'}, dimensions={0} | all-to-all | bytes 2097152 | tf_op jit(solution)/shard_map/all_to_all | solution.py:318
  62.8 8.6 %shard_map.67 = (f32[64,16,128]{2,1,0:T(8,128)S(1)}, f32[32,16,128]{2,1,0:T(8,128)}, f32[16,16,128]{2,1,0:T(8,128)S(1)}, f32[16,16,128]{2,1,0:T(8,128)S(1)}, f32...) custom-call(s32[408]{0:T(512)S(1)} %concatenate.6.refs_0_, ...), custom_call_target="tpu_custom_call" | custom-call | tf_op jit(solution)/shard_map/pallas_call | solution.py:303
  71.4 40.2 %all_to_all.67.refs_1_ = f32[16,4,16,128]{3,2,1,0:T(8,128)S(1)} all-to-all(f32[16,4,16,128]{3,2,1,0:T(8,128)S(1)} %bitcast.22), channel_id=1, replica_groups=mesh['prow'=16,'pcol'=16] {'pcol'}, dimensions={0} | all-to-all | bytes 1048576 | tf_op jit(solution)/shard_map/all_to_all | solution.py:318
  112.3 13.7 %all_to_all.68.refs_1_ = f32[16,4,16,128]{3,2,1,0:T(8,128)S(1)} all-to-all(f32[16,4,16,128]{3,2,1,0:T(8,128)S(1)} %shard_map.68), channel_id=1, replica_groups=mesh['prow'=16,'pcol'=16] {'prow'}, dimensions={0} | all-to-all | bytes 1048576 | tf_op jit(solution)/shard_map/all_to_all | solution.py:318
  126.0 6.7 %shard_map.69 = (f32[4,16,128]{2,1,0:T(8,128)S(1)}, f32[32,16,128]{2,1,0:T(8,128)}, f32[16,16,128]{2,1,0:T(8,128)S(1)}, f32[16,16,128]{2,1,0:T(8,128)S(1)}, f32[...) custom-call(s32[408]{0:T(512)S(1)} %concatenate.6.refs_0_, ...), custom_call_target="tpu_custom_call", output_to_operand_aliasing={{1}: (4, {}), {2}: (5, {}), {3}: (6, {}), {4}: (7, {}), {5}... | custom-call | tf_op jit(solution)/shard_map/pallas_call | solution.py:303
  132.7 4.0 %all-to-all-start.4 = ((f32[16,2,16,128]{3,2,1,0:T(8,128)}), f32[16,2,16,128]{3,2,1,0:T(8,128)S(1)}, u32[]{:S(2)}, u32[]{:S(2)}) async-start(f32[16,2,16,128]{3,2,1,0:T(8,128)} %bitcast.7), calls=%async_computation.4 | async-start | bytes 524288 | tf_op jit(solution)/shard_map/all_to_all | solution.py:318
  136.7 18.7 %all-gather.9.cloned.1.call-done = f32[96,32,512]{2,1,0:T(8,128)} async-done(((f32[6,32,512]{2,1,0:T(8,128)}), f32[96,32,512]{2,1,0:T(8,128)}) %all-gather.9.cloned.1.call-update) | async-done | bytes 6291472 | tf_op jit(solution)/shard_map/all_gather | solution.py:378
  158.5 14.6 %all_to_all.69.refs_1_ = f32[16,2,16,128]{3,2,1,0:T(8,128)S(1)} all-to-all(f32[16,2,16,128]{3,2,1,0:T(8,128)S(1)} %shard_map.70), channel_id=1, replica_groups=mesh['prow'=16,'pcol'=16] {'prow'}, dimensions={0} | all-to-all | bytes 524288 | tf_op jit(solution)/shard_map/all_to_all | solution.py:318
  173.1 3.6 %shard_map.71 = (f32[2,16,128]{2,1,0:T(8,128)S(1)}, f32[16,16,128]{2,1,0:T(8,128)S(1)}, f32[16,16,128]{2,1,0:T(8,128)S(1)}, f32[16,16,128]{2,1,0:T(8,128)S(1)}, ...) custom-call(s32[408]{0:T(512)S(1)} %concatenate.6.refs_0_, ...), custom_call_target="tpu_custom_call", output_to_operand_aliasing={{1}: (4, {}), {2}: (5, {}), {3}: (6, {}), {4}: (7, {}), {5}... | custom-call | tf_op jit(solution)/shard_map/pallas_call | solution.py:303
  176.7 14.7 %all_to_all.70.refs_1_ = f32[16,1,16,128]{3,2,1,0:T(8,128)S(1)} all-to-all(f32[16,1,16,128]{3,2,1,0:T(8,128)S(1)} %bitcast.21), channel_id=1, replica_groups=mesh['prow'=16,'pcol'=16] {'pcol'}, dimensions={0} | all-to-all | bytes 262144 | tf_op jit(solution)/shard_map/all_to_all | solution.py:318
  192.0 11.8 %all_to_all.71.refs_1_ = f32[16,1,16,128]{3,2,1,0:T(8,128)S(1)} all-to-all(f32[16,1,16,128]{3,2,1,0:T(8,128)S(1)} %shard_map.72), channel_id=1, replica_groups=mesh['prow'=16,'pcol'=16] {'prow'}, dimensions={0} | all-to-all | bytes 262144 | tf_op jit(solution)/shard_map/all_to_all | solution.py:318
  203.8 2.7 shard_map.73
  206.5 12.1 %all_to_all.72.refs_1_ = f32[16,1,16,128]{3,2,1,0:T(8,128)S(1)} all-to-all(f32[16,1,16,128]{3,2,1,0:T(8,128)S(1)} %bitcast.20), channel_id=1, replica_groups=mesh['prow'=16,'pcol'=16] {'pcol'}, dimensions={0} | all-to-all | bytes 262144 | tf_op jit(solution)/shard_map/all_to_all | solution.py:318
  219.2 11.7 %all_to_all.73.refs_1_ = f32[16,1,16,128]{3,2,1,0:T(8,128)S(1)} all-to-all(f32[16,1,16,128]{3,2,1,0:T(8,128)S(1)} %shard_map.74), channel_id=1, replica_groups=mesh['prow'=16,'pcol'=16] {'prow'}, dimensions={0} | all-to-all | bytes 262144 | tf_op jit(solution)/shard_map/all_to_all | solution.py:318
  234.3 12.2 %all_to_all.74.refs_1_ = f32[16,8,256]{2,1,0:T(8,128)S(1)} all-to-all(f32[16,8,256]{2,1,0:T(8,128)S(1)} %shard_map.76), channel_id=1, replica_groups=mesh['prow'=16,'pcol'=16] {'pcol'}, dimensions={0} | all-to-all | bytes 262144 | tf_op jit(solution)/shard_map/all_to_all | solution.py:318
  247.8 3.5 %all-to-all-start.11 = ((f32[16,8,256]{2,1,0:T(8,128)}), f32[16,8,256]{2,1,0:T(8,128)S(1)}, u32[]{:S(2)}, u32[]{:S(2)}) async-start(f32[16,8,256]{2,1,0:T(8,128)} %shard_map.77), calls=%async_computation.11 | async-start | bytes 262144 | tf_op jit(solution)/shard_map/all_to_all | solution.py:318
  251.3 7.4 %all-to-all-done.11.refs_1_ = f32[16,8,256]{2,1,0:T(8,128)S(1)} async-done(((f32[16,8,256]{2,1,0:T(8,128)}), f32[16,8,256]{2,1,0:T(8,128)S(1)}, u32[]{:S(2)}, u32[]{:S(2)}) %all-to-all-start.11) | async-done | bytes 131104 | tf_op jit(solution)/shard_map/all_to_all | solution.py:318
  258.7 9.1 %shard_map.79 = (f32[16,8,128]{2,1,0:T(8,128)S(1)}, f32[3,8,512]{2,1,0:T(8,128)S(1)}) custom-call(s32[408]{0:T(512)S(1)} %concatenate.6.refs_0_, f32[16,8,256]{2,1,0:T(8,128)S(1)} %all-to-all-done.11.refs_1_, f32[16,17,32,256]{3,2,1,0:T(8,128)} %bitcast.27), custom_call_target="tpu_custom_call" | custom-call | tf_op jit(solution)/shard_map/pallas_call | solution.py:303
  269.6 3.6 %shard_map.80 = (f32[16,8,128]{2,1,0:T(8,128)S(1)}, f32[8,512]{1,0:T(8,128)S(1)}) custom-call(s32[408]{0:T(512)S(1)} %concatenate.6.refs_0_, f32[3,8,512]{2,1,0:T(8,128)S(1)} %get-tuple-element.83.refs_1_, f32[3,8,512]{2,1,0:T(8,128)S(1)} %collective-permute-done.refs_2_, f32[16,8,128]{2,1,0:T(8,128)S(1)} %get-tuple-element.84.refs_3_, ...), custom_call_target="tpu_custom_call" | custom-call | tf_op jit(solution)/shard_map/pallas_call | solution.py:303
  277.0 3.6 %all-to-all-start.12 = ((f32[16,8,128]{2,1,0:T(8,128)}), f32[16,8,128]{2,1,0:T(8,128)S(1)}, u32[]{:S(2)}, u32[]{:S(2)}) async-start(f32[16,8,128]{2,1,0:T(8,128)} %shard_map.81), calls=%async_computation.12 | async-start | bytes 131072 | tf_op jit(solution)/shard_map/all_to_all | solution.py:318
  280.7 7.8 %all-to-all-done.12.refs_1_ = f32[16,8,128]{2,1,0:T(8,128)S(1)} async-done(((f32[16,8,128]{2,1,0:T(8,128)}), f32[16,8,128]{2,1,0:T(8,128)S(1)}, u32[]{:S(2)}, u32[]{:S(2)}) %all-to-all-start.12) | async-done | bytes 65568 | tf_op jit(solution)/shard_map/all_to_all | solution.py:318
  (37 shorter events, 18.8 us)
Async XLA Ops:
  6.5 119.5 %all-gather.7.cloned.1.call-start = ((), (), s32[]{:S(2)}) async-start(), calls=%async_computation.13 | async-start | bytes 8912896 | tf_op jit(solution)/shard_map/all_gather | solution.py:348
  8.2 2.9 copy-start
  11.0 144.5 %all-gather.9.cloned.1.call-start = ((), (), s32[]{:S(2)}) async-start(), calls=%async_computation.14 | async-start | bytes 6684672 | tf_op jit(solution)/shard_map/all_gather | solution.py:378
  132.7 22.7 %all-to-all-start.4 = ((f32[16,2,16,128]{3,2,1,0:T(8,128)}), f32[16,2,16,128]{3,2,1,0:T(8,128)S(1)}, u32[]{:S(2)}, u32[]{:S(2)}) async-start(f32[16,2,16,128]{3,2,1,0:T(8,128)} %bitcast.7), calls=%async_computation.4 | async-start | bytes 524288 | tf_op jit(solution)/shard_map/all_to_all | solution.py:318
  136.7 122.0 %all-gather.11.cloned.1.call-start = ((), (), s32[]{:S(2)}) async-start(), calls=%async_computation.15 | async-start | bytes 9469952 | tf_op jit(solution)/shard_map/all_gather | solution.py:433
  247.8 10.9 %all-to-all-start.11 = ((f32[16,8,256]{2,1,0:T(8,128)}), f32[16,8,256]{2,1,0:T(8,128)S(1)}, u32[]{:S(2)}, u32[]{:S(2)}) async-start(f32[16,8,256]{2,1,0:T(8,128)} %shard_map.77), calls=%async_computation.11 | async-start | bytes 262144 | tf_op jit(solution)/shard_map/all_to_all | solution.py:318
  267.8 1.7 collective-permute-start
  273.2 1.3 collective-permute-start.1
  277.0 11.5 %all-to-all-start.12 = ((f32[16,8,128]{2,1,0:T(8,128)}), f32[16,8,128]{2,1,0:T(8,128)S(1)}, u32[]{:S(2)}, u32[]{:S(2)}) async-start(f32[16,8,128]{2,1,0:T(8,128)} %shard_map.81), calls=%async_computation.12 | async-start | bytes 131072 | tf_op jit(solution)/shard_map/all_to_all | solution.py:318
  289.2 0.7 copy-start.1
Sparse Core Ops, SparseCore 0:
  11.1 89.6 all-gather.6
  102.6 52.7 all-gather.8
  158.1 79.1 all-gather.10

commit v3 on v2

--- a/solution.py
+++ b/solution.py
@@ -9,9 +9,9 @@
 
 LEVELS = 8
 LEAVES = 128
-GATHER_FROM = 1
-CUTS = (1, 5)
-SCRATCH = [pltpu.VMEM((512, 128), jnp.float32)]
+GATHER_FROM = 2
+CUTS = (2, 5)
+SCRATCH = [pltpu.VMEM((192, 512), jnp.float32)]
 TOP = 5
 VMEM_LIMIT = 24 * 1024 * 1024
 
@@ -56,26 +56,39 @@
     return dot(ah, bh) + (dot(ah, bl) + dot(al, bh))
 
 
-def unfold(x, scratch):
+def lower(shape):
+    return lax.broadcasted_iota(jnp.int32, shape, len(shape) - 1) < 64
+
+
+def from_own_order(x, scratch):
     n = x.shape[0]
-    scratch[pl.ds(0, n, stride=2), :] = x
-    scratch[pl.ds(1, n, stride=2), :] = pltpu.roll(x, 64, 1)
-    return scratch[pl.ds(0, 2 * n), :][:, :64]
-
-
-def fold(x, scratch):
-    n = x.shape[0] // 2
-    scratch[pl.ds(0, 2 * n), :] = jnp.concatenate([x, x], 1)
-    even = scratch[pl.ds(0, n, stride=2), :]
-    odd = scratch[pl.ds(1, n, stride=2), :]
-    lane = lax.broadcasted_iota(jnp.int32, (n, 128), 1)
-    return jnp.where(lane < 64, even, odd)
+    x = x.reshape(n * 16, 128)
+    scratch[pl.ds(0, n * 16, stride=2), :] = x
+    scratch[pl.ds(1, n * 16, stride=2), :] = pltpu.roll(x, 64, 1)
+    rows = scratch[pl.ds(0, n * 32), :].reshape(n, 2, 16, 128)
+    other = pltpu.roll(rows[:, 1].reshape(n * 16, 128), 64, 1).reshape(n, 16, 128)
+    return jnp.where(lower((n, 16, 128)), rows[:, 0], other)
+
+
+def to_own_order(x, scratch):
+    n = x.shape[0]
+    turned = pltpu.roll(x.reshape(n * 16, 128), 64, 1).reshape(n, 1, 16, 128)
+    scratch[pl.ds(0, n * 32), :] = jnp.concatenate([x.reshape(n, 1, 16, 128), turned], 1).reshape(n * 32, 128)
+    even = scratch[pl.ds(0, n * 16, stride=2), :]
+    odd = pltpu.roll(scratch[pl.ds(1, n * 16, stride=2), :], 64, 1)
+    return jnp.where(lower((n * 16, 128)), even, odd).reshape(n, 16, 128)
+
+
+def fold(x):
+    n = x.shape[0] // 32
+    x = x.reshape(n, 2, 16, 128)
+    return jnp.where(lower((n, 16, 128)), x[:, 0], x[:, 1])
 
 
 def own_mask(pos, sizes, slot, local, nodes):
     row = lax.broadcasted_iota(jnp.int32, (16, 128), 0)
     lane = lax.broadcasted_iota(jnp.int32, (16, 128), 1)
-    row_id = pos[0] * 32 + 2 * row + (lane >= 64).astype(jnp.int32)
+    row_id = pos[0] * 32 + row + 16 * (lane >= 64).astype(jnp.int32)
     limit = jnp.where(local * 16 + pos[1] < nodes, sizes[slot], 0)
     return row_id < limit
 
@@ -95,7 +108,7 @@
     recv = None
     if height > 0:
         recv, *refs = refs
-    rhs, inverse, out, scratch = refs
+    rhs, inverse, out = refs
     s = pl.program_id(0)
     z = rhs[0]
     if recv is not None:
@@ -105,9 +118,10 @@
         z = z - total
     keep = own_mask(pos, sizes, slot_base + s, s, NODES[height])
     z = jnp.where(keep, z, 0.0)
-    z = unfold(z, scratch)
-    part = dot3(inverse[0, 0], z, ((0,), (0,)))
-    out[:, 0] = fold(part, scratch).reshape(16, 16, 128)
+    turned = pltpu.roll(z, 64, 1)
+    low = lower((16, 128))
+    twice = jnp.concatenate([jnp.where(low, z, turned), jnp.where(low, turned, z)], 0)
+    out[:, 0] = fold(dot3(inverse[0, 0], twice, ((0,), (0,))))
 
 
 def solved_kernel(height, slots, slot_base, pos, parent, pattern, sizes, recv, out, sol):
@@ -139,21 +153,28 @@
         for i, ref in enumerate(after):
             ref[...] = before[i][...] if before else jnp.zeros_like(ref)
 
-    x = unfold(gathered[:, 0].reshape(256, 128), scratch)
+    x = gathered[:, 0].reshape(256, 128)
     slot = slot_base + s
     if whole:
-        y_t = dot3(x.T, inverse[:, 0].reshape(512, 512), ((1,), (0,)))
+        turned = x.T
+        z_t = jnp.concatenate([turned[:64], turned[64:]], 1)
+        rows = inverse[:, 0].reshape(16, 2, 16, 512)
+        rows = jnp.concatenate([rows[:, 0].reshape(256, 512), rows[:, 1].reshape(256, 512)], 0)
+        y_t = dot3(z_t, rows, ((1,), (0,)))
         limit = sizes[slot]
         y_t = jnp.where(lax.broadcasted_iota(jnp.int32, (64, 512), 1) < limit, y_t, 0.0)
-        y = y_t.T
-        scratch[...] = jnp.concatenate([y, y], 1)
-        own = scratch[pl.ds(pl.multiple_of(pos[0] * 32, 32), 32), :]
-        sol[0] = fold(own[:, :64], scratch)
+        scratch[pl.ds(0, 64), :] = y_t
+        lanes = scratch[pl.ds(0, 64), pl.ds(pl.multiple_of(pos[0] // 4 * 128, 128), 128)]
+        own = jnp.concatenate([lanes, lanes], 0).T
+        scratch[pl.ds(64, 128), pl.ds(0, 128)] = own
+        own = scratch[pl.ds(pl.multiple_of(64 + pos[0] % 4 * 32, 32), 32), pl.ds(0, 128)]
+        sol[...] = fold(own)
     else:
-        y_t = x.T
+        turned = pltpu.roll(x, 64, 1).reshape(16, 1, 16, 128)
+        y_t = jnp.concatenate([x.reshape(16, 1, 16, 128), turned], 1).reshape(512, 128).T[:64]
     if reach:
         block = panels[0, 0].reshape(reach * 32, 512)
-        update = fold(dot3(block, y_t, ((1,), (1,))), scratch)
+        update = fold(dot3(block, jnp.concatenate([y_t, y_t], 0), ((1,), (1,))))
         node = NODE_BASE[height] + jnp.minimum(s * 16 + pos[1], NODES[height] - 1)
         for d in range(reach):
             node = parent[node]
@@ -161,14 +182,16 @@
             j = node - NODE_BASE[target]
             where = (j % 16) * max(1, NODES[target] // 16) + j // 16
             scale = pattern[slot * 7 + d].astype(jnp.float32)
-            after[d][where] += scale * update[d * 16 : (d + 1) * 16]
-
-
-def pack_kernel(pos, parent, pattern, sizes, inv5, inv6, inv7, panel5, panel6, *refs):
-    half = len(refs) // 2
-    for source, target in zip(refs[:half], refs[half + 1 :]):
+            after[d][where] += scale * update[d]
+
+
+def pack_kernel(pos, parent, pattern, sizes, sides, inv5, inv6, inv7, panel5, panel6, *refs):
+    *refs, scratch = refs
+    half = len(refs) // 2 - 1
+    folded, out = refs[half : half + 2]
+    folded[...] = from_own_order(sides[...], scratch)
+    for source, target in zip(refs[:half], refs[half + 2 :]):
         target[...] = source[:, 0]
-    out = refs[half]
     for level, inv, panel, at in ((0, inv5, panel5, 3), (1, inv6, panel6, 0), (2, inv7, None, 2)):
         slot = 16 + level
         size = sizes[slot]
@@ -192,8 +215,8 @@
     for level, ref in enumerate((p5, p6, p7)):
         for j in range(4 >> level):
             piece = ref[j] - jnp.where(pos[1] == j, rhs[16 + level], 0.0)
-            scratch[pl.ds(at * 32, 16, stride=2), :] = piece
-            scratch[pl.ds(at * 32 + 1, 16, stride=2), :] = pltpu.roll(piece, 64, 1)
+            scratch[pl.ds(at * 32, 16), :] = piece
+            scratch[pl.ds(at * 32 + 16, 16), :] = pltpu.roll(piece, 64, 1)
             at += 1
     scratch[pl.ds(224, 32), :] = jnp.zeros((32, 128), jnp.float32)
     turned = scratch[pl.ds(0, 256), :].T
@@ -216,7 +239,7 @@
     return jnp.where(lane == level, pltpu.roll(lanes, level * 32, 1), own)
 
 
-def low_kernel(pos, parent, pattern, sizes, recv, block, out, left, z, y):
+def low_kernel(pos, parent, pattern, sizes, recv, block, out, left, z):
     step = pl.program_id(0)
 
     @pl.when(step == 0)
@@ -235,23 +258,14 @@
                     left[n - 4, :, g * 128 : (g + 1) * 128] = jnp.where(pos[1] % 2 == 0, -whole, 0.0)
         out[...] = jnp.zeros_like(out)
 
-    node, kind = step // 3, step % 3
-    matrix = block[:, 0].reshape(512, 256)
-
-    @pl.when(kind == 0)
-    def _():
-        solved = dot3(z[node], matrix, ((1,), (0,)))
-        y[...] = solved
-        out[node] = place(out[node], solved, 0, pos)
-
-    @pl.when(kind > 0)
-    def _():
-        update = dot3(y[...], matrix, ((1,), (1,)))
-        target = jnp.where(kind == 1, parent[NODE_BASE[TOP] + node] - NODE_BASE[TOP + 1], 2)
-        left[target] = left[target] - update
-
-
-def middle_kernel(pos, parent, pattern, sizes, left, other, before, block, out, after, y):
+    solved = dot3(z[step], block[:, 0].reshape(512, 256), ((1,), (0,)))
+    out[step] = place(out[step], solved, 0, pos)
+    target = parent[NODE_BASE[TOP] + step] - NODE_BASE[TOP + 1]
+    left[target] = left[target] - dot3(solved, block[:, 1].reshape(512, 256), ((1,), (1,)))
+    left[2] = left[2] - dot3(solved, block[:, 2].reshape(512, 256), ((1,), (1,)))
+
+
+def middle_kernel(pos, parent, pattern, sizes, left, other, before, block, out, after):
     step = pl.program_id(0)
 
     @pl.when(step == 0)
@@ -259,18 +273,9 @@
         out[...] = before[...]
         after[...] = left[2]
 
-    node, kind = step // 2, step % 2
-    matrix = block[:, 0].reshape(512, 256)
-
-    @pl.when(kind == 0)
-    def _():
-        solved = dot3(left[node] + other[node], matrix, ((1,), (0,)))
-        y[...] = solved
-        out[node] = place(out[node], solved, 1, pos)
-
-    @pl.when(kind > 0)
-    def _():
-        after[...] = after[...] - dot3(y[...], matrix, ((1,), (1,)))
+    solved = dot3(left[step] + other[step], block[:, 0].reshape(512, 256), ((1,), (0,)))
+    out[step] = place(out[step], solved, 1, pos)
+    after[...] = after[...] - dot3(solved, block[:, 1].reshape(512, 256), ((1,), (1,)))
 
 
 def root_kernel(pos, parent, pattern, sizes, left, other, before, block, out):
@@ -279,17 +284,12 @@
     out[0] = place(before[0], solved, 2, pos)
 
 
-def last_kernel(pos, parent, pattern, sizes, recv, out, scratch):
+def last_kernel(pos, parent, pattern, sizes, recv, *refs):
+    *parts, out, scratch = refs
     columns = jnp.concatenate([recv[2 * i + pos[0] // 8] for i in range(8)], 0)
-    scratch[pl.ds(0, 64), :] = columns
-    scratch[pl.ds(64, 64), :] = columns
-    turned = scratch[pl.ds(0, 128), :].T
-    scratch[pl.ds(128, 128), :] = turned
-    lane = lax.broadcasted_iota(jnp.int32, (16, 128), 1)
-    for level in range(3):
-        even = scratch[pl.ds(128 + level * 32, 16, stride=2), :]
-        odd = scratch[pl.ds(129 + level * 32, 16, stride=2), :]
-        out[level] = jnp.where(lane < 64, even, odd)
+    turned = jnp.concatenate([columns, columns], 0).T
+    parts = [ref[...] for ref in parts] + [fold(turned[:96])]
+    out[...] = to_own_order(jnp.concatenate(parts, 0), scratch)
 
 
 def on_device(right_side, inverse_rows, panels, pattern, node_sizes, parent):
@@ -331,21 +331,24 @@
         return spec
 
     spans = list(zip(cuts[:-1], cuts[1:]))
-    top, *wholes = call(
+    all_sides = pl.BlockSpec((19, 16, 128), lambda *_: (0, 0, 0))
+    tall = [pltpu.VMEM((19 * 32, 128), f32)]
+    rhs, top, *wholes = call(
         pack_kernel,
-        [],
+        tall,
         (1,),
-        [block()(0, 16), block()(0, 17), block()(0, 18), block(0)(2, 16), block(0)(1, 17)]
+        [all_sides, block()(0, 16), block()(0, 17), block()(0, 18), block(0)(2, 16), block(0)(1, 17)]
         + [pl.BlockSpec((hi - lo, 1, 32, 512), lambda *_, i=lo // (hi - lo): (i, 0, 0, 0)) for lo, hi in spans],
-        [rows] + [pl.BlockSpec((hi - lo, 32, 512), lambda *_: (0, 0, 0)) for lo, hi in spans],
-        [jax.ShapeDtypeStruct((6, 32, 512), f32)]
+        [all_sides, rows] + [pl.BlockSpec((hi - lo, 32, 512), lambda *_: (0, 0, 0)) for lo, hi in spans],
+        [jax.ShapeDtypeStruct((19, 16, 128), f32), jax.ShapeDtypeStruct((6, 32, 512), f32)]
         + [jax.ShapeDtypeStruct((hi - lo, 32, 512), f32) for lo, hi in spans],
         {},
+        rhs,
         *[inverse_rows] * 3,
         *[panels] * 2,
         *[inverse_rows] * len(spans),
     )
-    inverses = [(lo, lax.all_gather(part, "prow", axis=0)) for lo, part in zip(cuts[:-1], wholes)]
+    top = lax.all_gather(top, "pcol", axis=0)
     for height in range(TOP):
         count = slot_counts[height]
         base = bases[height]
@@ -371,11 +374,11 @@
             args = [rhs, inverse_rows]
             if height > 0:
                 in_specs, args = [one] + in_specs, [recv] + args
-            parts = call(functools.partial(partial_kernel, *info), SCRATCH, (count,), in_specs, one, piece, {}, *args)
+            parts = call(functools.partial(partial_kernel, *info), [], (count,), in_specs, one, piece, {}, *args)
             parts = exchange(parts, "prow")
             if height == 0:
-                top, parts = lax.optimization_barrier((top, parts))
-                top = lax.all_gather(top, "pcol", axis=0)
+                wholes, parts = lax.optimization_barrier((wholes, parts))
+                inverses = [(lo, lax.all_gather(part, "prow", axis=0)) for lo, part in zip(cuts[:-1], wholes)]
             y, sol = call(
                 functools.partial(solved_kernel, *info), [], (1,), [every], [every, every_own], [piece, own], {}, parts
             )
@@ -436,7 +439,7 @@
     sides_shape = jax.ShapeDtypeStruct((16, 8, 256), f32)
     turned = call(
         turn_kernel,
-        SCRATCH,
+        [pltpu.VMEM((256, 128), f32)],
         (1,),
         [many] * 3 + [pl.BlockSpec((19, 16, 128), lambda *_: (0, 0, 0))],
         sides,
@@ -447,8 +450,8 @@
     )
     total = call(sum_kernel, [], (1,), [sides], sides, sides_shape, {}, exchange(turned, "pcol"))
     gathered = exchange(total, "prow")
-    def halves_from(start):
-        return pl.BlockSpec((16, 1, 32, 256), lambda s, *_: (0, start + s, 0, 0))
+    def halves_from(start, n):
+        return pl.BlockSpec((16, n, 32, 256), lambda s, *_: (0, start // n + s, 0, 0))
 
     def whole_of(*shape):
         return pl.BlockSpec(shape, lambda *_: (0,) * len(shape)), jax.ShapeDtypeStruct(shape, f32)
@@ -459,12 +462,11 @@
     found, found_shape = whole_of(16, 8, 128)
     three, three_shape = whole_of(3, 8, 512)
     single, single_shape = whole_of(8, 512)
-    half_y = pltpu.VMEM((8, 256), f32)
     solved, left = call(
         low_kernel,
-        [pltpu.VMEM((4, 8, 512), f32), half_y],
-        (12,),
-        [sides, halves_from(0)],
+        [pltpu.VMEM((4, 8, 512), f32)],
+        (4,),
+        [sides, halves_from(0, 3)],
         [found, three],
         [found_shape, three_shape],
         {},
@@ -473,9 +475,9 @@
     )
     solved, left = call(
         middle_kernel,
-        [half_y],
-        (4,),
-        [three, three, found, halves_from(12)],
+        [],
+        (2,),
+        [three, three, found, halves_from(12, 2)],
         [found, single],
         [found_shape, single_shape],
         {},
@@ -488,7 +490,7 @@
         root_kernel,
         [],
         (1,),
-        [single, single, found, halves_from(16)],
+        [single, single, found, halves_from(16, 1)],
         found,
         found_shape,
         {},
@@ -497,19 +499,18 @@
         solved,
         top,
     )
-    outputs.append(
-        call(
-            last_kernel,
-            SCRATCH,
-            (1,),
-            [pl.BlockSpec((16, 8, 128), lambda *_: (0, 0, 0))],
-            pl.BlockSpec((3, 16, 128), lambda *_: (0, 0, 0)),
-            jax.ShapeDtypeStruct((3, 16, 128), f32),
-            {},
-            exchange(solved, "pcol"),
-        )
-    )
-    return jnp.concatenate(outputs, 0).reshape(19, 1, 2048)
+    out = call(
+        last_kernel,
+        tall,
+        (1,),
+        [found] + [pl.BlockSpec(x.shape, lambda *_: (0, 0, 0)) for x in outputs],
+        all_sides,
+        jax.ShapeDtypeStruct((19, 16, 128), f32),
+        {},
+        exchange(solved, "pcol"),
+        *outputs,
+    )
+    return out.reshape(19, 1, 2048)
 
 
 def solution(mesh):

time: 298 us -> 288 us (0.966)
  blocking collectives: 176 us -> 202 us
  waiting for transfers between devices: 35.7 us -> 13.1 us
  starting transfers between devices: 12.5 us -> 4.94 us
  Pallas kernels: 56.7 us -> 50.5 us
    all_to_all x10 -> x13, blocking collectives: 176 us -> 202 us  [exchange(): return lax.all_to_all(x, axis, 0, 0, tiled=True)]
    all_gather x1, waiting for transfers between devices: 18.7 us -> 0.01 us  [on_device(): top = lax.all_gather(top, 'pcol', axis=0)]
    all_to_all x3 -> x1, starting transfers between devices: 11.1 us -> 3.53 us  [exchange(): return lax.all_to_all(x, axis, 0, 0, tiled=True)]
    pallas_call x19 -> x20, Pallas kernels: 56.7 us -> 50.5 us  [call(): pl.pallas_call(functools.partial(with_parts, kernel), grid_spec=pltpu.Pre...]
    all_to_all x3 -> x1, waiting for transfers between devices: 15.2 us -> 11.3 us  [exchange(): return lax.all_to_all(x, axis, 0, 0, tiled=True)]
  transfers between devices with their start and end apart: 8 -> 6, of which waited for: 5 -> 3; matrix products, arithmetic and copies ran while one was open for 0% -> 0% of each run, Pallas kernels for 12% -> 13%
where the time goes in v3:
time: 288 us; the launch traced here: 286 us
  blocking collectives  202 us (70%)
  Pallas kernels  50.5 us (18%)
  between operations  13.2 us (5%)
  waiting for transfers between devices  13.1 us (5%)
  starting transfers between devices  4.94 us (2%)
    all_to_all x13, blocking collectives, exchange(): return lax.all_to_all(x, axis, 0, 0, tiled=True)  202 us
    pallas_call x20, Pallas kernels, call(): pl.pallas_call(functools.partial(with_parts, kernel), grid_spec=pltpu.Pre...  50.5 us
    all_to_all x1, waiting for transfers between devices, exchange(): return lax.all_to_all(x, axis, 0, 0, tiled=True)  11.3 us
  transfers between devices with their start and end apart: 6, of which 3 were waited for; matrix products, arithmetic and copies ran while one was open for 0% of the time, Pallas kernels for 13%

profile of v3, /device:TPU:1, one launch (start us, length us, event | category | flops | bytes accessed | tf_op | source)
XLA Modules:
  0.0 286.2 jit_solution(9582988495440856246)
XLA Ops:
  9.1 2.7 shard_map.64
  11.9 5.7 %shard_map.65 = f32[16,8,16,128]{3,2,1,0:T(8,128)S(1)} custom-call(s32[408]{0:T(512)S(1)} %concatenate.3.refs_0_, f32[19,16,128]{2,1,0:T(8,128)S(1)} %get-tuple-element.50.refs_1_.refs_2_.refs_4_, f32[19,1,32,512]{3,2,1,0:T(8,128)} %refs_3_.6), custom_call_target="tpu_custom_call" | custom-call | tf_op jit(solution)/shard_map/pallas_call | solution.py:303
  17.5 23.5 %all_to_all.70.refs_1_ = f32[16,8,16,128]{3,2,1,0:T(8,128)S(1)} all-to-all(f32[16,8,16,128]{3,2,1,0:T(8,128)S(1)} %shard_map.65), channel_id=1, replica_groups=mesh['prow'=16,'pcol'=16] {'prow'}, dimensions={0} | all-to-all | bytes 2097152 | tf_op jit(solution)/shard_map/all_to_all | solution.py:318
  41.8 19.0 %all_to_all.71.refs_1_ = f32[16,8,16,128]{3,2,1,0:T(8,128)S(1)} all-to-all(f32[16,8,16,128]{3,2,1,0:T(8,128)S(1)} %get-tuple-element.52), channel_id=1, replica_groups=mesh['prow'=16,'pcol'=16] {'prow'}, dimensions={0} | all-to-all | bytes 2097152 | tf_op jit(solution)/shard_map/all_to_all | solution.py:318
  60.8 7.5 %shard_map.67 = (f32[64,16,128]{2,1,0:T(8,128)S(1)}, f32[32,16,128]{2,1,0:T(8,128)S(1)}, f32[16,16,128]{2,1,0:T(8,128)S(1)}, f32[16,16,128]{2,1,0:T(8,128)S(1)},...) custom-call(s32[408]{0:T(512)S(1)} %concatenate.3.refs_0_, ...), custom_call_target="tpu_custom_call" | custom-call | tf_op jit(solution)/shard_map/pallas_call | solution.py:303
  68.2 28.1 %all_to_all.72.refs_1_ = f32[16,4,16,128]{3,2,1,0:T(8,128)S(1)} all-to-all(f32[16,4,16,128]{3,2,1,0:T(8,128)S(1)} %bitcast.17), channel_id=1, replica_groups=mesh['prow'=16,'pcol'=16] {'pcol'}, dimensions={0} | all-to-all | bytes 1048576 | tf_op jit(solution)/shard_map/all_to_all | solution.py:318
  96.3 3.4 %shard_map.68 = f32[16,4,16,128]{3,2,1,0:T(8,128)S(1)} custom-call(s32[408]{0:T(512)S(1)} %concatenate.3.refs_0_, f32[16,4,16,128]{3,2,1,0:T(8,128)S(1)} %all_to_all.72.refs_1_, f32[19,16,128]{2,1,0:T(8,128)S(1)} %get-tuple-element.50.refs_1_.refs_2_.refs_4_, f32[19,1,32,512]{3,2,1,0:T(8,128)} %refs_3_.6), custom_call_target="tpu_custom_call" | custom-call | tf_op jit(solution)/shard_map/pallas_call | solution.py:303
  99.7 19.8 %all_to_all.73.refs_1_ = f32[16,4,16,128]{3,2,1,0:T(8,128)S(1)} all-to-all(f32[16,4,16,128]{3,2,1,0:T(8,128)S(1)} %shard_map.68), channel_id=1, replica_groups=mesh['prow'=16,'pcol'=16] {'prow'}, dimensions={0} | all-to-all | bytes 1048576 | tf_op jit(solution)/shard_map/all_to_all | solution.py:318
  120.1 13.8 %all_to_all.74.refs_1_ = f32[16,4,16,128]{3,2,1,0:T(8,128)S(1)} all-to-all(f32[16,4,16,128]{3,2,1,0:T(8,128)S(1)} %get-tuple-element.54), channel_id=1, replica_groups=mesh['prow'=16,'pcol'=16] {'prow'}, dimensions={0} | all-to-all | bytes 1048576 | tf_op jit(solution)/shard_map/all_to_all | solution.py:318
  133.9 4.2 %shard_map.70 = (f32[32,16,128]{2,1,0:T(8,128)S(1)}, f32[16,16,128]{2,1,0:T(8,128)S(1)}, f32[16,16,128]{2,1,0:T(8,128)S(1)}, f32[16,16,128]{2,1,0:T(8,128)S(1)},...) custom-call(s32[408]{0:T(512)S(1)} %concatenate.3.refs_0_, ...), custom_call_target="tpu_custom_call", output_to_operand_aliasing={{0}: (3, {}), {1}: (4, {}), {2}: (5, {}), {3}: (6, {}), {4}... | custom-call | tf_op jit(solution)/shard_map/pallas_call | solution.py:303
  138.1 17.4 %all_to_all.75.refs_1_ = f32[16,2,16,128]{3,2,1,0:T(8,128)S(1)} all-to-all(f32[16,2,16,128]{3,2,1,0:T(8,128)S(1)} %bitcast.16), channel_id=1, replica_groups=mesh['prow'=16,'pcol'=16] {'pcol'}, dimensions={0} | all-to-all | bytes 524288 | tf_op jit(solution)/shard_map/all_to_all | solution.py:318
  159.2 3.5 %all-to-all-start.6 = ((f32[16,2,16,128]{3,2,1,0:T(8,128)}), f32[16,2,16,128]{3,2,1,0:T(8,128)S(1)}, u32[]{:S(2)}, u32[]{:S(2)}) async-start(f32[16,2,16,128]{3,2,1,0:T(8,128)} %shard_map.71), calls=%async_computation.6 | async-start | bytes 524288 | tf_op jit(solution)/shard_map/all_to_all | solution.py:318
  162.8 11.3 %all-to-all-done.6.refs_1_ = f32[16,2,16,128]{3,2,1,0:T(8,128)S(1)} async-done(((f32[16,2,16,128]{3,2,1,0:T(8,128)}), f32[16,2,16,128]{3,2,1,0:T(8,128)S(1)}, u32[]{:S(2)}, u32[]{:S(2)}) %all-to-all-start.6) | async-done | bytes 262176 | tf_op jit(solution)/shard_map/all_to_all | solution.py:318
  174.1 3.3 %shard_map.72 = (f32[2,16,128]{2,1,0:T(8,128)S(1)}, f32[16,16,128]{2,1,0:T(8,128)S(1)}, f32[16,16,128]{2,1,0:T(8,128)S(1)}, f32[16,16,128]{2,1,0:T(8,128)S(1)}, ...) custom-call(s32[408]{0:T(512)S(1)} %concatenate.3.refs_0_, ...), custom_call_target="tpu_custom_call", output_to_operand_aliasing={{1}: (4, {}), {2}: (5, {}), {3}: (6, {}), {4}: (7, {}), {5}... | custom-call | tf_op jit(solution)/shard_map/pallas_call | solution.py:303
  177.3 12.1 %all_to_all.76.refs_1_ = f32[16,1,16,128]{3,2,1,0:T(8,128)S(1)} all-to-all(f32[16,1,16,128]{3,2,1,0:T(8,128)S(1)} %bitcast.15), channel_id=1, replica_groups=mesh['prow'=16,'pcol'=16] {'pcol'}, dimensions={0} | all-to-all | bytes 262144 | tf_op jit(solution)/shard_map/all_to_all | solution.py:318
  190.0 11.7 %all_to_all.77.refs_1_ = f32[16,1,16,128]{3,2,1,0:T(8,128)S(1)} all-to-all(f32[16,1,16,128]{3,2,1,0:T(8,128)S(1)} %shard_map.73), channel_id=1, replica_groups=mesh['prow'=16,'pcol'=16] {'prow'}, dimensions={0} | all-to-all | bytes 262144 | tf_op jit(solution)/shard_map/all_to_all | solution.py:318
  201.8 2.6 shard_map.74
  204.4 12.2 %all_to_all.78.refs_1_ = f32[16,1,16,128]{3,2,1,0:T(8,128)S(1)} all-to-all(f32[16,1,16,128]{3,2,1,0:T(8,128)S(1)} %bitcast.14), channel_id=1, replica_groups=mesh['prow'=16,'pcol'=16] {'pcol'}, dimensions={0} | all-to-all | bytes 262144 | tf_op jit(solution)/shard_map/all_to_all | solution.py:318
  217.1 11.7 %all_to_all.79.refs_1_ = f32[16,1,16,128]{3,2,1,0:T(8,128)S(1)} all-to-all(f32[16,1,16,128]{3,2,1,0:T(8,128)S(1)} %shard_map.75), channel_id=1, replica_groups=mesh['prow'=16,'pcol'=16] {'prow'}, dimensions={0} | all-to-all | bytes 262144 | tf_op jit(solution)/shard_map/all_to_all | solution.py:318
  228.9 2.6 shard_map.76
  232.2 12.2 %all_to_all.80.refs_1_ = f32[16,8,256]{2,1,0:T(8,128)S(1)} all-to-all(f32[16,8,256]{2,1,0:T(8,128)S(1)} %shard_map.77), channel_id=1, replica_groups=mesh['prow'=16,'pcol'=16] {'pcol'}, dimensions={0} | all-to-all | bytes 262144 | tf_op jit(solution)/shard_map/all_to_all | solution.py:318
  245.0 10.0 %all_to_all.81.refs_1_ = f32[16,8,256]{2,1,0:T(8,128)S(1)} all-to-all(f32[16,8,256]{2,1,0:T(8,128)S(1)} %shard_map.78), channel_id=1, replica_groups=mesh['prow'=16,'pcol'=16] {'prow'}, dimensions={0} | all-to-all | bytes 262144 | tf_op jit(solution)/shard_map/all_to_all | solution.py:318
  255.0 5.2 %shard_map.80 = (f32[16,8,128]{2,1,0:T(8,128)S(1)}, f32[3,8,512]{2,1,0:T(8,128)S(1)}) custom-call(s32[408]{0:T(512)S(1)} %concatenate.3.refs_0_, f32[16,8,256]{2,1,0:T(8,128)S(1)} %all_to_all.81.refs_1_, f32[16,17,32,256]{3,2,1,0:T(8,128)} %bitcast.19), custom_call_target="tpu_custom_call" | custom-call | tf_op jit(solution)/shard_map/pallas_call | solution.py:303
  267.6 10.6 %all_to_all.82.refs_1_ = f32[16,8,128]{2,1,0:T(8,128)S(1)} all-to-all(f32[16,8,128]{2,1,0:T(8,128)S(1)} %shard_map.82), channel_id=1, replica_groups=mesh['prow'=16,'pcol'=16] {'pcol'}, dimensions={0} | all-to-all | bytes 131072 | tf_op jit(solution)/shard_map/all_to_all | solution.py:318
  (29 shorter events, 19.2 us)
Async XLA Ops:
  6.5 148.9 %all-gather.7.cloned.1.call-start = ((), (), s32[]{:S(2)}) async-start(), calls=%async_computation.14 | async-start | bytes 6684672 | tf_op jit(solution)/shard_map/all_gather | solution.py:351
  8.2 0.9 copy-start
  11.8 151.0 %all-gather.9.cloned.1.call-start = ((), (), s32[]{:S(2)}) async-start(), calls=%async_computation.15 | async-start | bytes 4456448 | tf_op jit(solution)/shard_map/all_gather | solution.py:381
  41.1 213.9 %all-gather.11.cloned.1.call-start = ((), (), s32[]{:S(2)}) async-start(), calls=%async_computation.16 | async-start | bytes 9469952 | tf_op jit(solution)/shard_map/all_gather | solution.py:436
  159.2 14.8 %all-to-all-start.6 = ((f32[16,2,16,128]{3,2,1,0:T(8,128)}), f32[16,2,16,128]{3,2,1,0:T(8,128)S(1)}, u32[]{:S(2)}, u32[]{:S(2)}) async-start(f32[16,2,16,128]{3,2,1,0:T(8,128)} %shard_map.71), calls=%async_computation.6 | async-start | bytes 524288 | tf_op jit(solution)/shard_map/all_to_all | solution.py:318
  260.2 1.8 collective-permute-start
  264.4 1.3 collective-permute-start.1
Sparse Core Ops, SparseCore 0:
  11.9 50.2 all-gather.6
  64.7 60.5 all-gather.8
  158.1 73.5 all-gather.10

commit v4 on v3

--- a/solution.py
+++ b/solution.py
@@ -109,19 +109,20 @@
     if height > 0:
         recv, *refs = refs
     rhs, inverse, out = refs
-    s = pl.program_id(0)
-    z = rhs[0]
-    if recv is not None:
-        total = recv[0, 0]
-        for i in range(1, 16):
-            total = total + recv[i, 0]
-        z = z - total
-    keep = own_mask(pos, sizes, slot_base + s, s, NODES[height])
-    z = jnp.where(keep, z, 0.0)
-    turned = pltpu.roll(z, 64, 1)
     low = lower((16, 128))
-    twice = jnp.concatenate([jnp.where(low, z, turned), jnp.where(low, turned, z)], 0)
-    out[:, 0] = fold(dot3(inverse[0, 0], twice, ((0,), (0,))))
+    for i in range(rhs.shape[0]):
+        s = pl.program_id(0) * rhs.shape[0] + i
+        z = rhs[i]
+        if recv is not None:
+            total = recv[0, i]
+            for k in range(1, recv.shape[0]):
+                total = total + recv[k, i]
+            z = z - total
+        keep = own_mask(pos, sizes, slot_base + s, s, NODES[height])
+        z = jnp.where(keep, z, 0.0)
+        turned = pltpu.roll(z, 64, 1)
+        twice = jnp.concatenate([jnp.where(low, z, turned), jnp.where(low, turned, z)], 0)
+        out[:, i] = fold(dot3(inverse[i, 0], twice, ((0,), (0,))))
 
 
 def solved_kernel(height, slots, slot_base, pos, parent, pattern, sizes, recv, out, sol):
@@ -136,53 +137,66 @@
             out[i, s] = y
 
 
-def spread_kernel(height, slots, slot_base, whole, pos, parent, pattern, sizes, *refs):
-    reach = LEVELS - 1 - height
+def spread_kernel(height, slots, slot_base, source, first, end, pos, parent, pattern, sizes, *refs):
     refs = list(refs)
-    gathered = refs.pop(0)
-    inverse = refs.pop(0) if whole else None
-    panels = refs.pop(0) if reach else None
-    before = [refs.pop(0) for _ in range(reach)] if height > 0 else []
-    sol = refs.pop(0) if whole else None
-    after = [refs.pop(0) for _ in range(reach)]
+    given = refs.pop(0)
+    inverse = refs.pop(0) if source == "z" else None
+    panels = refs.pop(0)
+    before = [refs.pop(0) for _ in range(first, end)] if height > 0 else []
+    sol = refs.pop(0) if source == "z" else None
+    kept = refs.pop(0) if source == "z" and end < LEVELS - 1 - height else None
+    after = [refs.pop(0) for _ in range(first, end)]
     scratch = refs.pop(0)
-    s = pl.program_id(0)
-
-    @pl.when(s == 0)
+
+    @pl.when(pl.program_id(0) == 0)
     def _():
         for i, ref in enumerate(after):
             ref[...] = before[i][...] if before else jnp.zeros_like(ref)
 
-    x = gathered[:, 0].reshape(256, 128)
-    slot = slot_base + s
-    if whole:
-        turned = x.T
-        z_t = jnp.concatenate([turned[:64], turned[64:]], 1)
-        rows = inverse[:, 0].reshape(16, 2, 16, 512)
-        rows = jnp.concatenate([rows[:, 0].reshape(256, 512), rows[:, 1].reshape(256, 512)], 0)
-        y_t = dot3(z_t, rows, ((1,), (0,)))
-        limit = sizes[slot]
-        y_t = jnp.where(lax.broadcasted_iota(jnp.int32, (64, 512), 1) < limit, y_t, 0.0)
-        scratch[pl.ds(0, 64), :] = y_t
-        lanes = scratch[pl.ds(0, 64), pl.ds(pl.multiple_of(pos[0] // 4 * 128, 128), 128)]
-        own = jnp.concatenate([lanes, lanes], 0).T
-        scratch[pl.ds(64, 128), pl.ds(0, 128)] = own
-        own = scratch[pl.ds(pl.multiple_of(64 + pos[0] % 4 * 32, 32), 32), pl.ds(0, 128)]
-        sol[...] = fold(own)
-    else:
-        turned = pltpu.roll(x, 64, 1).reshape(16, 1, 16, 128)
-        y_t = jnp.concatenate([x.reshape(16, 1, 16, 128), turned], 1).reshape(512, 128).T[:64]
-    if reach:
-        block = panels[0, 0].reshape(reach * 32, 512)
+    for k in range(panels.shape[0]):
+        s = pl.program_id(0) * panels.shape[0] + k
+        slot = slot_base + s
+        if source == "z":
+            turned = given[:, k].reshape(256, 128).T
+            z_t = jnp.concatenate([turned[:64], turned[64:]], 1)
+            rows = inverse[:, k].reshape(16, 2, 16, 512)
+            rows = jnp.concatenate([rows[:, 0].reshape(256, 512), rows[:, 1].reshape(256, 512)], 0)
+            y_t = dot3(z_t, rows, ((1,), (0,)))
+            limit = sizes[slot]
+            y_t = jnp.where(lax.broadcasted_iota(jnp.int32, (64, 512), 1) < limit, y_t, 0.0)
+            scratch[pl.ds(0, 64), :] = y_t
+            lanes = scratch[pl.ds(0, 64), pl.ds(pl.multiple_of(pos[0] // 4 * 128, 128), 128)]
+            own = jnp.concatenate([lanes, lanes], 0).T
+            scratch[pl.ds(64, 128), pl.ds(0, 128)] = own
+            own = scratch[pl.ds(pl.multiple_of(64 + pos[0] % 4 * 32, 32), 32), pl.ds(0, 128)]
+            sol[k] = fold(own)[0]
+            if kept is not None:
+                kept[k] = y_t
+        elif source == "y":
+            x = given[:, k].reshape(256, 128)
+            turned = pltpu.roll(x, 64, 1).reshape(16, 1, 16, 128)
+            y_t = jnp.concatenate([x.reshape(16, 1, 16, 128), turned], 1).reshape(512, 128).T[:64]
+        else:
+            y_t = given[k]
+        block = panels[k, 0, first:end].reshape((end - first) * 32, 512)
         update = fold(dot3(block, jnp.concatenate([y_t, y_t], 0), ((1,), (1,))))
         node = NODE_BASE[height] + jnp.minimum(s * 16 + pos[1], NODES[height] - 1)
-        for d in range(reach):
+        for d in range(end):
             node = parent[node]
+            if d < first:
+                continue
             target = height + 1 + d
             j = node - NODE_BASE[target]
-            where = (j % 16) * max(1, NODES[target] // 16) + j // 16
+            if target == 1:
+                where = ((j + pos[1]) % 2 * 8 + j % 16 // 2) * 4 + j // 16
+            else:
+                where = (j % 16) * max(1, NODES[target] // 16) + j // 16
             scale = pattern[slot * 7 + d].astype(jnp.float32)
-            after[d][where] += scale * update[d]
+            after[d - first][where] += scale * update[d - first]
+
+
+def join_kernel(pos, parent, pattern, sizes, here, there, out):
+    out[...] = (here[...] + there[...]).reshape(out.shape)
 
 
 def pack_kernel(pos, parent, pattern, sizes, sides, inv5, inv6, inv7, panel5, panel6, *refs):
@@ -359,7 +373,6 @@
         own = jax.ShapeDtypeStruct((count, 16, 128), f32)
         every = pl.BlockSpec((16, count, 16, 128), lambda *_: (0, 0, 0, 0))
         every_own = pl.BlockSpec((count, 16, 128), lambda *_: (0, 0, 0))
-        one = pl.BlockSpec((16, 1, 16, 128), lambda s, *_: (0, s, 0, 0))
         rhs_all = pl.BlockSpec((count, 16, 128), lambda *_, b=base // count: (b, 0, 0))
         if whole:
             z = call(
@@ -367,14 +380,18 @@
             )
             gathered = exchange(z, "prow")
         else:
+            per = min(4, count)
             in_specs = [
-                pl.BlockSpec((1, 16, 128), lambda s, *_, b=base: (b + s, 0, 0)),
-                pl.BlockSpec((1, 1, 32, 512), lambda s, *_, b=base: (b + s, 0, 0, 0)),
+                pl.BlockSpec((per, 16, 128), lambda s, *_, b=base // per: (b + s, 0, 0)),
+                pl.BlockSpec((per, 1, 32, 512), lambda s, *_, b=base // per: (b + s, 0, 0, 0)),
             ]
             args = [rhs, inverse_rows]
             if height > 0:
-                in_specs, args = [one] + in_specs, [recv] + args
-            parts = call(functools.partial(partial_kernel, *info), [], (count,), in_specs, one, piece, {}, *args)
+                in_specs = [pl.BlockSpec((recv.shape[0], per, 16, 128), lambda s, *_: (0, s, 0, 0))] + in_specs
+                args = [recv] + args
+            some = pl.BlockSpec((16, per, 16, 128), lambda s, *_: (0, s, 0, 0))
+            kernel = functools.partial(partial_kernel, *info)
+            parts = call(kernel, [], (count // per,), in_specs, some, piece, {}, *args)
             parts = exchange(parts, "prow")
             if height == 0:
                 wholes, parts = lax.optimization_barrier((wholes, parts))
@@ -384,39 +401,83 @@
             )
             outputs.append(sol)
             gathered = exchange(y, "prow")
-        in_specs, args = [one], [gathered]
-        out_specs, out_shape = [], []
-        if whole:
-            lo, inverse = [pair for pair in inverses if pair[0] <= base][-1]
-            in_specs.append(pl.BlockSpec((16, 1, 32, 512), lambda s, *_, b=base - lo: (0, b + s, 0, 0)))
-            args.append(inverse)
-            out_specs.append(pl.BlockSpec((1, 16, 128), lambda s, *_: (s, 0, 0)))
-            out_shape.append(own)
-        if reach:
+        steps = [(0, 1), (1, reach)] if height + 1 < TOP else [(0, reach)]
+        updated = []
+        given, source = gathered, "z" if whole else "y"
+        for start, end in steps:
+            per = 1 if source == "z" else min(2, count)
+            in_specs = [pl.BlockSpec((16, per, 16, 128), lambda s, *_: (0, s, 0, 0))]
+            if source == "t":
+                in_specs = [pl.BlockSpec((per, 64, 512), lambda s, *_: (s, 0, 0))]
+            args = [given]
+            out_specs, out_shape = [], []
+            if source == "z":
+                lo, inverse = [pair for pair in inverses if pair[0] <= base][-1]
+                in_specs.append(pl.BlockSpec((16, 1, 32, 512), lambda s, *_, b=base - lo: (0, b + s, 0, 0)))
+                args.append(inverse)
+                out_specs.append(pl.BlockSpec((1, 16, 128), lambda s, *_: (s, 0, 0)))
+                out_shape.append(own)
+                if end < reach:
+                    out_specs.append(pl.BlockSpec((1, 64, 512), lambda s, *_: (s, 0, 0)))
+                    out_shape.append(jax.ShapeDtypeStruct((count, 64, 512), f32))
             in_specs.append(
-                pl.BlockSpec((1, 1, reach, 32, 512), lambda s, *_, b=base: (b + s, 0, 0, 0, 0))
+                pl.BlockSpec((per, 1, end, 32, 512), lambda s, *_, b=base // per: (b + s, 0, 0, 0, 0))
             )
             args.append(panels)
-        aliases = {}
-        for d in range(reach):
-            shape = (16 * slot_counts[height + 1 + d], 16, 128)
-            spec = pl.BlockSpec(shape, lambda *_: (0, 0, 0))
-            if height > 0:
-                aliases[len(in_specs)] = len(out_specs)
-                in_specs.append(spec)
-                args.append(pending[d])
-            out_specs.append(spec)
-            out_shape.append(jax.ShapeDtypeStruct(shape, f32))
-        results = call(
-            functools.partial(spread_kernel, *info, whole), SCRATCH, (count,), in_specs, out_specs, out_shape, aliases, *args
-        )
-        results = list(results)
-        if whole:
-            outputs.append(results.pop(0))
+            aliases = {}
+            for d in range(start, end):
+                shape = (16 * slot_counts[height + 1 + d], 16, 128)
+                spec = pl.BlockSpec(shape, lambda *_: (0, 0, 0))
+                if height > 0:
+                    aliases[len(in_specs)] = len(out_specs)
+                    in_specs.append(spec)
+                    args.append(pending[d])
+                out_specs.append(spec)
+                out_shape.append(jax.ShapeDtypeStruct(shape, f32))
+            results = call(
+                functools.partial(spread_kernel, *info, source, start, end),
+                SCRATCH,
+                (count // per,),
+                in_specs,
+                out_specs,
+                out_shape,
+                aliases,
+                *args,
+            )
+            results = list(results)
+            if source == "z":
+                outputs.append(results.pop(0))
+                if end < reach:
+                    given, source = results.pop(0), "t"
+            updated += results
+        results = updated
         if height + 1 < TOP:
             following = slot_counts[height + 1]
-            recv = exchange(results[0].reshape(16, following, 16, 128), "pcol")
             pending = results[1:]
+            if height == 0:
+                half = pl.BlockSpec((32, 16, 128), lambda *_: (0, 0, 0))
+                there = lax.ppermute(results[0][32:], "pcol", [(i, i ^ 1) for i in range(16)])
+                joined = call(
+                    join_kernel,
+                    [],
+                    (1,),
+                    [half, half],
+                    pl.BlockSpec((8, 4, 16, 128), lambda *_: (0, 0, 0, 0)),
+                    jax.ShapeDtypeStruct((8, 4, 16, 128), f32),
+                    {},
+                    results[0],
+                    there,
+                )
+                recv = lax.all_to_all(
+                    joined,
+                    "pcol",
+                    0,
+                    0,
+                    tiled=True,
+                    axis_index_groups=[[core + 2 * z for z in range(8)] for core in range(2)],
+                )
+            else:
+                recv = exchange(results[0].reshape(16, following, 16, 128), "pcol")
         if height == 1:
             top, recv = lax.optimization_barrier((top, recv))
             halves = [(4, 3, 0, 1), (2, 2, 0, 0), (1, 1, 0, 2)]

time: 288 us -> 276 us (0.958)
  blocking collectives: 202 us -> 149 us
  waiting for transfers between devices: 13.1 us -> 36.3 us
  starting transfers between devices: 4.94 us -> 18.1 us
  Pallas kernels: 50.5 us -> 55.8 us
    all_to_all x13 -> x9, blocking collectives: 202 us -> 130 us  [exchange(): return lax.all_to_all(x, axis, 0, 0, tiled=True)]
    all_to_all x1 -> x4, waiting for transfers between devices: 11.3 us -> 33.3 us  [exchange(): return lax.all_to_all(x, axis, 0, 0, tiled=True)]
    all_to_all x0 -> x1, blocking collectives: none -> 19.1 us  [on_device(): lax.all_to_all(joined, 'pcol', 0, 0, tiled=True, axis_index_groups=[[core...]
    all_to_all x1 -> x4, starting transfers between devices: 3.53 us -> 14.1 us  [exchange(): return lax.all_to_all(x, axis, 0, 0, tiled=True)]
    pallas_call x20 -> x25, Pallas kernels: 50.5 us -> 55.8 us  [call(): pl.pallas_call(functools.partial(with_parts, kernel), grid_spec=pltpu.Pre...]
  transfers between devices with their start and end apart: 6 -> 10, of which waited for: 3 -> 7; matrix products, arithmetic and copies ran while one was open for 0% -> 0% of each run, Pallas kernels for 13% -> 15%
where the time goes in v4:
time: 276 us; the launch traced here: 275 us
  blocking collectives  149 us (54%)
  Pallas kernels  55.8 us (20%)
  waiting for transfers between devices  36.3 us (13%)
  starting transfers between devices  18.1 us (7%)
  between operations  13.3 us (5%)
    all_to_all x9, blocking collectives, exchange(): return lax.all_to_all(x, axis, 0, 0, tiled=True)  130 us
    pallas_call x25, Pallas kernels, call(): pl.pallas_call(functools.partial(with_parts, kernel), grid_spec=pltpu.Pre...  55.8 us
    all_to_all x4, waiting for transfers between devices, exchange(): return lax.all_to_all(x, axis, 0, 0, tiled=True)  33.3 us
    all_to_all x1, blocking collectives, on_device(): lax.all_to_all(joined, 'pcol', 0, 0, tiled=True, axis_index_groups=[[core...  19.1 us
    all_to_all x4, starting transfers between devices, exchange(): return lax.all_to_all(x, axis, 0, 0, tiled=True)  14.1 us
  transfers between devices with their start and end apart: 10, of which 7 were waited for; matrix products, arithmetic and copies ran while one was open for 0% of the time, Pallas kernels for 15%

profile of v4, /device:TPU:1, one launch (start us, length us, event | category | flops | bytes accessed | tf_op | source)
XLA Modules:
  0.0 275.0 jit_solution(17650437877559766170)
XLA Ops:
  11.8 2.9 %shard_map.65 = f32[16,8,16,128]{3,2,1,0:T(8,128)S(1)} custom-call(s32[408]{0:T(512)S(1)} %concatenate.3.refs_0_, f32[19,16,128]{2,1,0:T(8,128)S(1)} %get-tuple-element.50.refs_1_.refs_2_.refs_4_, f32[19,1,32,512]{3,2,1,0:T(8,128)} %refs_3_.6), custom_call_target="tpu_custom_call" | custom-call | tf_op jit(solution)/shard_map/pallas_call | solution.py:317
  14.7 23.5 %all_to_all.70.refs_1_ = f32[16,8,16,128]{3,2,1,0:T(8,128)S(1)} all-to-all(f32[16,8,16,128]{3,2,1,0:T(8,128)S(1)} %shard_map.65), channel_id=1, replica_groups=mesh['prow'=16,'pcol'=16] {'prow'}, dimensions={0} | all-to-all | bytes 2097152 | tf_op jit(solution)/shard_map/all_to_all | solution.py:332
  38.9 19.0 %all_to_all.71.refs_1_ = f32[16,8,16,128]{3,2,1,0:T(8,128)S(1)} all-to-all(f32[16,8,16,128]{3,2,1,0:T(8,128)S(1)} %get-tuple-element.52), channel_id=1, replica_groups=mesh['prow'=16,'pcol'=16] {'prow'}, dimensions={0} | all-to-all | bytes 2097152 | tf_op jit(solution)/shard_map/all_to_all | solution.py:332
  57.9 4.0 %shard_map.67.refs_1_ = f32[64,16,128]{2,1,0:T(8,128)S(1)} custom-call(s32[408]{0:T(512)S(1)} %concatenate.3.refs_0_, f32[16,8,16,128]{3,2,1,0:T(8,128)S(1)} %all_to_all.71.refs_1_, f32[19,1,7,32,512]{4,3,2,1,0:T(8,128)} %refs_3_.9), custom_call_target="tpu_custom_call" | custom-call | tf_op jit(solution)/shard_map/pallas_call | solution.py:317
  66.3 19.1 %all_to_all.72.refs_1_ = f32[8,4,16,128]{3,2,1,0:T(8,128)S(1)} all-to-all(f32[8,4,16,128]{3,2,1,0:T(8,128)S(1)} %shard_map.68), channel_id=1, replica_groups={{0,2,4,6,8,10,12,14},{1,3,5,7,9,11,13,15},{16,18,20,22,24,26,28,30},{17..., dimensions={0} | all-to-all | bytes 524288 | tf_op jit(solution)/shard_map/all_to_all | solution.py:471
  87.5 12.3 %all_to_all.73.refs_1_ = f32[16,4,16,128]{3,2,1,0:T(8,128)S(1)} all-to-all(f32[16,4,16,128]{3,2,1,0:T(8,128)S(1)} %shard_map.69), channel_id=1, replica_groups=mesh['prow'=16,'pcol'=16] {'prow'}, dimensions={0} | all-to-all | bytes 1048576 | tf_op jit(solution)/shard_map/all_to_all | solution.py:332
  101.2 3.6 %all-to-all-start.4 = ((f32[16,4,16,128]{3,2,1,0:T(8,128)}), f32[16,4,16,128]{3,2,1,0:T(8,128)S(1)}, u32[]{:S(2)}, u32[]{:S(2)}) async-start(f32[16,4,16,128]{3,2,1,0:T(8,128)} %get-tuple-element.53), calls=%async_computation.4 | async-start | bytes 1048576 | tf_op jit(solution)/shard_map/all_to_all | solution.py:332
  104.9 5.2 %shard_map.71 = (f32[32,16,128]{2,1,0:T(8,128)S(1)}, f32[16,16,128]{2,1,0:T(8,128)S(1)}, f32[16,16,128]{2,1,0:T(8,128)S(1)}, f32[16,16,128]{2,1,0:T(8,128)S(1)},...) custom-call(s32[408]{0:T(512)S(1)} %concatenate.3.refs_0_, f32[16,8,16,128]{3,2,1,0:T(8,128)S(1)} %all_to_all.71.refs_1_, ...), custom_call_target="tpu_custom_call" | custom-call | tf_op jit(solution)/shard_map/pallas_call | solution.py:317
  110.1 10.9 %all-to-all-done.4.refs_1_ = f32[16,4,16,128]{3,2,1,0:T(8,128)S(1)} async-done(((f32[16,4,16,128]{3,2,1,0:T(8,128)}), f32[16,4,16,128]{3,2,1,0:T(8,128)S(1)}, u32[]{:S(2)}, u32[]{:S(2)}) %all-to-all-start.4) | async-done | bytes 524320 | tf_op jit(solution)/shard_map/all_to_all | solution.py:332
  123.6 18.2 %all_to_all.74.refs_1_ = f32[16,2,16,128]{3,2,1,0:T(8,128)S(1)} all-to-all(f32[16,2,16,128]{3,2,1,0:T(8,128)S(1)} %bitcast.15), channel_id=1, replica_groups=mesh['prow'=16,'pcol'=16] {'pcol'}, dimensions={0} | all-to-all | bytes 524288 | tf_op jit(solution)/shard_map/all_to_all | solution.py:332
  145.5 3.5 %all-to-all-start.6 = ((f32[16,2,16,128]{3,2,1,0:T(8,128)}), f32[16,2,16,128]{3,2,1,0:T(8,128)S(1)}, u32[]{:S(2)}, u32[]{:S(2)}) async-start(f32[16,2,16,128]{3,2,1,0:T(8,128)} %shard_map.73), calls=%async_computation.6 | async-start | bytes 524288 | tf_op jit(solution)/shard_map/all_to_all | solution.py:332
  149.1 3.1 %shard_map.74 = (f32[16,16,128]{2,1,0:T(8,128)S(1)}, f32[16,16,128]{2,1,0:T(8,128)S(1)}, f32[16,16,128]{2,1,0:T(8,128)S(1)}, f32[16,16,128]{2,1,0:T(8,128)S(1)}, f32[16,16,128]{2,1,0:T(8,128)S(1)}) custom-call(s32[408]{0:T(512)S(1)} %concatenate.3.refs_0_, ...), custom_call_target="tpu_custom_call", output_to_operand_aliasing={{0}: (3, {}), {1}: (4, {}), {2}: (5, {}), {3}: (6, {}), {4}... | custom-call | tf_op jit(solution)/shard_map/pallas_call | solution.py:317
  152.2 8.1 %all-to-all-done.6.refs_1_ = f32[16,2,16,128]{3,2,1,0:T(8,128)S(1)} async-done(((f32[16,2,16,128]{3,2,1,0:T(8,128)}), f32[16,2,16,128]{3,2,1,0:T(8,128)S(1)}, u32[]{:S(2)}, u32[]{:S(2)}) %all-to-all-start.6) | async-done | bytes 262176 | tf_op jit(solution)/shard_map/all_to_all | solution.py:332
  160.4 2.9 %shard_map.75 = (f32[2,16,128]{2,1,0:T(8,128)S(1)}, f32[2,64,512]{2,1,0:T(8,128)S(1)}, f32[16,16,128]{2,1,0:T(8,128)S(1)}) custom-call(s32[408]{0:T(512)S(1)} %concatenate.3.refs_0_, f32[16,2,16,128]{3,2,1,0:T(8,128)S(1)} %all-to-all-done.6.refs_1_, f32[16,4,32,512]{3,2,1,0:T(8,128)} %bitcast.23, ...), custom_call_target="tpu_custom_call", output_to_operand_aliasing={{2}: (4, {})} | custom-call | tf_op jit(solution)/shard_map/pallas_call | solution.py:317
  163.3 12.0 %all_to_all.75.refs_1_ = f32[16,1,16,128]{3,2,1,0:T(8,128)S(1)} all-to-all(f32[16,1,16,128]{3,2,1,0:T(8,128)S(1)} %bitcast.14), channel_id=1, replica_groups=mesh['prow'=16,'pcol'=16] {'pcol'}, dimensions={0} | all-to-all | bytes 262144 | tf_op jit(solution)/shard_map/all_to_all | solution.py:332
  176.6 3.5 %all-to-all-start.8 = ((f32[16,1,16,128]{3,2,1,0:T(8,128)}), f32[16,1,16,128]{3,2,1,0:T(8,128)S(1)}, u32[]{:S(2)}, u32[]{:S(2)}) async-start(f32[16,1,16,128]{3,2,1,0:T(8,128)} %shard_map.76), calls=%async_computation.8 | async-start | bytes 262144 | tf_op jit(solution)/shard_map/all_to_all | solution.py:332
  182.2 7.0 %all-to-all-done.8.refs_1_ = f32[16,1,16,128]{3,2,1,0:T(8,128)S(1)} async-done(((f32[16,1,16,128]{3,2,1,0:T(8,128)}), f32[16,1,16,128]{3,2,1,0:T(8,128)S(1)}, u32[]{:S(2)}, u32[]{:S(2)}) %all-to-all-start.8) | async-done | bytes 131104 | tf_op jit(solution)/shard_map/all_to_all | solution.py:332
  191.6 12.2 %all_to_all.76.refs_1_ = f32[16,1,16,128]{3,2,1,0:T(8,128)S(1)} all-to-all(f32[16,1,16,128]{3,2,1,0:T(8,128)S(1)} %bitcast.13), channel_id=1, replica_groups=mesh['prow'=16,'pcol'=16] {'pcol'}, dimensions={0} | all-to-all | bytes 262144 | tf_op jit(solution)/shard_map/all_to_all | solution.py:332
  205.0 3.5 %all-to-all-start.10 = ((f32[16,1,16,128]{3,2,1,0:T(8,128)}), f32[16,1,16,128]{3,2,1,0:T(8,128)S(1)}, u32[]{:S(2)}, u32[]{:S(2)}) async-start(f32[16,1,16,128]{3,2,1,0:T(8,128)} %shard_map.79), calls=%async_computation.10 | async-start | bytes 262144 | tf_op jit(solution)/shard_map/all_to_all | solution.py:332
  210.4 7.3 %all-to-all-done.10.refs_1_ = f32[16,1,16,128]{3,2,1,0:T(8,128)S(1)} async-done(((f32[16,1,16,128]{3,2,1,0:T(8,128)}), f32[16,1,16,128]{3,2,1,0:T(8,128)S(1)}, u32[]{:S(2)}, u32[]{:S(2)}) %all-to-all-start.10) | async-done | bytes 131104 | tf_op jit(solution)/shard_map/all_to_all | solution.py:332
  221.0 12.2 %all_to_all.77.refs_1_ = f32[16,8,256]{2,1,0:T(8,128)S(1)} all-to-all(f32[16,8,256]{2,1,0:T(8,128)S(1)} %shard_map.82), channel_id=1, replica_groups=mesh['prow'=16,'pcol'=16] {'pcol'}, dimensions={0} | all-to-all | bytes 262144 | tf_op jit(solution)/shard_map/all_to_all | solution.py:332
  233.8 10.0 %all_to_all.78.refs_1_ = f32[16,8,256]{2,1,0:T(8,128)S(1)} all-to-all(f32[16,8,256]{2,1,0:T(8,128)S(1)} %shard_map.83), channel_id=1, replica_groups=mesh['prow'=16,'pcol'=16] {'prow'}, dimensions={0} | all-to-all | bytes 262144 | tf_op jit(solution)/shard_map/all_to_all | solution.py:332
  243.8 5.2 %shard_map.85 = (f32[16,8,128]{2,1,0:T(8,128)S(1)}, f32[3,8,512]{2,1,0:T(8,128)S(1)}) custom-call(s32[408]{0:T(512)S(1)} %concatenate.3.refs_0_, f32[16,8,256]{2,1,0:T(8,128)S(1)} %all_to_all.78.refs_1_, f32[16,17,32,256]{3,2,1,0:T(8,128)} %bitcast.17), custom_call_target="tpu_custom_call" | custom-call | tf_op jit(solution)/shard_map/pallas_call | solution.py:317
  256.4 10.6 %all_to_all.79.refs_1_ = f32[16,8,128]{2,1,0:T(8,128)S(1)} all-to-all(f32[16,8,128]{2,1,0:T(8,128)S(1)} %shard_map.87), channel_id=1, replica_groups=mesh['prow'=16,'pcol'=16] {'pcol'}, dimensions={0} | all-to-all | bytes 131072 | tf_op jit(solution)/shard_map/all_to_all | solution.py:332
  (40 shorter events, 41.9 us)
Async XLA Ops:
  6.5 135.2 %all-gather.7.cloned.1.call-start = ((), (), s32[]{:S(2)}) async-start(), calls=%async_computation.14 | async-start | bytes 6684672 | tf_op jit(solution)/shard_map/all_gather | solution.py:365
  8.2 0.9 copy-start
  11.8 140.5 %all-gather.9.cloned.1.call-start = ((), (), s32[]{:S(2)}) async-start(), calls=%async_computation.15 | async-start | bytes 4456448 | tf_op jit(solution)/shard_map/all_gather | solution.py:398
  62.0 3.7 %collective-permute-start = (f32[32,16,128]{2,1,0:T(8,128)S(1)}, f32[32,16,128]{2,1,0:T(8,128)S(1)}, u32[]{:S(2)}, u32[]{:S(2)}) collective-permute-start(f32[32,16,128]{2,1,0:T(8,128)S(1)} %slice.4), channel_id=1, source_target_pairs={{0,1},{1,0},{2,3},{3,2},{4,5},{5,4},{6,7},{7,6},{8,9},{9,8},{10,11... | collective-permute-start | bytes 786440 | tf_op jit(solution)/shard_map/ppermute | solution.py:459
  101.2 19.8 %all-to-all-start.4 = ((f32[16,4,16,128]{3,2,1,0:T(8,128)}), f32[16,4,16,128]{3,2,1,0:T(8,128)S(1)}, u32[]{:S(2)}, u32[]{:S(2)}) async-start(f32[16,4,16,128]{3,2,1,0:T(8,128)} %get-tuple-element.53), calls=%async_computation.4 | async-start | bytes 1048576 | tf_op jit(solution)/shard_map/all_to_all | solution.py:332
  104.8 138.9 %all-gather.11.cloned.1.call-start = ((), (), s32[]{:S(2)}) async-start(), calls=%async_computation.16 | async-start | bytes 9469952 | tf_op jit(solution)/shard_map/all_gather | solution.py:497
  145.5 14.8 %all-to-all-start.6 = ((f32[16,2,16,128]{3,2,1,0:T(8,128)}), f32[16,2,16,128]{3,2,1,0:T(8,128)S(1)}, u32[]{:S(2)}, u32[]{:S(2)}) async-start(f32[16,2,16,128]{3,2,1,0:T(8,128)} %shard_map.73), calls=%async_computation.6 | async-start | bytes 524288 | tf_op jit(solution)/shard_map/all_to_all | solution.py:332
  176.6 12.6 %all-to-all-start.8 = ((f32[16,1,16,128]{3,2,1,0:T(8,128)}), f32[16,1,16,128]{3,2,1,0:T(8,128)S(1)}, u32[]{:S(2)}, u32[]{:S(2)}) async-start(f32[16,1,16,128]{3,2,1,0:T(8,128)} %shard_map.76), calls=%async_computation.8 | async-start | bytes 262144 | tf_op jit(solution)/shard_map/all_to_all | solution.py:332
  205.0 12.6 %all-to-all-start.10 = ((f32[16,1,16,128]{3,2,1,0:T(8,128)}), f32[16,1,16,128]{3,2,1,0:T(8,128)S(1)}, u32[]{:S(2)}, u32[]{:S(2)}) async-start(f32[16,1,16,128]{3,2,1,0:T(8,128)} %shard_map.79), calls=%async_computation.10 | async-start | bytes 262144 | tf_op jit(solution)/shard_map/all_to_all | solution.py:332
  248.9 1.8 collective-permute-start.1
  253.2 1.3 collective-permute-start.2
Sparse Core Ops, SparseCore 0:
  11.9 50.2 all-gather.6
  64.7 60.6 all-gather.8
  144.4 73.3 all-gather.10

commit v5 on v4

--- a/solution.py
+++ b/solution.py
@@ -38,21 +38,18 @@
 
 
 def dot3(a, b, dims):
-    bh, bl = split(b)
+    bh, bl = b if isinstance(b, tuple) else split(b)
+    dot = functools.partial(
+        lax.dot_general, dimension_numbers=(dims, ((), ())), preferred_element_type=jnp.float32
+    )
     n = a.shape[0]
     if n <= 64 and dims[0] == (1,):
         high = a.astype(jnp.bfloat16).astype(jnp.float32)
         both = jnp.concatenate([high, a - high], 0).astype(jnp.bfloat16)
-        dot = functools.partial(
-            lax.dot_general, dimension_numbers=(dims, ((), ())), preferred_element_type=jnp.float32
-        )
         first = dot(both, bh)
         second = dot(high.astype(jnp.bfloat16), bl)
         return first[:n] + (first[n:] + second)
     ah, al = split(a)
-    dot = functools.partial(
-        lax.dot_general, dimension_numbers=(dims, ((), ())), preferred_element_type=jnp.float32
-    )
     return dot(ah, bh) + (dot(ah, bl) + dot(al, bh))
 
 
@@ -108,11 +105,12 @@
     recv = None
     if height > 0:
         recv, *refs = refs
-    rhs, inverse, out = refs
+    rhs, inverse, out, scratch = refs
     low = lower((16, 128))
+    sides = from_own_order(rhs[...], scratch)
     for i in range(rhs.shape[0]):
         s = pl.program_id(0) * rhs.shape[0] + i
-        z = rhs[i]
+        z = sides[i]
         if recv is not None:
             total = recv[0, i]
             for k in range(1, recv.shape[0]):
@@ -140,7 +138,7 @@
 def spread_kernel(height, slots, slot_base, source, first, end, pos, parent, pattern, sizes, *refs):
     refs = list(refs)
     given = refs.pop(0)
-    inverse = refs.pop(0) if source == "z" else None
+    inverse = (refs.pop(0), refs.pop(0)) if source == "z" else None
     panels = refs.pop(0)
     before = [refs.pop(0) for _ in range(first, end)] if height > 0 else []
     sol = refs.pop(0) if source == "z" else None
@@ -159,9 +157,7 @@
         if source == "z":
             turned = given[:, k].reshape(256, 128).T
             z_t = jnp.concatenate([turned[:64], turned[64:]], 1)
-            rows = inverse[:, k].reshape(16, 2, 16, 512)
-            rows = jnp.concatenate([rows[:, 0].reshape(256, 512), rows[:, 1].reshape(256, 512)], 0)
-            y_t = dot3(z_t, rows, ((1,), (0,)))
+            y_t = dot3(z_t, (inverse[0][k], inverse[1][k]), ((1,), (0,)))
             limit = sizes[slot]
             y_t = jnp.where(lax.broadcasted_iota(jnp.int32, (64, 512), 1) < limit, y_t, 0.0)
             scratch[pl.ds(0, 64), :] = y_t
@@ -195,6 +191,16 @@
             after[d - first][where] += scale * update[d - first]
 
 
+def split_inverse_kernel(pos, parent, pattern, sizes, inverse, high, low):
+    rows = inverse[:, 0].reshape(16, 2, 16, 512)
+    rows = jnp.concatenate([rows[:, 0].reshape(256, 512), rows[:, 1].reshape(256, 512)], 0)
+    high[0], low[0] = split(rows)
+
+
+def split_top_kernel(pos, parent, pattern, sizes, block, high, low):
+    high[0], low[0] = split(block[:, 0].reshape(512, 256))
+
+
 def join_kernel(pos, parent, pattern, sizes, here, there, out):
     out[...] = (here[...] + there[...]).reshape(out.shape)
 
@@ -253,7 +259,7 @@
     return jnp.where(lane == level, pltpu.roll(lanes, level * 32, 1), own)
 
 
-def low_kernel(pos, parent, pattern, sizes, recv, block, out, left, z):
+def low_kernel(pos, parent, pattern, sizes, recv, high, low, out, left, z):
     step = pl.program_id(0)
 
     @pl.when(step == 0)
@@ -272,14 +278,14 @@
                     left[n - 4, :, g * 128 : (g + 1) * 128] = jnp.where(pos[1] % 2 == 0, -whole, 0.0)
         out[...] = jnp.zeros_like(out)
 
-    solved = dot3(z[step], block[:, 0].reshape(512, 256), ((1,), (0,)))
+    solved = dot3(z[step], (high[0], low[0]), ((1,), (0,)))
     out[step] = place(out[step], solved, 0, pos)
     target = parent[NODE_BASE[TOP] + step] - NODE_BASE[TOP + 1]
-    left[target] = left[target] - dot3(solved, block[:, 1].reshape(512, 256), ((1,), (1,)))
-    left[2] = left[2] - dot3(solved, block[:, 2].reshape(512, 256), ((1,), (1,)))
-
-
-def middle_kernel(pos, parent, pattern, sizes, left, other, before, block, out, after):
+    left[target] = left[target] - dot3(solved, (high[1], low[1]), ((1,), (1,)))
+    left[2] = left[2] - dot3(solved, (high[2], low[2]), ((1,), (1,)))
+
+
+def middle_kernel(pos, parent, pattern, sizes, left, other, before, high, low, out, after):
     step = pl.program_id(0)
 
     @pl.when(step == 0)
@@ -287,13 +293,13 @@
         out[...] = before[...]
         after[...] = left[2]
 
-    solved = dot3(left[step] + other[step], block[:, 0].reshape(512, 256), ((1,), (0,)))
+    solved = dot3(left[step] + other[step], (high[0], low[0]), ((1,), (0,)))
     out[step] = place(out[step], solved, 1, pos)
-    after[...] = after[...] - dot3(solved, block[:, 1].reshape(512, 256), ((1,), (1,)))
-
-
-def root_kernel(pos, parent, pattern, sizes, left, other, before, block, out):
-    solved = dot3(left[...] + other[...], block[:, 0].reshape(512, 256), ((1,), (0,)))
+    after[...] = after[...] - dot3(solved, (high[1], low[1]), ((1,), (1,)))
+
+
+def root_kernel(pos, parent, pattern, sizes, left, other, before, high, low, out):
+    solved = dot3(left[...] + other[...], (high[0], low[0]), ((1,), (0,)))
     out[...] = before[...]
     out[0] = place(before[0], solved, 2, pos)
 
@@ -308,7 +314,7 @@
 
 def on_device(right_side, inverse_rows, panels, pattern, node_sizes, parent):
     pos = jnp.stack([lax.axis_index("prow"), lax.axis_index("pcol")]).astype(jnp.int32)
-    rhs = right_side.reshape(19, 16, 128)
+    natural = right_side.reshape(19, 16, 128)
     scalars = jnp.concatenate([pos, parent, pattern.reshape(-1), node_sizes.reshape(-1)])
     slot_counts = [max(1, n // 16) for n in NODES]
     bases = [sum(slot_counts[:h]) for h in range(LEVELS)]
@@ -357,7 +363,7 @@
         [jax.ShapeDtypeStruct((19, 16, 128), f32), jax.ShapeDtypeStruct((6, 32, 512), f32)]
         + [jax.ShapeDtypeStruct((hi - lo, 32, 512), f32) for lo, hi in spans],
         {},
-        rhs,
+        natural,
         *[inverse_rows] * 3,
         *[panels] * 2,
         *[inverse_rows] * len(spans),
@@ -379,19 +385,31 @@
                 functools.partial(residue_kernel, *info), [], (1,), [every, rhs_all], every, piece, {}, recv, rhs
             )
             gathered = exchange(z, "prow")
+            lo, inverse = [pair for pair in inverses if pair[0] <= base][-1]
+            inverse, _ = lax.optimization_barrier((inverse, z))
+            inverse = call(
+                split_inverse_kernel,
+                [],
+                (count,),
+                [pl.BlockSpec((16, 1, 32, 512), lambda s, *_, b=base - lo: (0, b + s, 0, 0))],
+                [pl.BlockSpec((1, 512, 512), lambda s, *_: (s, 0, 0))] * 2,
+                [jax.ShapeDtypeStruct((count, 512, 512), jnp.bfloat16)] * 2,
+                {},
+                inverse,
+            )
         else:
             per = min(4, count)
             in_specs = [
                 pl.BlockSpec((per, 16, 128), lambda s, *_, b=base // per: (b + s, 0, 0)),
                 pl.BlockSpec((per, 1, 32, 512), lambda s, *_, b=base // per: (b + s, 0, 0, 0)),
             ]
-            args = [rhs, inverse_rows]
+            args = [natural, inverse_rows]
             if height > 0:
                 in_specs = [pl.BlockSpec((recv.shape[0], per, 16, 128), lambda s, *_: (0, s, 0, 0))] + in_specs
                 args = [recv] + args
             some = pl.BlockSpec((16, per, 16, 128), lambda s, *_: (0, s, 0, 0))
             kernel = functools.partial(partial_kernel, *info)
-            parts = call(kernel, [], (count // per,), in_specs, some, piece, {}, *args)
+            parts = call(kernel, [pltpu.VMEM((per * 32, 128), f32)], (count // per,), in_specs, some, piece, {}, *args)
             parts = exchange(parts, "prow")
             if height == 0:
                 wholes, parts = lax.optimization_barrier((wholes, parts))
@@ -401,6 +419,23 @@
             )
             outputs.append(sol)
             gathered = exchange(y, "prow")
+        if height == 1:
+            chosen_from, _ = lax.optimization_barrier((top, y))
+            halves = [(4, 3, 0, 1), (2, 2, 0, 0), (1, 1, 0, 2)]
+            chosen = call(
+                choose_kernel,
+                [],
+                (1,),
+                [
+                    pl.BlockSpec((m, n, 32, 256), lambda _, info, a=a, b=b: (a, b, 0, info[1] % 2))
+                    for m, n, a, b in halves
+                ],
+                pl.BlockSpec((17, 32, 256), lambda *_: (0, 0, 0)),
+                jax.ShapeDtypeStruct((17, 32, 256), f32),
+                {},
+                *[chosen_from] * 3,
+            )
+            top = lax.all_gather(chosen, "prow", axis=0)
         steps = [(0, 1), (1, reach)] if height + 1 < TOP else [(0, reach)]
         updated = []
         given, source = gathered, "z" if whole else "y"
@@ -412,9 +447,8 @@
             args = [given]
             out_specs, out_shape = [], []
             if source == "z":
-                lo, inverse = [pair for pair in inverses if pair[0] <= base][-1]
-                in_specs.append(pl.BlockSpec((16, 1, 32, 512), lambda s, *_, b=base - lo: (0, b + s, 0, 0)))
-                args.append(inverse)
+                in_specs += [pl.BlockSpec((1, 512, 512), lambda s, *_: (s, 0, 0))] * 2
+                args += inverse
                 out_specs.append(pl.BlockSpec((1, 16, 128), lambda s, *_: (s, 0, 0)))
                 out_shape.append(own)
                 if end < reach:
@@ -478,23 +512,6 @@
                 )
             else:
                 recv = exchange(results[0].reshape(16, following, 16, 128), "pcol")
-        if height == 1:
-            top, recv = lax.optimization_barrier((top, recv))
-            halves = [(4, 3, 0, 1), (2, 2, 0, 0), (1, 1, 0, 2)]
-            chosen = call(
-                choose_kernel,
-                [],
-                (1,),
-                [
-                    pl.BlockSpec((m, n, 32, 256), lambda _, info, a=a, b=b: (a, b, 0, info[1] % 2))
-                    for m, n, a, b in halves
-                ],
-                pl.BlockSpec((17, 32, 256), lambda *_: (0, 0, 0)),
-                jax.ShapeDtypeStruct((17, 32, 256), f32),
-                {},
-                *[top] * 3,
-            )
-            top = lax.all_gather(chosen, "prow", axis=0)
     many = pl.BlockSpec((16, 16, 128), lambda *_: (0, 0, 0))
     sides = pl.BlockSpec((16, 8, 256), lambda *_: (0, 0, 0))
     sides_shape = jax.ShapeDtypeStruct((16, 8, 256), f32)
@@ -511,8 +528,19 @@
     )
     total = call(sum_kernel, [], (1,), [sides], sides, sides_shape, {}, exchange(turned, "pcol"))
     gathered = exchange(total, "prow")
+    top, _ = lax.optimization_barrier((top, total))
+    top = call(
+        split_top_kernel,
+        [],
+        (17,),
+        [pl.BlockSpec((16, 1, 32, 256), lambda s, *_: (0, s, 0, 0))],
+        [pl.BlockSpec((1, 512, 256), lambda s, *_: (s, 0, 0))] * 2,
+        [jax.ShapeDtypeStruct((17, 512, 256), jnp.bfloat16)] * 2,
+        {},
+        top,
+    )
     def halves_from(start, n):
-        return pl.BlockSpec((16, n, 32, 256), lambda s, *_: (0, start // n + s, 0, 0))
+        return [pl.BlockSpec((n, 512, 256), lambda s, *_: (start // n + s, 0, 0))] * 2
 
     def whole_of(*shape):
         return pl.BlockSpec(shape, lambda *_: (0,) * len(shape)), jax.ShapeDtypeStruct(shape, f32)
@@ -527,38 +555,38 @@
         low_kernel,
         [pltpu.VMEM((4, 8, 512), f32)],
         (4,),
-        [sides, halves_from(0, 3)],
+        [sides] + halves_from(0, 3),
         [found, three],
         [found_shape, three_shape],
         {},
         gathered,
-        top,
+        *top,
     )
     solved, left = call(
         middle_kernel,
         [],
         (2,),
-        [three, three, found, halves_from(12, 2)],
+        [three, three, found] + halves_from(12, 2),
         [found, single],
         [found_shape, single_shape],
         {},
         left,
         other_core(left),
         solved,
-        top,
+        *top,
     )
     solved = call(
         root_kernel,
         [],
         (1,),
-        [single, single, found, halves_from(16, 1)],
+        [single, single, found] + halves_from(16, 1),
         found,
         found_shape,
         {},
         left,
         other_core(left),
         solved,
-        top,
+        *top,
     )
     out = call(
         last_kernel,

time: 276 us -> 285 us (1.033)
  Pallas kernels: 55.8 us -> 73.6 us
  waiting for transfers between devices: 36.3 us -> 25.4 us
  blocking collectives: 149 us -> 141 us
  local copies, waits for them, and re-layouts: 2.56 us -> 8.66 us
    pallas_call x25 -> x29, Pallas kernels: 55.8 us -> 73.6 us  [call(): pl.pallas_call(functools.partial(with_parts, kernel), grid_spec=pltpu.Pre...]
    all_to_all x4 -> x5, waiting for transfers between devices: 33.3 us -> 21.9 us  [exchange(): return lax.all_to_all(x, axis, 0, 0, tiled=True)]
    all_to_all x9 -> x8, blocking collectives: 130 us -> 122 us  [exchange(): return lax.all_to_all(x, axis, 0, 0, tiled=True)]
    unnamed x3 -> x13, local copies, waits for them, and re-layouts: 1.69 us -> 7.79 us
    all_to_all x4 -> x5, starting transfers between devices: 14.1 us -> 17.7 us  [exchange(): return lax.all_to_all(x, axis, 0, 0, tiled=True)]
  transfers between devices with their start and end apart: 10 -> 11, of which waited for: 7 -> 7; matrix products, arithmetic and copies ran while one was open for 0% -> 0% of each run, Pallas kernels for 15% -> 21%
where the time goes in v5:
time: 285 us; the launch traced here: 283 us
  blocking collectives  141 us (49%)
  Pallas kernels  73.6 us (26%)
  waiting for transfers between devices  25.4 us (9%)
  starting transfers between devices  20.6 us (7%)
  between operations  13.3 us (5%)
  local copies, waits for them, and re-layouts  8.66 us (3%)
    all_to_all x8, blocking collectives, exchange(): return lax.all_to_all(x, axis, 0, 0, tiled=True)  122 us
    pallas_call x29, Pallas kernels, call(): pl.pallas_call(functools.partial(with_parts, kernel), grid_spec=pltpu.Pre...  73.6 us
    all_to_all x5, waiting for transfers between devices, exchange(): return lax.all_to_all(x, axis, 0, 0, tiled=True)  21.9 us
    all_to_all x1, blocking collectives, on_device(): lax.all_to_all(joined, 'pcol', 0, 0, tiled=True, axis_index_groups=[[core...  19.1 us
    all_to_all x5, starting transfers between devices, exchange(): return lax.all_to_all(x, axis, 0, 0, tiled=True)  17.7 us
    unnamed x13, local copies, waits for them, and re-layouts  7.79 us
  transfers between devices with their start and end apart: 11, of which 7 were waited for; matrix products, arithmetic and copies ran while one was open for 0% of the time, Pallas kernels for 21%

profile of v5, /device:TPU:1, one launch (start us, length us, event | category | flops | bytes accessed | tf_op | source)
XLA Modules:
  0.0 282.9 jit_solution(5280309828603577076)
XLA Ops:
  11.9 3.3 %shard_map.65 = f32[16,8,16,128]{3,2,1,0:T(8,128)S(1)} custom-call(s32[408]{0:T(512)S(1)} %concatenate.3.refs_0_, f32[19,16,128]{2,1,0:T(8,128)S(1)} %bitcast.15, f32[19,1,32,512]{3,2,1,0:T(8,128)} %refs_3_.3), custom_call_target="tpu_custom_call" | custom-call | tf_op jit(solution)/shard_map/pallas_call | solution.py:323
  15.2 23.5 %all_to_all.70.refs_1_ = f32[16,8,16,128]{3,2,1,0:T(8,128)S(1)} all-to-all(f32[16,8,16,128]{3,2,1,0:T(8,128)S(1)} %shard_map.65), channel_id=1, replica_groups=mesh['prow'=16,'pcol'=16] {'prow'}, dimensions={0} | all-to-all | bytes 2097152 | tf_op jit(solution)/shard_map/all_to_all | solution.py:338
  39.5 19.0 %all_to_all.71.refs_1_ = f32[16,8,16,128]{3,2,1,0:T(8,128)S(1)} all-to-all(f32[16,8,16,128]{3,2,1,0:T(8,128)S(1)} %get-tuple-element.61), channel_id=1, replica_groups=mesh['prow'=16,'pcol'=16] {'prow'}, dimensions={0} | all-to-all | bytes 2097152 | tf_op jit(solution)/shard_map/all_to_all | solution.py:338
  58.4 4.0 %shard_map.67.refs_1_ = f32[64,16,128]{2,1,0:T(8,128)S(1)} custom-call(s32[408]{0:T(512)S(1)} %concatenate.3.refs_0_, f32[16,8,16,128]{3,2,1,0:T(8,128)S(1)} %all_to_all.71.refs_1_, f32[19,1,7,32,512]{4,3,2,1,0:T(8,128)} %refs_4_.7), custom_call_target="tpu_custom_call" | custom-call | tf_op jit(solution)/shard_map/pallas_call | solution.py:323
  66.8 19.1 %all_to_all.72.refs_1_ = f32[8,4,16,128]{3,2,1,0:T(8,128)S(1)} all-to-all(f32[8,4,16,128]{3,2,1,0:T(8,128)S(1)} %shard_map.68), channel_id=1, replica_groups={{0,2,4,6,8,10,12,14},{1,3,5,7,9,11,13,15},{16,18,20,22,24,26,28,30},{17..., dimensions={0} | all-to-all | bytes 524288 | tf_op jit(solution)/shard_map/all_to_all | solution.py:505
  88.3 12.3 %all_to_all.73.refs_1_ = f32[16,4,16,128]{3,2,1,0:T(8,128)S(1)} all-to-all(f32[16,4,16,128]{3,2,1,0:T(8,128)S(1)} %shard_map.69), channel_id=1, replica_groups=mesh['prow'=16,'pcol'=16] {'prow'}, dimensions={0} | all-to-all | bytes 1048576 | tf_op jit(solution)/shard_map/all_to_all | solution.py:338
  104.5 3.6 %all-to-all-start.4 = ((f32[16,4,16,128]{3,2,1,0:T(8,128)}), f32[16,4,16,128]{3,2,1,0:T(8,128)S(1)}, u32[]{:S(2)}, u32[]{:S(2)}) async-start(f32[16,4,16,128]{3,2,1,0:T(8,128)} %get-tuple-element.62), calls=%async_computation.4 | async-start | bytes 1048576 | tf_op jit(solution)/shard_map/all_to_all | solution.py:338
  108.1 5.3 %shard_map.71 = (f32[32,16,128]{2,1,0:T(8,128)S(1)}, f32[16,16,128]{2,1,0:T(8,128)S(1)}, f32[16,16,128]{2,1,0:T(8,128)S(1)}, f32[16,16,128]{2,1,0:T(8,128)S(1)},...) custom-call(s32[408]{0:T(512)S(1)} %concatenate.3.refs_0_, f32[16,8,16,128]{3,2,1,0:T(8,128)S(1)} %all_to_all.71.refs_1_, ...), custom_call_target="tpu_custom_call" | custom-call | tf_op jit(solution)/shard_map/pallas_call | solution.py:323
  113.4 10.9 %all-to-all-done.4.refs_1_ = f32[16,4,16,128]{3,2,1,0:T(8,128)S(1)} async-done(((f32[16,4,16,128]{3,2,1,0:T(8,128)}), f32[16,4,16,128]{3,2,1,0:T(8,128)S(1)}, u32[]{:S(2)}, u32[]{:S(2)}) %all-to-all-start.4) | async-done | bytes 524320 | tf_op jit(solution)/shard_map/all_to_all | solution.py:338
  126.8 18.2 %all_to_all.74.refs_1_ = f32[16,2,16,128]{3,2,1,0:T(8,128)S(1)} all-to-all(f32[16,2,16,128]{3,2,1,0:T(8,128)S(1)} %bitcast.18), channel_id=1, replica_groups=mesh['prow'=16,'pcol'=16] {'pcol'}, dimensions={0} | all-to-all | bytes 524288 | tf_op jit(solution)/shard_map/all_to_all | solution.py:338
  146.3 3.5 %all-to-all-start.6 = ((f32[16,2,16,128]{3,2,1,0:T(8,128)}), f32[16,2,16,128]{3,2,1,0:T(8,128)S(1)}, u32[]{:S(2)}, u32[]{:S(2)}) async-start(f32[16,2,16,128]{3,2,1,0:T(8,128)} %shard_map.73), calls=%async_computation.6 | async-start | bytes 524288 | tf_op jit(solution)/shard_map/all_to_all | solution.py:338
  149.8 3.1 %shard_map.75 = (f32[16,16,128]{2,1,0:T(8,128)S(1)}, f32[16,16,128]{2,1,0:T(8,128)S(1)}, f32[16,16,128]{2,1,0:T(8,128)S(1)}, f32[16,16,128]{2,1,0:T(8,128)S(1)}, f32[16,16,128]{2,1,0:T(8,128)S(1)}) custom-call(s32[408]{0:T(512)S(1)} %concatenate.3.refs_0_, ...), custom_call_target="tpu_custom_call", output_to_operand_aliasing={{0}: (3, {}), {1}: (4, {}), {2}: (5, {}), {3}: (6, {}), {4}... | custom-call | tf_op jit(solution)/shard_map/pallas_call | solution.py:323
  159.6 2.9 %shard_map.76 = (f32[2,16,128]{2,1,0:T(8,128)S(1)}, f32[2,64,512]{2,1,0:T(8,128)S(1)}, f32[16,16,128]{2,1,0:T(8,128)S(1)}) custom-call(s32[408]{0:T(512)S(1)} %concatenate.3.refs_0_, f32[16,2,16,128]{3,2,1,0:T(8,128)S(1)} %all-to-all-done.6.refs_1_, bf16[2,512,512]{2,1,0:T(8,128)(2,1)} %copy-done.4, ...), custom_call_target="tpu_custom_call", output_to_operand_aliasing={{2}: (5, {})} | custom-call | tf_op jit(solution)/shard_map/pallas_call | solution.py:323
  162.5 13.8 %all_to_all.75.refs_1_ = f32[16,1,16,128]{3,2,1,0:T(8,128)S(1)} all-to-all(f32[16,1,16,128]{3,2,1,0:T(8,128)S(1)} %bitcast.17), channel_id=1, replica_groups=mesh['prow'=16,'pcol'=16] {'pcol'}, dimensions={0} | all-to-all | bytes 262144 | tf_op jit(solution)/shard_map/all_to_all | solution.py:338
  177.6 3.5 %all-to-all-start.8 = ((f32[16,1,16,128]{3,2,1,0:T(8,128)}), f32[16,1,16,128]{3,2,1,0:T(8,128)S(1)}, u32[]{:S(2)}, u32[]{:S(2)}) async-start(f32[16,1,16,128]{3,2,1,0:T(8,128)} %shard_map.77), calls=%async_computation.8 | async-start | bytes 262144 | tf_op jit(solution)/shard_map/all_to_all | solution.py:338
  185.1 5.1 %all-to-all-done.8.refs_1_ = f32[16,1,16,128]{3,2,1,0:T(8,128)S(1)} async-done(((f32[16,1,16,128]{3,2,1,0:T(8,128)}), f32[16,1,16,128]{3,2,1,0:T(8,128)S(1)}, u32[]{:S(2)}, u32[]{:S(2)}) %all-to-all-start.8) | async-done | bytes 131104 | tf_op jit(solution)/shard_map/all_to_all | solution.py:338
  192.2 12.2 %all_to_all.76.refs_1_ = f32[16,1,16,128]{3,2,1,0:T(8,128)S(1)} all-to-all(f32[16,1,16,128]{3,2,1,0:T(8,128)S(1)} %bitcast.13), channel_id=1, replica_groups=mesh['prow'=16,'pcol'=16] {'pcol'}, dimensions={0} | all-to-all | bytes 262144 | tf_op jit(solution)/shard_map/all_to_all | solution.py:338
  205.6 3.5 %all-to-all-start.10 = ((f32[16,1,16,128]{3,2,1,0:T(8,128)}), f32[16,1,16,128]{3,2,1,0:T(8,128)S(1)}, u32[]{:S(2)}, u32[]{:S(2)}) async-start(f32[16,1,16,128]{3,2,1,0:T(8,128)} %shard_map.81), calls=%async_computation.10 | async-start | bytes 262144 | tf_op jit(solution)/shard_map/all_to_all | solution.py:338
  212.9 3.6 %all-to-all-done.10.refs_1_ = f32[16,1,16,128]{3,2,1,0:T(8,128)S(1)} async-done(((f32[16,1,16,128]{3,2,1,0:T(8,128)}), f32[16,1,16,128]{3,2,1,0:T(8,128)S(1)}, u32[]{:S(2)}, u32[]{:S(2)}) %all-to-all-start.10) | async-done | bytes 131104 | tf_op jit(solution)/shard_map/all_to_all | solution.py:338
  219.5 12.9 %all_to_all.77.refs_1_ = f32[16,8,256]{2,1,0:T(8,128)S(1)} all-to-all(f32[16,8,256]{2,1,0:T(8,128)S(1)} %shard_map.85), channel_id=1, replica_groups=mesh['prow'=16,'pcol'=16] {'pcol'}, dimensions={0} | all-to-all | bytes 262144 | tf_op jit(solution)/shard_map/all_to_all | solution.py:338
  233.6 3.5 %all-to-all-start.12 = ((f32[16,8,256]{2,1,0:T(8,128)}), f32[16,8,256]{2,1,0:T(8,128)S(1)}, u32[]{:S(2)}, u32[]{:S(2)}) async-start(f32[16,8,256]{2,1,0:T(8,128)} %shard_map.86), calls=%async_computation.12 | async-start | bytes 262144 | tf_op jit(solution)/shard_map/all_to_all | solution.py:338
  237.2 11.1 %shard_map.88 = (bf16[17,512,256]{2,1,0:T(8,128)(2,1)S(1)}, bf16[17,512,256]{2,1,0:T(8,128)(2,1)S(1)}) custom-call(s32[408]{0:T(512)S(1)} %concatenate.3.refs_0_, f32[16,17,32,256]{3,2,1,0:T(8,128)} %bitcast.25), custom_call_target="tpu_custom_call" | custom-call | tf_op jit(solution)/shard_map/pallas_call | solution.py:323
  252.5 5.1 %shard_map.89 = (f32[16,8,128]{2,1,0:T(8,128)S(1)}, f32[3,8,512]{2,1,0:T(8,128)S(1)}) custom-call(s32[408]{0:T(512)S(1)} %concatenate.3.refs_0_, f32[16,8,256]{2,1,0:T(8,128)S(1)} %all-to-all-done.12.refs_1_, bf16[17,512,256]{2,1,0:T(8,128)(2,1)} %copy-done, bf16[17,512,256]{2,1,0:T(8,128)(2,1)} %copy-done.1), custom_call_target="tpu_custom_call" | custom-call | tf_op jit(solution)/shard_map/pallas_call | solution.py:323
  264.5 10.4 %all_to_all.78.refs_1_ = f32[16,8,128]{2,1,0:T(8,128)S(1)} all-to-all(f32[16,8,128]{2,1,0:T(8,128)S(1)} %shard_map.91), channel_id=1, replica_groups=mesh['prow'=16,'pcol'=16] {'pcol'}, dimensions={0} | all-to-all | bytes 131072 | tf_op jit(solution)/shard_map/all_to_all | solution.py:338
  (55 shorter events, 56.2 us)
Async XLA Ops:
  6.5 95.5 %all-gather.9.cloned.1.call-start = ((), (), s32[]{:S(2)}) async-start(), calls=%async_computation.15 | async-start | bytes 6684672 | tf_op jit(solution)/shard_map/all_gather | solution.py:371
  8.2 0.9 copy-start.2
  9.1 2.8 copy-start.3
  11.8 141.2 %all-gather.7.cloned.1.call-start = ((), (), s32[]{:S(2)}) async-start(), calls=%async_computation.14 | async-start | bytes 4456448 | tf_op jit(solution)/shard_map/all_gather | solution.py:416
  38.7 198.4 %all-gather.11.cloned.1.call-start = ((), (), s32[]{:S(2)}) async-start(), calls=%async_computation.16 | async-start | bytes 9469952 | tf_op jit(solution)/shard_map/all_gather | solution.py:438
  62.5 3.7 %collective-permute-start = (f32[32,16,128]{2,1,0:T(8,128)S(1)}, f32[32,16,128]{2,1,0:T(8,128)S(1)}, u32[]{:S(2)}, u32[]{:S(2)}) collective-permute-start(f32[32,16,128]{2,1,0:T(8,128)S(1)} %slice.4), channel_id=1, source_target_pairs={{0,1},{1,0},{2,3},{3,2},{4,5},{5,4},{6,7},{7,6},{8,9},{9,8},{10,11... | collective-permute-start | bytes 786440 | tf_op jit(solution)/shard_map/ppermute | solution.py:493
  104.5 19.8 %all-to-all-start.4 = ((f32[16,4,16,128]{3,2,1,0:T(8,128)}), f32[16,4,16,128]{3,2,1,0:T(8,128)S(1)}, u32[]{:S(2)}, u32[]{:S(2)}) async-start(f32[16,4,16,128]{3,2,1,0:T(8,128)} %get-tuple-element.62), calls=%async_computation.4 | async-start | bytes 1048576 | tf_op jit(solution)/shard_map/all_to_all | solution.py:338
  146.3 13.3 %all-to-all-start.6 = ((f32[16,2,16,128]{3,2,1,0:T(8,128)}), f32[16,2,16,128]{3,2,1,0:T(8,128)S(1)}, u32[]{:S(2)}, u32[]{:S(2)}) async-start(f32[16,2,16,128]{3,2,1,0:T(8,128)} %shard_map.73), calls=%async_computation.6 | async-start | bytes 524288 | tf_op jit(solution)/shard_map/all_to_all | solution.py:338
  155.3 1.0 copy-start.4
  156.2 1.0 copy-start.5
  177.6 12.7 %all-to-all-start.8 = ((f32[16,1,16,128]{3,2,1,0:T(8,128)}), f32[16,1,16,128]{3,2,1,0:T(8,128)S(1)}, u32[]{:S(2)}, u32[]{:S(2)}) async-start(f32[16,1,16,128]{3,2,1,0:T(8,128)} %shard_map.77), calls=%async_computation.8 | async-start | bytes 262144 | tf_op jit(solution)/shard_map/all_to_all | solution.py:338
  205.6 10.9 %all-to-all-start.10 = ((f32[16,1,16,128]{3,2,1,0:T(8,128)}), f32[16,1,16,128]{3,2,1,0:T(8,128)S(1)}, u32[]{:S(2)}, u32[]{:S(2)}) async-start(f32[16,1,16,128]{3,2,1,0:T(8,128)} %shard_map.81), calls=%async_computation.10 | async-start | bytes 262144 | tf_op jit(solution)/shard_map/all_to_all | solution.py:338
  233.6 18.8 %all-to-all-start.12 = ((f32[16,8,256]{2,1,0:T(8,128)}), f32[16,8,256]{2,1,0:T(8,128)S(1)}, u32[]{:S(2)}, u32[]{:S(2)}) async-start(f32[16,8,256]{2,1,0:T(8,128)} %shard_map.86), calls=%async_computation.12 | async-start | bytes 262144 | tf_op jit(solution)/shard_map/all_to_all | solution.py:338
  248.3 2.1 copy-start
  250.4 2.1 copy-start.1
  257.5 1.3 collective-permute-start.1
  261.3 1.3 collective-permute-start.2
Sparse Core Ops, SparseCore 0:
  11.9 50.2 all-gather.8
  64.6 60.4 all-gather.6
  127.6 81.8 all-gather.10

commit v6 on v5

--- a/solution.py
+++ b/solution.py
@@ -168,14 +168,18 @@
             sol[k] = fold(own)[0]
             if kept is not None:
                 kept[k] = y_t
-        elif source == "y":
-            x = given[:, k].reshape(256, 128)
-            turned = pltpu.roll(x, 64, 1).reshape(16, 1, 16, 128)
-            y_t = jnp.concatenate([x.reshape(16, 1, 16, 128), turned], 1).reshape(512, 128).T[:64]
-        else:
+        elif source == "t":
             y_t = given[k]
         block = panels[k, 0, first:end].reshape((end - first) * 32, 512)
-        update = fold(dot3(block, jnp.concatenate([y_t, y_t], 0), ((1,), (1,))))
+        if source == "y":
+            x = given[:, k]
+            turned = pltpu.roll(x.reshape(256, 128), 64, 1).reshape(16, 16, 128)
+            low = lower((16, 16, 128))
+            halves = [jnp.where(low, x, turned)[:, None], jnp.where(low, turned, x)[:, None]]
+            y = jnp.concatenate(halves, 1).reshape(512, 128)
+            update = fold(dot3(block, y, ((1,), (0,))))
+        else:
+            update = fold(dot3(block, jnp.concatenate([y_t, y_t], 0), ((1,), (1,))))
         node = NODE_BASE[height] + jnp.minimum(s * 16 + pos[1], NODES[height] - 1)
         for d in range(end):
             node = parent[node]
@@ -195,10 +199,6 @@
     rows = inverse[:, 0].reshape(16, 2, 16, 512)
     rows = jnp.concatenate([rows[:, 0].reshape(256, 512), rows[:, 1].reshape(256, 512)], 0)
     high[0], low[0] = split(rows)
-
-
-def split_top_kernel(pos, parent, pattern, sizes, block, high, low):
-    high[0], low[0] = split(block[:, 0].reshape(512, 256))
 
 
 def join_kernel(pos, parent, pattern, sizes, here, there, out):
@@ -259,7 +259,7 @@
     return jnp.where(lane == level, pltpu.roll(lanes, level * 32, 1), own)
 
 
-def low_kernel(pos, parent, pattern, sizes, recv, high, low, out, left, z):
+def low_kernel(pos, parent, pattern, sizes, recv, block, out, left, z):
     step = pl.program_id(0)
 
     @pl.when(step == 0)
@@ -278,28 +278,34 @@
                     left[n - 4, :, g * 128 : (g + 1) * 128] = jnp.where(pos[1] % 2 == 0, -whole, 0.0)
         out[...] = jnp.zeros_like(out)
 
-    solved = dot3(z[step], (high[0], low[0]), ((1,), (0,)))
-    out[step] = place(out[step], solved, 0, pos)
-    target = parent[NODE_BASE[TOP] + step] - NODE_BASE[TOP + 1]
-    left[target] = left[target] - dot3(solved, (high[1], low[1]), ((1,), (1,)))
-    left[2] = left[2] - dot3(solved, (high[2], low[2]), ((1,), (1,)))
-
-
-def middle_kernel(pos, parent, pattern, sizes, left, other, before, high, low, out, after):
-    step = pl.program_id(0)
-
-    @pl.when(step == 0)
-    def _():
-        out[...] = before[...]
-        after[...] = left[2]
-
-    solved = dot3(left[step] + other[step], (high[0], low[0]), ((1,), (0,)))
-    out[step] = place(out[step], solved, 1, pos)
-    after[...] = after[...] - dot3(solved, (high[1], low[1]), ((1,), (1,)))
-
-
-def root_kernel(pos, parent, pattern, sizes, left, other, before, high, low, out):
-    solved = dot3(left[...] + other[...], (high[0], low[0]), ((1,), (0,)))
+    def matrix(i):
+        return block[:, i].reshape(512, 256)
+
+    solved = [dot3(z[2 * step + k], matrix(3 * k), ((1,), (0,))) for k in range(2)]
+    near = [dot3(solved[k], matrix(3 * k + 1), ((1,), (1,))) for k in range(2)]
+    far = [dot3(solved[k], matrix(3 * k + 2), ((1,), (1,))) for k in range(2)]
+    left[2] = left[2] - (far[0] + far[1])
+    for k in range(2):
+        node = 2 * step + k
+        out[node] = place(out[node], solved[k], 0, pos)
+        target = parent[NODE_BASE[TOP] + node] - NODE_BASE[TOP + 1]
+        left[target] = left[target] - near[k]
+
+
+def middle_kernel(pos, parent, pattern, sizes, left, other, before, block, out, after):
+    def matrix(i):
+        return block[:, i].reshape(512, 256)
+
+    solved = [dot3(left[k] + other[k], matrix(2 * k), ((1,), (0,))) for k in range(2)]
+    update = [dot3(solved[k], matrix(2 * k + 1), ((1,), (1,))) for k in range(2)]
+    out[...] = before[...]
+    for k in range(2):
+        out[k] = place(before[k], solved[k], 1, pos)
+    after[...] = left[2] - (update[0] + update[1])
+
+
+def root_kernel(pos, parent, pattern, sizes, left, other, before, block, out):
+    solved = dot3(left[...] + other[...], block[:, 0].reshape(512, 256), ((1,), (0,)))
     out[...] = before[...]
     out[0] = place(before[0], solved, 2, pos)
 
@@ -319,7 +325,7 @@
     slot_counts = [max(1, n // 16) for n in NODES]
     bases = [sum(slot_counts[:h]) for h in range(LEVELS)]
     def call(kernel, scratch, grid, in_specs, out_specs, out_shape, aliases, *args):
-        args = [pltpu.with_memory_space_constraint(a, pltpu.HBM) if a.size > 1 << 18 else a for a in args]
+        args = [pltpu.with_memory_space_constraint(a, pltpu.HBM) if a.size > 1 << 18 and a.dtype == f32 else a for a in args]
         return pl.pallas_call(
             functools.partial(with_parts, kernel),
             grid_spec=pltpu.PrefetchScalarGridSpec(
@@ -528,19 +534,8 @@
     )
     total = call(sum_kernel, [], (1,), [sides], sides, sides_shape, {}, exchange(turned, "pcol"))
     gathered = exchange(total, "prow")
-    top, _ = lax.optimization_barrier((top, total))
-    top = call(
-        split_top_kernel,
-        [],
-        (17,),
-        [pl.BlockSpec((16, 1, 32, 256), lambda s, *_: (0, s, 0, 0))],
-        [pl.BlockSpec((1, 512, 256), lambda s, *_: (s, 0, 0))] * 2,
-        [jax.ShapeDtypeStruct((17, 512, 256), jnp.bfloat16)] * 2,
-        {},
-        top,
-    )
     def halves_from(start, n):
-        return [pl.BlockSpec((n, 512, 256), lambda s, *_: (start // n + s, 0, 0))] * 2
+        return [pl.BlockSpec((16, n, 32, 256), lambda s, *_: (0, start // n + s, 0, 0))]
 
     def whole_of(*shape):
         return pl.BlockSpec(shape, lambda *_: (0,) * len(shape)), jax.ShapeDtypeStruct(shape, f32)
@@ -554,26 +549,26 @@
     solved, left = call(
         low_kernel,
         [pltpu.VMEM((4, 8, 512), f32)],
-        (4,),
-        [sides] + halves_from(0, 3),
+        (2,),
+        [sides] + halves_from(0, 6),
         [found, three],
         [found_shape, three_shape],
         {},
         gathered,
-        *top,
+        top,
     )
     solved, left = call(
         middle_kernel,
         [],
-        (2,),
-        [three, three, found] + halves_from(12, 2),
+        (1,),
+        [three, three, found] + halves_from(12, 4),
         [found, single],
         [found_shape, single_shape],
         {},
         left,
         other_core(left),
         solved,
-        *top,
+        top,
     )
     solved = call(
         root_kernel,
@@ -586,7 +581,7 @@
         left,
         other_core(left),
         solved,
-        *top,
+        top,
     )
     out = call(
         last_kernel,

time: 285 us -> 275 us (0.965)
  Pallas kernels: 73.6 us -> 59.4 us
  blocking collectives: 141 us -> 152 us
  local copies, waits for them, and re-layouts: 8.66 us -> 2.56 us
    pallas_call x29 -> x28, Pallas kernels: 73.6 us -> 59.4 us  [call(): pl.pallas_call(functools.partial(with_parts, kernel), grid_spec=pltpu.Pre...]
    all_to_all x8 -> x9, blocking collectives: 122 us -> 133 us  [exchange(): return lax.all_to_all(x, axis, 0, 0, tiled=True)]
    unnamed x13 -> x5, local copies, waits for them, and re-layouts: 7.79 us -> 1.69 us
    all_to_all x5 -> x4, waiting for transfers between devices: 21.9 us -> 25.1 us  [exchange(): return lax.all_to_all(x, axis, 0, 0, tiled=True)]
    all_to_all x5 -> x4, starting transfers between devices: 17.7 us -> 14.8 us  [exchange(): return lax.all_to_all(x, axis, 0, 0, tiled=True)]
  transfers between devices with their start and end apart: 11 -> 10, of which waited for: 7 -> 7; matrix products, arithmetic and copies ran while one was open for 0% -> 0% of each run, Pallas kernels for 21% -> 17%
where the time goes in v6:
time: 275 us; the launch traced here: 274 us
  blocking collectives  152 us (55%)
  Pallas kernels  59.4 us (22%)
  waiting for transfers between devices  28.1 us (10%)
  starting transfers between devices  18.8 us (7%)
  between operations  13.3 us (5%)
    all_to_all x9, blocking collectives, exchange(): return lax.all_to_all(x, axis, 0, 0, tiled=True)  133 us
    pallas_call x28, Pallas kernels, call(): pl.pallas_call(functools.partial(with_parts, kernel), grid_spec=pltpu.Pre...  59.4 us
    all_to_all x4, waiting for transfers between devices, exchange(): return lax.all_to_all(x, axis, 0, 0, tiled=True)  25.1 us
    all_to_all x1, blocking collectives, on_device(): lax.all_to_all(joined, 'pcol', 0, 0, tiled=True, axis_index_groups=[[core...  19.1 us
    all_to_all x4, starting transfers between devices, exchange(): return lax.all_to_all(x, axis, 0, 0, tiled=True)  14.8 us
  transfers between devices with their start and end apart: 10, of which 7 were waited for; matrix products, arithmetic and copies ran while one was open for 0% of the time, Pallas kernels for 17%

profile of v6, /device:TPU:1, one launch (start us, length us, event | category | flops | bytes accessed | tf_op | source)
XLA Modules:
  0.0 273.8 jit_solution(16353469848210717117)
XLA Ops:
  9.1 2.7 shard_map.64
  11.9 3.3 %shard_map.65 = f32[16,8,16,128]{3,2,1,0:T(8,128)S(1)} custom-call(s32[408]{0:T(512)S(1)} %concatenate.3.refs_0_, f32[19,16,128]{2,1,0:T(8,128)S(1)} %bitcast.15, f32[19,1,32,512]{3,2,1,0:T(8,128)} %refs_3_.3), custom_call_target="tpu_custom_call" | custom-call | tf_op jit(solution)/shard_map/pallas_call | solution.py:329
  15.2 23.5 %all_to_all.70.refs_1_ = f32[16,8,16,128]{3,2,1,0:T(8,128)S(1)} all-to-all(f32[16,8,16,128]{3,2,1,0:T(8,128)S(1)} %shard_map.65), channel_id=1, replica_groups=mesh['prow'=16,'pcol'=16] {'prow'}, dimensions={0} | all-to-all | bytes 2097152 | tf_op jit(solution)/shard_map/all_to_all | solution.py:344
  39.5 19.0 %all_to_all.71.refs_1_ = f32[16,8,16,128]{3,2,1,0:T(8,128)S(1)} all-to-all(f32[16,8,16,128]{3,2,1,0:T(8,128)S(1)} %get-tuple-element.58), channel_id=1, replica_groups=mesh['prow'=16,'pcol'=16] {'prow'}, dimensions={0} | all-to-all | bytes 2097152 | tf_op jit(solution)/shard_map/all_to_all | solution.py:344
  58.5 3.5 %shard_map.67.refs_1_ = f32[64,16,128]{2,1,0:T(8,128)S(1)} custom-call(s32[408]{0:T(512)S(1)} %concatenate.3.refs_0_, f32[16,8,16,128]{3,2,1,0:T(8,128)S(1)} %all_to_all.71.refs_1_, f32[19,1,7,32,512]{4,3,2,1,0:T(8,128)} %refs_4_.7), custom_call_target="tpu_custom_call" | custom-call | tf_op jit(solution)/shard_map/pallas_call | solution.py:329
  66.3 19.1 %all_to_all.72.refs_1_ = f32[8,4,16,128]{3,2,1,0:T(8,128)S(1)} all-to-all(f32[8,4,16,128]{3,2,1,0:T(8,128)S(1)} %shard_map.68), channel_id=1, replica_groups={{0,2,4,6,8,10,12,14},{1,3,5,7,9,11,13,15},{16,18,20,22,24,26,28,30},{17..., dimensions={0} | all-to-all | bytes 524288 | tf_op jit(solution)/shard_map/all_to_all | solution.py:511
  87.8 12.3 %all_to_all.73.refs_1_ = f32[16,4,16,128]{3,2,1,0:T(8,128)S(1)} all-to-all(f32[16,4,16,128]{3,2,1,0:T(8,128)S(1)} %shard_map.69), channel_id=1, replica_groups=mesh['prow'=16,'pcol'=16] {'prow'}, dimensions={0} | all-to-all | bytes 1048576 | tf_op jit(solution)/shard_map/all_to_all | solution.py:344
  103.9 3.6 %all-to-all-start.4 = ((f32[16,4,16,128]{3,2,1,0:T(8,128)}), f32[16,4,16,128]{3,2,1,0:T(8,128)S(1)}, u32[]{:S(2)}, u32[]{:S(2)}) async-start(f32[16,4,16,128]{3,2,1,0:T(8,128)} %get-tuple-element.59), calls=%async_computation.4 | async-start | bytes 1048576 | tf_op jit(solution)/shard_map/all_to_all | solution.py:344
  107.5 4.9 %shard_map.71 = (f32[32,16,128]{2,1,0:T(8,128)S(1)}, f32[16,16,128]{2,1,0:T(8,128)S(1)}, f32[16,16,128]{2,1,0:T(8,128)S(1)}, f32[16,16,128]{2,1,0:T(8,128)S(1)},...) custom-call(s32[408]{0:T(512)S(1)} %concatenate.3.refs_0_, f32[16,8,16,128]{3,2,1,0:T(8,128)S(1)} %all_to_all.71.refs_1_, ...), custom_call_target="tpu_custom_call" | custom-call | tf_op jit(solution)/shard_map/pallas_call | solution.py:329
  112.4 11.3 %all-to-all-done.4.refs_1_ = f32[16,4,16,128]{3,2,1,0:T(8,128)S(1)} async-done(((f32[16,4,16,128]{3,2,1,0:T(8,128)}), f32[16,4,16,128]{3,2,1,0:T(8,128)S(1)}, u32[]{:S(2)}, u32[]{:S(2)}) %all-to-all-start.4) | async-done | bytes 524320 | tf_op jit(solution)/shard_map/all_to_all | solution.py:344
  125.9 18.2 %all_to_all.74.refs_1_ = f32[16,2,16,128]{3,2,1,0:T(8,128)S(1)} all-to-all(f32[16,2,16,128]{3,2,1,0:T(8,128)S(1)} %bitcast.18), channel_id=1, replica_groups=mesh['prow'=16,'pcol'=16] {'pcol'}, dimensions={0} | all-to-all | bytes 524288 | tf_op jit(solution)/shard_map/all_to_all | solution.py:344
  145.4 4.2 %all-to-all-start.6 = ((f32[16,2,16,128]{3,2,1,0:T(8,128)}), f32[16,2,16,128]{3,2,1,0:T(8,128)}, u32[]{:S(2)}, u32[]{:S(2)}) async-start(f32[16,2,16,128]{3,2,1,0:T(8,128)} %shard_map.73), calls=%async_computation.6 | async-start | bytes 524288 | tf_op jit(solution)/shard_map/all_to_all | solution.py:344
  149.6 2.9 %shard_map.75 = (f32[16,16,128]{2,1,0:T(8,128)S(1)}, f32[16,16,128]{2,1,0:T(8,128)S(1)}, f32[16,16,128]{2,1,0:T(8,128)S(1)}, f32[16,16,128]{2,1,0:T(8,128)S(1)}, f32[16,16,128]{2,1,0:T(8,128)S(1)}) custom-call(s32[408]{0:T(512)S(1)} %concatenate.3.refs_0_, ...), custom_call_target="tpu_custom_call", output_to_operand_aliasing={{0}: (3, {}), {1}: (4, {}), {2}: (5, {}), {3}: (6, {}), {4}... | custom-call | tf_op jit(solution)/shard_map/pallas_call | solution.py:329
  154.8 5.1 %all-to-all-done.6.refs_1_ = f32[16,2,16,128]{3,2,1,0:T(8,128)} async-done(((f32[16,2,16,128]{3,2,1,0:T(8,128)}), f32[16,2,16,128]{3,2,1,0:T(8,128)}, u32[]{:S(2)}, u32[]{:S(2)}) %all-to-all-start.6) | async-done | bytes 262176 | tf_op jit(solution)/shard_map/all_to_all | solution.py:344
  162.5 13.9 %all_to_all.75.refs_1_ = f32[16,1,16,128]{3,2,1,0:T(8,128)S(1)} all-to-all(f32[16,1,16,128]{3,2,1,0:T(8,128)S(1)} %bitcast.17), channel_id=1, replica_groups=mesh['prow'=16,'pcol'=16] {'pcol'}, dimensions={0} | all-to-all | bytes 262144 | tf_op jit(solution)/shard_map/all_to_all | solution.py:344
  177.6 3.5 %all-to-all-start.8 = ((f32[16,1,16,128]{3,2,1,0:T(8,128)}), f32[16,1,16,128]{3,2,1,0:T(8,128)S(1)}, u32[]{:S(2)}, u32[]{:S(2)}) async-start(f32[16,1,16,128]{3,2,1,0:T(8,128)} %shard_map.77), calls=%async_computation.8 | async-start | bytes 262144 | tf_op jit(solution)/shard_map/all_to_all | solution.py:344
  185.2 5.1 %all-to-all-done.8.refs_1_ = f32[16,1,16,128]{3,2,1,0:T(8,128)S(1)} async-done(((f32[16,1,16,128]{3,2,1,0:T(8,128)}), f32[16,1,16,128]{3,2,1,0:T(8,128)S(1)}, u32[]{:S(2)}, u32[]{:S(2)}) %all-to-all-start.8) | async-done | bytes 131104 | tf_op jit(solution)/shard_map/all_to_all | solution.py:344
  192.2 12.2 %all_to_all.76.refs_1_ = f32[16,1,16,128]{3,2,1,0:T(8,128)S(1)} all-to-all(f32[16,1,16,128]{3,2,1,0:T(8,128)S(1)} %bitcast.13), channel_id=1, replica_groups=mesh['prow'=16,'pcol'=16] {'pcol'}, dimensions={0} | all-to-all | bytes 262144 | tf_op jit(solution)/shard_map/all_to_all | solution.py:344
  205.7 3.5 %all-to-all-start.10 = ((f32[16,1,16,128]{3,2,1,0:T(8,128)}), f32[16,1,16,128]{3,2,1,0:T(8,128)S(1)}, u32[]{:S(2)}, u32[]{:S(2)}) async-start(f32[16,1,16,128]{3,2,1,0:T(8,128)} %shard_map.81), calls=%async_computation.10 | async-start | bytes 262144 | tf_op jit(solution)/shard_map/all_to_all | solution.py:344
  213.0 3.6 %all-to-all-done.10.refs_1_ = f32[16,1,16,128]{3,2,1,0:T(8,128)S(1)} async-done(((f32[16,1,16,128]{3,2,1,0:T(8,128)}), f32[16,1,16,128]{3,2,1,0:T(8,128)S(1)}, u32[]{:S(2)}, u32[]{:S(2)}) %all-to-all-start.10) | async-done | bytes 131104 | tf_op jit(solution)/shard_map/all_to_all | solution.py:344
  219.6 12.8 %all_to_all.77.refs_1_ = f32[16,8,256]{2,1,0:T(8,128)S(1)} all-to-all(f32[16,8,256]{2,1,0:T(8,128)S(1)} %shard_map.85), channel_id=1, replica_groups=mesh['prow'=16,'pcol'=16] {'pcol'}, dimensions={0} | all-to-all | bytes 262144 | tf_op jit(solution)/shard_map/all_to_all | solution.py:344
  233.0 10.2 %all_to_all.78.refs_1_ = f32[16,8,256]{2,1,0:T(8,128)S(1)} all-to-all(f32[16,8,256]{2,1,0:T(8,128)S(1)} %shard_map.86), channel_id=1, replica_groups=mesh['prow'=16,'pcol'=16] {'prow'}, dimensions={0} | all-to-all | bytes 262144 | tf_op jit(solution)/shard_map/all_to_all | solution.py:344
  243.2 4.3 %shard_map.88 = (f32[16,8,128]{2,1,0:T(8,128)S(1)}, f32[3,8,512]{2,1,0:T(8,128)S(1)}) custom-call(s32[408]{0:T(512)S(1)} %concatenate.3.refs_0_, f32[16,8,256]{2,1,0:T(8,128)S(1)} %all_to_all.78.refs_1_, f32[16,17,32,256]{3,2,1,0:T(8,128)} %bitcast.19), custom_call_target="tpu_custom_call" | custom-call | tf_op jit(solution)/shard_map/pallas_call | solution.py:329
  255.2 10.6 %all_to_all.79.refs_1_ = f32[16,8,128]{2,1,0:T(8,128)S(1)} all-to-all(f32[16,8,128]{2,1,0:T(8,128)S(1)} %shard_map.90), channel_id=1, replica_groups=mesh['prow'=16,'pcol'=16] {'pcol'}, dimensions={0} | all-to-all | bytes 131072 | tf_op jit(solution)/shard_map/all_to_all | solution.py:344
  (45 shorter events, 47.3 us)
Async XLA Ops:
  6.5 94.9 %all-gather.9.cloned.1.call-start = ((), (), s32[]{:S(2)}) async-start(), calls=%async_computation.15 | async-start | bytes 6684672 | tf_op jit(solution)/shard_map/all_gather | solution.py:377
  8.2 0.9 copy-start
  9.1 2.8 %copy-start.1 = (f32[19,1,2048]{2,1,0:T(1,128)S(1)}, f32[19,1,2048]{2,1,0:T(1,128)}, u32[]{:S(2)}) copy-start(f32[19,1,2048]{2,1,0:T(1,128)} %param.6) | copy-start | bytes 466948
  11.8 140.7 %all-gather.7.cloned.1.call-start = ((), (), s32[]{:S(2)}) async-start(), calls=%async_computation.14 | async-start | bytes 4456448 | tf_op jit(solution)/shard_map/all_gather | solution.py:422
  38.8 204.4 %all-gather.11.cloned.1.call-start = ((), (), s32[]{:S(2)}) async-start(), calls=%async_computation.16 | async-start | bytes 9469952 | tf_op jit(solution)/shard_map/all_gather | solution.py:444
  62.0 3.7 %collective-permute-start = (f32[32,16,128]{2,1,0:T(8,128)S(1)}, f32[32,16,128]{2,1,0:T(8,128)S(1)}, u32[]{:S(2)}, u32[]{:S(2)}) collective-permute-start(f32[32,16,128]{2,1,0:T(8,128)S(1)} %slice.4), channel_id=1, source_target_pairs={{0,1},{1,0},{2,3},{3,2},{4,5},{5,4},{6,7},{7,6},{8,9},{9,8},{10,11... | collective-permute-start | bytes 786440 | tf_op jit(solution)/shard_map/ppermute | solution.py:499
  103.9 19.8 %all-to-all-start.4 = ((f32[16,4,16,128]{3,2,1,0:T(8,128)}), f32[16,4,16,128]{3,2,1,0:T(8,128)S(1)}, u32[]{:S(2)}, u32[]{:S(2)}) async-start(f32[16,4,16,128]{3,2,1,0:T(8,128)} %get-tuple-element.59), calls=%async_computation.4 | async-start | bytes 1048576 | tf_op jit(solution)/shard_map/all_to_all | solution.py:344
  145.4 14.5 %all-to-all-start.6 = ((f32[16,2,16,128]{3,2,1,0:T(8,128)}), f32[16,2,16,128]{3,2,1,0:T(8,128)}, u32[]{:S(2)}, u32[]{:S(2)}) async-start(f32[16,2,16,128]{3,2,1,0:T(8,128)} %shard_map.73), calls=%async_computation.6 | async-start | bytes 524288 | tf_op jit(solution)/shard_map/all_to_all | solution.py:344
  177.6 12.7 %all-to-all-start.8 = ((f32[16,1,16,128]{3,2,1,0:T(8,128)}), f32[16,1,16,128]{3,2,1,0:T(8,128)S(1)}, u32[]{:S(2)}, u32[]{:S(2)}) async-start(f32[16,1,16,128]{3,2,1,0:T(8,128)} %shard_map.77), calls=%async_computation.8 | async-start | bytes 262144 | tf_op jit(solution)/shard_map/all_to_all | solution.py:344
  205.7 10.9 %all-to-all-start.10 = ((f32[16,1,16,128]{3,2,1,0:T(8,128)}), f32[16,1,16,128]{3,2,1,0:T(8,128)S(1)}, u32[]{:S(2)}, u32[]{:S(2)}) async-start(f32[16,1,16,128]{3,2,1,0:T(8,128)} %shard_map.81), calls=%async_computation.10 | async-start | bytes 262144 | tf_op jit(solution)/shard_map/all_to_all | solution.py:344
  247.5 1.8 collective-permute-start.1
  252.0 1.3 collective-permute-start.2
Sparse Core Ops, SparseCore 0:
  11.9 50.2 all-gather.8
  64.7 60.1 all-gather.6
  127.4 82.0 all-gather.10

commit v7 on v6

--- a/solution.py
+++ b/solution.py
@@ -12,6 +12,7 @@
 GATHER_FROM = 2
 CUTS = (2, 5)
 SCRATCH = [pltpu.VMEM((192, 512), jnp.float32)]
+PAIRED = 2
 TOP = 5
 VMEM_LIMIT = 24 * 1024 * 1024
 
@@ -93,7 +94,7 @@
 def residue_kernel(height, slots, slot_base, pos, parent, pattern, sizes, recv, rhs, out):
     for s in range(slots):
         total = recv[0, s]
-        for i in range(1, 16):
+        for i in range(1, recv.shape[0]):
             total = total + recv[i, s]
         keep = own_mask(pos, sizes, slot_base + s, s, NODES[height])
         z = jnp.where(keep, rhs[s] - total, 0.0)
@@ -138,7 +139,7 @@
 def spread_kernel(height, slots, slot_base, source, first, end, pos, parent, pattern, sizes, *refs):
     refs = list(refs)
     given = refs.pop(0)
-    inverse = (refs.pop(0), refs.pop(0)) if source == "z" else None
+    inverse = refs.pop(0) if source == "z" else None
     panels = refs.pop(0)
     before = [refs.pop(0) for _ in range(first, end)] if height > 0 else []
     sol = refs.pop(0) if source == "z" else None
@@ -157,7 +158,7 @@
         if source == "z":
             turned = given[:, k].reshape(256, 128).T
             z_t = jnp.concatenate([turned[:64], turned[64:]], 1)
-            y_t = dot3(z_t, (inverse[0][k], inverse[1][k]), ((1,), (0,)))
+            y_t = dot3(z_t, (inverse[k, :512], inverse[k, 512:]), ((1,), (0,)))
             limit = sizes[slot]
             y_t = jnp.where(lax.broadcasted_iota(jnp.int32, (64, 512), 1) < limit, y_t, 0.0)
             scratch[pl.ds(0, 64), :] = y_t
@@ -187,18 +188,19 @@
                 continue
             target = height + 1 + d
             j = node - NODE_BASE[target]
-            if target == 1:
-                where = ((j + pos[1]) % 2 * 8 + j % 16 // 2) * 4 + j // 16
+            many = max(1, NODES[target] // 16)
+            if target <= PAIRED:
+                where = ((j + pos[1]) % 2 * 8 + j % 16 // 2) * many + j // 16
             else:
-                where = (j % 16) * max(1, NODES[target] // 16) + j // 16
+                where = (j % 16) * many + j // 16
             scale = pattern[slot * 7 + d].astype(jnp.float32)
             after[d - first][where] += scale * update[d - first]
 
 
-def split_inverse_kernel(pos, parent, pattern, sizes, inverse, high, low):
+def split_inverse_kernel(pos, parent, pattern, sizes, inverse, both):
     rows = inverse[:, 0].reshape(16, 2, 16, 512)
     rows = jnp.concatenate([rows[:, 0].reshape(256, 512), rows[:, 1].reshape(256, 512)], 0)
-    high[0], low[0] = split(rows)
+    both[0, :512], both[0, 512:] = split(rows)
 
 
 def join_kernel(pos, parent, pattern, sizes, here, there, out):
@@ -325,7 +327,12 @@
     slot_counts = [max(1, n // 16) for n in NODES]
     bases = [sum(slot_counts[:h]) for h in range(LEVELS)]
     def call(kernel, scratch, grid, in_specs, out_specs, out_shape, aliases, *args):
-        args = [pltpu.with_memory_space_constraint(a, pltpu.HBM) if a.size > 1 << 18 and a.dtype == f32 else a for a in args]
+        args = [
+            pltpu.with_memory_space_constraint(a, pltpu.HBM)
+            if a.size > 1 << 18 and a.dtype == f32
+            else a
+            for a in args
+        ]
         return pl.pallas_call(
             functools.partial(with_parts, kernel),
             grid_spec=pltpu.PrefetchScalarGridSpec(
@@ -388,7 +395,15 @@
         rhs_all = pl.BlockSpec((count, 16, 128), lambda *_, b=base // count: (b, 0, 0))
         if whole:
             z = call(
-                functools.partial(residue_kernel, *info), [], (1,), [every, rhs_all], every, piece, {}, recv, rhs
+                functools.partial(residue_kernel, *info),
+                [],
+                (1,),
+                [pl.BlockSpec(recv.shape, lambda *_: (0, 0, 0, 0)), rhs_all],
+                every,
+                piece,
+                {},
+                recv,
+                rhs,
             )
             gathered = exchange(z, "prow")
             lo, inverse = [pair for pair in inverses if pair[0] <= base][-1]
@@ -398,8 +413,8 @@
                 [],
                 (count,),
                 [pl.BlockSpec((16, 1, 32, 512), lambda s, *_, b=base - lo: (0, b + s, 0, 0))],
-                [pl.BlockSpec((1, 512, 512), lambda s, *_: (s, 0, 0))] * 2,
-                [jax.ShapeDtypeStruct((count, 512, 512), jnp.bfloat16)] * 2,
+                pl.BlockSpec((1, 1024, 512), lambda s, *_: (s, 0, 0)),
+                jax.ShapeDtypeStruct((count, 1024, 512), jnp.bfloat16),
                 {},
                 inverse,
             )
@@ -453,8 +468,8 @@
             args = [given]
             out_specs, out_shape = [], []
             if source == "z":
-                in_specs += [pl.BlockSpec((1, 512, 512), lambda s, *_: (s, 0, 0))] * 2
-                args += inverse
+                in_specs.append(pl.BlockSpec((1, 1024, 512), lambda s, *_: (s, 0, 0)))
+                args.append(inverse)
                 out_specs.append(pl.BlockSpec((1, 16, 128), lambda s, *_: (s, 0, 0)))
                 out_shape.append(own)
                 if end < reach:
@@ -494,16 +509,16 @@
         if height + 1 < TOP:
             following = slot_counts[height + 1]
             pending = results[1:]
-            if height == 0:
-                half = pl.BlockSpec((32, 16, 128), lambda *_: (0, 0, 0))
-                there = lax.ppermute(results[0][32:], "pcol", [(i, i ^ 1) for i in range(16)])
+            if height < PAIRED:
+                half = pl.BlockSpec((8 * following, 16, 128), lambda *_: (0, 0, 0))
+                there = lax.ppermute(results[0][8 * following :], "pcol", [(i, i ^ 1) for i in range(16)])
                 joined = call(
                     join_kernel,
                     [],
                     (1,),
                     [half, half],
-                    pl.BlockSpec((8, 4, 16, 128), lambda *_: (0, 0, 0, 0)),
-                    jax.ShapeDtypeStruct((8, 4, 16, 128), f32),
+                    pl.BlockSpec((8, following, 16, 128), lambda *_: (0, 0, 0, 0)),
+                    jax.ShapeDtypeStruct((8, following, 16, 128), f32),
                     {},
                     results[0],
                     there,

time: 275 us -> 274 us (level)
  blocking collectives: 152 us -> 148 us
  starting transfers between devices: 18.8 us -> 22.2 us
    all_to_all x9 -> x8, blocking collectives: 133 us -> 118 us  [exchange(): return lax.all_to_all(x, axis, 0, 0, tiled=True)]
    all_to_all x1 -> x2, blocking collectives: 19.1 us -> 29.7 us  [on_device(): lax.all_to_all(joined, 'pcol', 0, 0, tiled=True, axis_index_groups=[[core...]
    ppermute x1 -> x2, starting transfers between devices: 2.56 us -> 6.6 us  [on_device(): lax.ppermute(results[0][8 * following:], 'pcol', [(i, i ^ 1) for i in ran...]
    pallas_call x28 -> x29, Pallas kernels: 59.4 us -> 59.9 us  [call(): pl.pallas_call(functools.partial(with_parts, kernel), grid_spec=pltpu.Pre...]
  transfers between devices with their start and end apart: 10 -> 11, of which waited for: 7 -> 8; matrix products, arithmetic and copies ran while one was open for 0% -> 0% of each run, Pallas kernels for 17% -> 17%
where the time goes in v7:
time: 274 us; the launch traced here: 273 us
  blocking collectives  148 us (54%)
  Pallas kernels  59.9 us (22%)
  waiting for transfers between devices  27.3 us (10%)
  starting transfers between devices  22.2 us (8%)
  between operations  13.3 us (5%)
    all_to_all x8, blocking collectives, exchange(): return lax.all_to_all(x, axis, 0, 0, tiled=True)  118 us
    pallas_call x29, Pallas kernels, call(): pl.pallas_call(functools.partial(with_parts, kernel), grid_spec=pltpu.Pre...  59.9 us
    all_to_all x2, blocking collectives, on_device(): lax.all_to_all(joined, 'pcol', 0, 0, tiled=True, axis_index_groups=[[core...  29.7 us
    all_to_all x4, waiting for transfers between devices, exchange(): return lax.all_to_all(x, axis, 0, 0, tiled=True)  23.3 us
    all_to_all x4, starting transfers between devices, exchange(): return lax.all_to_all(x, axis, 0, 0, tiled=True)  14.1 us
    ppermute x2, starting transfers between devices, on_device(): lax.ppermute(results[0][8 * following:], 'pcol', [(i, i ^ 1) for i in ran...  6.6 us
  transfers between devices with their start and end apart: 11, of which 8 were waited for; matrix products, arithmetic and copies ran while one was open for 0% of the time, Pallas kernels for 17%

profile of v7, /device:TPU:1, one launch (start us, length us, event | category | flops | bytes accessed | tf_op | source)
XLA Modules:
  0.0 272.8 jit_solution(7913063132641616806)
XLA Ops:
  11.9 3.3 %shard_map.65 = f32[16,8,16,128]{3,2,1,0:T(8,128)S(1)} custom-call(s32[408]{0:T(512)S(1)} %concatenate.3.refs_0_, f32[19,16,128]{2,1,0:T(8,128)S(1)} %bitcast.14, f32[19,1,32,512]{3,2,1,0:T(8,128)} %refs_3_.6), custom_call_target="tpu_custom_call" | custom-call | tf_op jit(solution)/shard_map/pallas_call | solution.py:336
  15.2 23.5 %all_to_all.70.refs_1_ = f32[16,8,16,128]{3,2,1,0:T(8,128)S(1)} all-to-all(f32[16,8,16,128]{3,2,1,0:T(8,128)S(1)} %shard_map.65), channel_id=1, replica_groups=mesh['prow'=16,'pcol'=16] {'prow'}, dimensions={0} | all-to-all | bytes 2097152 | tf_op jit(solution)/shard_map/all_to_all | solution.py:351
  39.5 19.0 %all_to_all.71.refs_1_ = f32[16,8,16,128]{3,2,1,0:T(8,128)S(1)} all-to-all(f32[16,8,16,128]{3,2,1,0:T(8,128)S(1)} %get-tuple-element.52), channel_id=1, replica_groups=mesh['prow'=16,'pcol'=16] {'prow'}, dimensions={0} | all-to-all | bytes 2097152 | tf_op jit(solution)/shard_map/all_to_all | solution.py:351
  58.5 3.5 %shard_map.67.refs_1_ = f32[64,16,128]{2,1,0:T(8,128)S(1)} custom-call(s32[408]{0:T(512)S(1)} %concatenate.3.refs_0_, f32[16,8,16,128]{3,2,1,0:T(8,128)S(1)} %all_to_all.71.refs_1_, f32[19,1,7,32,512]{4,3,2,1,0:T(8,128)} %refs_3_.9), custom_call_target="tpu_custom_call" | custom-call | tf_op jit(solution)/shard_map/pallas_call | solution.py:336
  66.3 19.1 %all_to_all.72.refs_1_ = f32[8,4,16,128]{3,2,1,0:T(8,128)S(1)} all-to-all(f32[8,4,16,128]{3,2,1,0:T(8,128)S(1)} %shard_map.68), channel_id=1, replica_groups={{0,2,4,6,8,10,12,14},{1,3,5,7,9,11,13,15},{16,18,20,22,24,26,28,30},{17..., dimensions={0} | all-to-all | bytes 524288 | tf_op jit(solution)/shard_map/all_to_all | solution.py:526
  87.8 12.3 %all_to_all.73.refs_1_ = f32[16,4,16,128]{3,2,1,0:T(8,128)S(1)} all-to-all(f32[16,4,16,128]{3,2,1,0:T(8,128)S(1)} %shard_map.69), channel_id=1, replica_groups=mesh['prow'=16,'pcol'=16] {'prow'}, dimensions={0} | all-to-all | bytes 1048576 | tf_op jit(solution)/shard_map/all_to_all | solution.py:351
  103.9 3.6 %all-to-all-start.4 = ((f32[16,4,16,128]{3,2,1,0:T(8,128)}), f32[16,4,16,128]{3,2,1,0:T(8,128)S(1)}, u32[]{:S(2)}, u32[]{:S(2)}) async-start(f32[16,4,16,128]{3,2,1,0:T(8,128)} %get-tuple-element.53), calls=%async_computation.4 | async-start | bytes 1048576 | tf_op jit(solution)/shard_map/all_to_all | solution.py:351
  107.5 4.9 %shard_map.71 = (f32[32,16,128]{2,1,0:T(8,128)S(1)}, f32[16,16,128]{2,1,0:T(8,128)S(1)}, f32[16,16,128]{2,1,0:T(8,128)S(1)}, f32[16,16,128]{2,1,0:T(8,128)S(1)},...) custom-call(s32[408]{0:T(512)S(1)} %concatenate.3.refs_0_, f32[16,8,16,128]{3,2,1,0:T(8,128)S(1)} %all_to_all.71.refs_1_, ...), custom_call_target="tpu_custom_call" | custom-call | tf_op jit(solution)/shard_map/pallas_call | solution.py:336
  112.4 11.3 %all-to-all-done.4.refs_1_ = f32[16,4,16,128]{3,2,1,0:T(8,128)S(1)} async-done(((f32[16,4,16,128]{3,2,1,0:T(8,128)}), f32[16,4,16,128]{3,2,1,0:T(8,128)S(1)}, u32[]{:S(2)}, u32[]{:S(2)}) %all-to-all-start.4) | async-done | bytes 524320 | tf_op jit(solution)/shard_map/all_to_all | solution.py:351
  126.0 4.0 %collective-permute-start.1 = (f32[16,16,128]{2,1,0:T(8,128)S(1)}, f32[16,16,128]{2,1,0:T(8,128)S(1)}, u32[]{:S(2)}, u32[]{:S(2)}) collective-permute-start(f32[16,16,128]{2,1,0:T(8,128)S(1)} %slice.9), channel_id=1, source_target_pairs={{0,1},{1,0},{2,3},{3,2},{4,5},{5,4},{6,7},{7,6},{8,9},{9,8},{10,11... | collective-permute-start | bytes 393224 | tf_op jit(solution)/shard_map/ppermute | solution.py:514
  131.6 10.6 %all_to_all.74.refs_1_ = f32[8,2,16,128]{3,2,1,0:T(8,128)S(1)} all-to-all(f32[8,2,16,128]{3,2,1,0:T(8,128)S(1)} %shard_map.73), channel_id=1, replica_groups={{0,2,4,6,8,10,12,14},{1,3,5,7,9,11,13,15},{16,18,20,22,24,26,28,30},{17..., dimensions={0} | all-to-all | bytes 262144 | tf_op jit(solution)/shard_map/all_to_all | solution.py:526
  143.5 3.5 %all-to-all-start.6 = ((f32[16,2,16,128]{3,2,1,0:T(8,128)}), f32[16,2,16,128]{3,2,1,0:T(8,128)S(1)}, u32[]{:S(2)}, u32[]{:S(2)}) async-start(f32[16,2,16,128]{3,2,1,0:T(8,128)} %shard_map.74), calls=%async_computation.6 | async-start | bytes 524288 | tf_op jit(solution)/shard_map/all_to_all | solution.py:351
  147.0 2.9 %shard_map.76 = (f32[16,16,128]{2,1,0:T(8,128)S(1)}, f32[16,16,128]{2,1,0:T(8,128)S(1)}, f32[16,16,128]{2,1,0:T(8,128)S(1)}, f32[16,16,128]{2,1,0:T(8,128)S(1)}, f32[16,16,128]{2,1,0:T(8,128)S(1)}) custom-call(s32[408]{0:T(512)S(1)} %concatenate.3.refs_0_, ...), custom_call_target="tpu_custom_call", output_to_operand_aliasing={{0}: (3, {}), {1}: (4, {}), {2}: (5, {}), {3}: (6, {}), {4}... | custom-call | tf_op jit(solution)/shard_map/pallas_call | solution.py:336
  152.2 3.3 %all-to-all-done.6.refs_1_ = f32[16,2,16,128]{3,2,1,0:T(8,128)S(1)} async-done(((f32[16,2,16,128]{3,2,1,0:T(8,128)}), f32[16,2,16,128]{3,2,1,0:T(8,128)S(1)}, u32[]{:S(2)}, u32[]{:S(2)}) %all-to-all-start.6) | async-done | bytes 262176 | tf_op jit(solution)/shard_map/all_to_all | solution.py:351
  158.1 16.4 %all_to_all.75.refs_1_ = f32[16,1,16,128]{3,2,1,0:T(8,128)S(1)} all-to-all(f32[16,1,16,128]{3,2,1,0:T(8,128)S(1)} %bitcast.16), channel_id=1, replica_groups=mesh['prow'=16,'pcol'=16] {'pcol'}, dimensions={0} | all-to-all | bytes 262144 | tf_op jit(solution)/shard_map/all_to_all | solution.py:351
  175.7 3.5 %all-to-all-start.8 = ((f32[16,1,16,128]{3,2,1,0:T(8,128)}), f32[16,1,16,128]{3,2,1,0:T(8,128)S(1)}, u32[]{:S(2)}, u32[]{:S(2)}) async-start(f32[16,1,16,128]{3,2,1,0:T(8,128)} %shard_map.78), calls=%async_computation.8 | async-start | bytes 262144 | tf_op jit(solution)/shard_map/all_to_all | solution.py:351
  183.3 5.0 %all-to-all-done.8.refs_1_ = f32[16,1,16,128]{3,2,1,0:T(8,128)S(1)} async-done(((f32[16,1,16,128]{3,2,1,0:T(8,128)}), f32[16,1,16,128]{3,2,1,0:T(8,128)S(1)}, u32[]{:S(2)}, u32[]{:S(2)}) %all-to-all-start.8) | async-done | bytes 131104 | tf_op jit(solution)/shard_map/all_to_all | solution.py:351
  190.4 12.2 %all_to_all.76.refs_1_ = f32[16,1,16,128]{3,2,1,0:T(8,128)S(1)} all-to-all(f32[16,1,16,128]{3,2,1,0:T(8,128)S(1)} %bitcast.12), channel_id=1, replica_groups=mesh['prow'=16,'pcol'=16] {'pcol'}, dimensions={0} | all-to-all | bytes 262144 | tf_op jit(solution)/shard_map/all_to_all | solution.py:351
  203.8 3.5 %all-to-all-start.10 = ((f32[16,1,16,128]{3,2,1,0:T(8,128)}), f32[16,1,16,128]{3,2,1,0:T(8,128)S(1)}, u32[]{:S(2)}, u32[]{:S(2)}) async-start(f32[16,1,16,128]{3,2,1,0:T(8,128)} %shard_map.82), calls=%async_computation.10 | async-start | bytes 262144 | tf_op jit(solution)/shard_map/all_to_all | solution.py:351
  211.0 3.6 %all-to-all-done.10.refs_1_ = f32[16,1,16,128]{3,2,1,0:T(8,128)S(1)} async-done(((f32[16,1,16,128]{3,2,1,0:T(8,128)}), f32[16,1,16,128]{3,2,1,0:T(8,128)S(1)}, u32[]{:S(2)}, u32[]{:S(2)}) %all-to-all-start.10) | async-done | bytes 131104 | tf_op jit(solution)/shard_map/all_to_all | solution.py:351
  217.6 13.9 %all_to_all.77.refs_1_ = f32[16,8,256]{2,1,0:T(8,128)S(1)} all-to-all(f32[16,8,256]{2,1,0:T(8,128)S(1)} %shard_map.86), channel_id=1, replica_groups=mesh['prow'=16,'pcol'=16] {'pcol'}, dimensions={0} | all-to-all | bytes 262144 | tf_op jit(solution)/shard_map/all_to_all | solution.py:351
  232.2 10.0 %all_to_all.78.refs_1_ = f32[16,8,256]{2,1,0:T(8,128)S(1)} all-to-all(f32[16,8,256]{2,1,0:T(8,128)S(1)} %shard_map.87), channel_id=1, replica_groups=mesh['prow'=16,'pcol'=16] {'prow'}, dimensions={0} | all-to-all | bytes 262144 | tf_op jit(solution)/shard_map/all_to_all | solution.py:351
  242.2 4.3 %shard_map.89 = (f32[16,8,128]{2,1,0:T(8,128)S(1)}, f32[3,8,512]{2,1,0:T(8,128)S(1)}) custom-call(s32[408]{0:T(512)S(1)} %concatenate.3.refs_0_, f32[16,8,256]{2,1,0:T(8,128)S(1)} %all_to_all.78.refs_1_, f32[16,17,32,256]{3,2,1,0:T(8,128)} %bitcast.17), custom_call_target="tpu_custom_call" | custom-call | tf_op jit(solution)/shard_map/pallas_call | solution.py:336
  254.2 10.6 %all_to_all.79.refs_1_ = f32[16,8,128]{2,1,0:T(8,128)S(1)} all-to-all(f32[16,8,128]{2,1,0:T(8,128)S(1)} %shard_map.91), channel_id=1, replica_groups=mesh['prow'=16,'pcol'=16] {'pcol'}, dimensions={0} | all-to-all | bytes 131072 | tf_op jit(solution)/shard_map/all_to_all | solution.py:351
  (49 shorter events, 51.6 us)
Async XLA Ops:
  6.5 95.0 %all-gather.9.cloned.1.call-start = ((), (), s32[]{:S(2)}) async-start(), calls=%async_computation.15 | async-start | bytes 6684672 | tf_op jit(solution)/shard_map/all_gather | solution.py:384
  8.2 0.9 copy-start
  9.1 2.8 %copy-start.1 = (f32[19,1,2048]{2,1,0:T(1,128)S(1)}, f32[19,1,2048]{2,1,0:T(1,128)}, u32[]{:S(2)}) copy-start(f32[19,1,2048]{2,1,0:T(1,128)} %param.6) | copy-start | bytes 466948
  11.8 138.1 %all-gather.7.cloned.1.call-start = ((), (), s32[]{:S(2)}) async-start(), calls=%async_computation.14 | async-start | bytes 4456448 | tf_op jit(solution)/shard_map/all_gather | solution.py:437
  38.8 203.4 %all-gather.11.cloned.1.call-start = ((), (), s32[]{:S(2)}) async-start(), calls=%async_computation.16 | async-start | bytes 9469952 | tf_op jit(solution)/shard_map/all_gather | solution.py:459
  62.0 3.7 %collective-permute-start = (f32[32,16,128]{2,1,0:T(8,128)S(1)}, f32[32,16,128]{2,1,0:T(8,128)S(1)}, u32[]{:S(2)}, u32[]{:S(2)}) collective-permute-start(f32[32,16,128]{2,1,0:T(8,128)S(1)} %slice.8), channel_id=1, source_target_pairs={{0,1},{1,0},{2,3},{3,2},{4,5},{5,4},{6,7},{7,6},{8,9},{9,8},{10,11... | collective-permute-start | bytes 786440 | tf_op jit(solution)/shard_map/ppermute | solution.py:514
  103.9 19.8 %all-to-all-start.4 = ((f32[16,4,16,128]{3,2,1,0:T(8,128)}), f32[16,4,16,128]{3,2,1,0:T(8,128)S(1)}, u32[]{:S(2)}, u32[]{:S(2)}) async-start(f32[16,4,16,128]{3,2,1,0:T(8,128)} %get-tuple-element.53), calls=%async_computation.4 | async-start | bytes 1048576 | tf_op jit(solution)/shard_map/all_to_all | solution.py:351
  126.0 5.0 %collective-permute-start.1 = (f32[16,16,128]{2,1,0:T(8,128)S(1)}, f32[16,16,128]{2,1,0:T(8,128)S(1)}, u32[]{:S(2)}, u32[]{:S(2)}) collective-permute-start(f32[16,16,128]{2,1,0:T(8,128)S(1)} %slice.9), channel_id=1, source_target_pairs={{0,1},{1,0},{2,3},{3,2},{4,5},{5,4},{6,7},{7,6},{8,9},{9,8},{10,11... | collective-permute-start | bytes 393224 | tf_op jit(solution)/shard_map/ppermute | solution.py:514
  143.5 12.1 %all-to-all-start.6 = ((f32[16,2,16,128]{3,2,1,0:T(8,128)}), f32[16,2,16,128]{3,2,1,0:T(8,128)S(1)}, u32[]{:S(2)}, u32[]{:S(2)}) async-start(f32[16,2,16,128]{3,2,1,0:T(8,128)} %shard_map.74), calls=%async_computation.6 | async-start | bytes 524288 | tf_op jit(solution)/shard_map/all_to_all | solution.py:351
  175.7 12.6 %all-to-all-start.8 = ((f32[16,1,16,128]{3,2,1,0:T(8,128)}), f32[16,1,16,128]{3,2,1,0:T(8,128)S(1)}, u32[]{:S(2)}, u32[]{:S(2)}) async-start(f32[16,1,16,128]{3,2,1,0:T(8,128)} %shard_map.78), calls=%async_computation.8 | async-start | bytes 262144 | tf_op jit(solution)/shard_map/all_to_all | solution.py:351
  203.8 10.9 %all-to-all-start.10 = ((f32[16,1,16,128]{3,2,1,0:T(8,128)}), f32[16,1,16,128]{3,2,1,0:T(8,128)S(1)}, u32[]{:S(2)}, u32[]{:S(2)}) async-start(f32[16,1,16,128]{3,2,1,0:T(8,128)} %shard_map.82), calls=%async_computation.10 | async-start | bytes 262144 | tf_op jit(solution)/shard_map/all_to_all | solution.py:351
  246.5 1.8 collective-permute-start.2
  251.0 1.3 collective-permute-start.3
Sparse Core Ops, SparseCore 0:
  11.9 50.2 all-gather.8
  64.7 60.1 all-gather.6
  127.4 81.6 all-gather.10

commit v8 on v7

--- a/solution.py
+++ b/solution.py
@@ -11,7 +11,7 @@
 LEAVES = 128
 GATHER_FROM = 2
 CUTS = (2, 5)
-SCRATCH = [pltpu.VMEM((192, 512), jnp.float32)]
+SCRATCH = [pltpu.VMEM((384, 512), jnp.float32)]
 PAIRED = 2
 TOP = 5
 VMEM_LIMIT = 24 * 1024 * 1024
@@ -161,11 +161,11 @@
             y_t = dot3(z_t, (inverse[k, :512], inverse[k, 512:]), ((1,), (0,)))
             limit = sizes[slot]
             y_t = jnp.where(lax.broadcasted_iota(jnp.int32, (64, 512), 1) < limit, y_t, 0.0)
-            scratch[pl.ds(0, 64), :] = y_t
-            lanes = scratch[pl.ds(0, 64), pl.ds(pl.multiple_of(pos[0] // 4 * 128, 128), 128)]
+            scratch[pl.ds(192 * k, 64), :] = y_t
+            lanes = scratch[pl.ds(192 * k, 64), pl.ds(pl.multiple_of(pos[0] // 4 * 128, 128), 128)]
             own = jnp.concatenate([lanes, lanes], 0).T
-            scratch[pl.ds(64, 128), pl.ds(0, 128)] = own
-            own = scratch[pl.ds(pl.multiple_of(64 + pos[0] % 4 * 32, 32), 32), pl.ds(0, 128)]
+            scratch[pl.ds(192 * k + 64, 128), pl.ds(0, 128)] = own
+            own = scratch[pl.ds(pl.multiple_of(192 * k + 64 + pos[0] % 4 * 32, 32), 32), pl.ds(0, 128)]
             sol[k] = fold(own)[0]
             if kept is not None:
                 kept[k] = y_t
@@ -329,7 +329,7 @@
     def call(kernel, scratch, grid, in_specs, out_specs, out_shape, aliases, *args):
         args = [
             pltpu.with_memory_space_constraint(a, pltpu.HBM)
-            if a.size > 1 << 18 and a.dtype == f32
+            if a is natural or (a.size > 1 << 18 and a.dtype == f32)
             else a
             for a in args
         ]
@@ -461,19 +461,19 @@
         updated = []
         given, source = gathered, "z" if whole else "y"
         for start, end in steps:
-            per = 1 if source == "z" else min(2, count)
+            per = min(2, count)
             in_specs = [pl.BlockSpec((16, per, 16, 128), lambda s, *_: (0, s, 0, 0))]
             if source == "t":
                 in_specs = [pl.BlockSpec((per, 64, 512), lambda s, *_: (s, 0, 0))]
             args = [given]
             out_specs, out_shape = [], []
             if source == "z":
-                in_specs.append(pl.BlockSpec((1, 1024, 512), lambda s, *_: (s, 0, 0)))
+                in_specs.append(pl.BlockSpec((per, 1024, 512), lambda s, *_: (s, 0, 0)))
                 args.append(inverse)
-                out_specs.append(pl.BlockSpec((1, 16, 128), lambda s, *_: (s, 0, 0)))
+                out_specs.append(pl.BlockSpec((per, 16, 128), lambda s, *_: (s, 0, 0)))
                 out_shape.append(own)
                 if end < reach:
-                    out_specs.append(pl.BlockSpec((1, 64, 512), lambda s, *_: (s, 0, 0)))
+                    out_specs.append(pl.BlockSpec((per, 64, 512), lambda s, *_: (s, 0, 0)))
                     out_shape.append(jax.ShapeDtypeStruct((count, 64, 512), f32))
             in_specs.append(
                 pl.BlockSpec((per, 1, end, 32, 512), lambda s, *_, b=base // per: (b + s, 0, 0, 0, 0))

time: 274 us -> 273 us (level)
  no operation moved by 1% of the time
where the time goes in v8:
time: 273 us; the launch traced here: 272 us
  blocking collectives  148 us (54%)
  Pallas kernels  59.8 us (22%)
  waiting for transfers between devices  27.1 us (10%)
  starting transfers between devices  22.2 us (8%)
  between operations  13.3 us (5%)
    all_to_all x8, blocking collectives, exchange(): return lax.all_to_all(x, axis, 0, 0, tiled=True)  118 us
    pallas_call x29, Pallas kernels, call(): pl.pallas_call(functools.partial(with_parts, kernel), grid_spec=pltpu.Pre...  59.8 us
    all_to_all x2, blocking collectives, on_device(): lax.all_to_all(joined, 'pcol', 0, 0, tiled=True, axis_index_groups=[[core...  29.6 us
    all_to_all x4, waiting for transfers between devices, exchange(): return lax.all_to_all(x, axis, 0, 0, tiled=True)  23.2 us
    all_to_all x4, starting transfers between devices, exchange(): return lax.all_to_all(x, axis, 0, 0, tiled=True)  14.1 us
    ppermute x2, starting transfers between devices, on_device(): lax.ppermute(results[0][8 * following:], 'pcol', [(i, i ^ 1) for i in ran...  6.58 us
  transfers between devices with their start and end apart: 11, of which 8 were waited for; matrix products, arithmetic and copies ran while one was open for 0% of the time, Pallas kernels for 17%

profile of v8, /device:TPU:1, one launch (start us, length us, event | category | flops | bytes accessed | tf_op | source)
XLA Modules:
  0.0 271.7 jit_solution(2326919746139646478)
XLA Ops:
  11.0 3.4 %shard_map.65 = f32[16,8,16,128]{3,2,1,0:T(8,128)S(1)} custom-call(s32[408]{0:T(512)S(1)} %concatenate.3.refs_0_, f32[19,16,128]{2,1,0:T(8,128)} %bitcast.24, f32[19,1,32,512]{3,2,1,0:T(8,128)} %refs_3_.6), custom_call_target="tpu_custom_call" | custom-call | tf_op jit(solution)/shard_map/pallas_call | solution.py:336
  14.4 23.5 %all_to_all.70.refs_1_ = f32[16,8,16,128]{3,2,1,0:T(8,128)S(1)} all-to-all(f32[16,8,16,128]{3,2,1,0:T(8,128)S(1)} %shard_map.65), channel_id=1, replica_groups=mesh['prow'=16,'pcol'=16] {'prow'}, dimensions={0} | all-to-all | bytes 2097152 | tf_op jit(solution)/shard_map/all_to_all | solution.py:351
  38.7 19.0 %all_to_all.71.refs_1_ = f32[16,8,16,128]{3,2,1,0:T(8,128)S(1)} all-to-all(f32[16,8,16,128]{3,2,1,0:T(8,128)S(1)} %get-tuple-element.52), channel_id=1, replica_groups=mesh['prow'=16,'pcol'=16] {'prow'}, dimensions={0} | all-to-all | bytes 2097152 | tf_op jit(solution)/shard_map/all_to_all | solution.py:351
  57.6 3.5 %shard_map.67.refs_1_ = f32[64,16,128]{2,1,0:T(8,128)S(1)} custom-call(s32[408]{0:T(512)S(1)} %concatenate.3.refs_0_, f32[16,8,16,128]{3,2,1,0:T(8,128)S(1)} %all_to_all.71.refs_1_, f32[19,1,7,32,512]{4,3,2,1,0:T(8,128)} %refs_3_.9), custom_call_target="tpu_custom_call" | custom-call | tf_op jit(solution)/shard_map/pallas_call | solution.py:336
  65.5 19.1 %all_to_all.72.refs_1_ = f32[8,4,16,128]{3,2,1,0:T(8,128)S(1)} all-to-all(f32[8,4,16,128]{3,2,1,0:T(8,128)S(1)} %shard_map.68), channel_id=1, replica_groups={{0,2,4,6,8,10,12,14},{1,3,5,7,9,11,13,15},{16,18,20,22,24,26,28,30},{17..., dimensions={0} | all-to-all | bytes 524288 | tf_op jit(solution)/shard_map/all_to_all | solution.py:526
  86.9 12.3 %all_to_all.73.refs_1_ = f32[16,4,16,128]{3,2,1,0:T(8,128)S(1)} all-to-all(f32[16,4,16,128]{3,2,1,0:T(8,128)S(1)} %shard_map.69), channel_id=1, replica_groups=mesh['prow'=16,'pcol'=16] {'prow'}, dimensions={0} | all-to-all | bytes 1048576 | tf_op jit(solution)/shard_map/all_to_all | solution.py:351
  103.1 3.6 %all-to-all-start.4 = ((f32[16,4,16,128]{3,2,1,0:T(8,128)}), f32[16,4,16,128]{3,2,1,0:T(8,128)S(1)}, u32[]{:S(2)}, u32[]{:S(2)}) async-start(f32[16,4,16,128]{3,2,1,0:T(8,128)} %get-tuple-element.53), calls=%async_computation.4 | async-start | bytes 1048576 | tf_op jit(solution)/shard_map/all_to_all | solution.py:351
  106.7 4.9 %shard_map.71 = (f32[32,16,128]{2,1,0:T(8,128)S(1)}, f32[16,16,128]{2,1,0:T(8,128)S(1)}, f32[16,16,128]{2,1,0:T(8,128)S(1)}, f32[16,16,128]{2,1,0:T(8,128)S(1)},...) custom-call(s32[408]{0:T(512)S(1)} %concatenate.3.refs_0_, f32[16,8,16,128]{3,2,1,0:T(8,128)S(1)} %all_to_all.71.refs_1_, ...), custom_call_target="tpu_custom_call" | custom-call | tf_op jit(solution)/shard_map/pallas_call | solution.py:336
  111.6 11.3 %all-to-all-done.4.refs_1_ = f32[16,4,16,128]{3,2,1,0:T(8,128)S(1)} async-done(((f32[16,4,16,128]{3,2,1,0:T(8,128)}), f32[16,4,16,128]{3,2,1,0:T(8,128)S(1)}, u32[]{:S(2)}, u32[]{:S(2)}) %all-to-all-start.4) | async-done | bytes 524320 | tf_op jit(solution)/shard_map/all_to_all | solution.py:351
  125.1 4.0 %collective-permute-start.1 = (f32[16,16,128]{2,1,0:T(8,128)S(1)}, f32[16,16,128]{2,1,0:T(8,128)S(1)}, u32[]{:S(2)}, u32[]{:S(2)}) collective-permute-start(f32[16,16,128]{2,1,0:T(8,128)S(1)} %slice.9), channel_id=1, source_target_pairs={{0,1},{1,0},{2,3},{3,2},{4,5},{5,4},{6,7},{7,6},{8,9},{9,8},{10,11... | collective-permute-start | bytes 393224 | tf_op jit(solution)/shard_map/ppermute | solution.py:514
  130.7 10.6 %all_to_all.74.refs_1_ = f32[8,2,16,128]{3,2,1,0:T(8,128)S(1)} all-to-all(f32[8,2,16,128]{3,2,1,0:T(8,128)S(1)} %shard_map.73), channel_id=1, replica_groups={{0,2,4,6,8,10,12,14},{1,3,5,7,9,11,13,15},{16,18,20,22,24,26,28,30},{17..., dimensions={0} | all-to-all | bytes 262144 | tf_op jit(solution)/shard_map/all_to_all | solution.py:526
  142.6 3.5 %all-to-all-start.6 = ((f32[16,2,16,128]{3,2,1,0:T(8,128)}), f32[16,2,16,128]{3,2,1,0:T(8,128)S(1)}, u32[]{:S(2)}, u32[]{:S(2)}) async-start(f32[16,2,16,128]{3,2,1,0:T(8,128)} %shard_map.74), calls=%async_computation.6 | async-start | bytes 524288 | tf_op jit(solution)/shard_map/all_to_all | solution.py:351
  146.1 2.9 %shard_map.76 = (f32[16,16,128]{2,1,0:T(8,128)S(1)}, f32[16,16,128]{2,1,0:T(8,128)S(1)}, f32[16,16,128]{2,1,0:T(8,128)S(1)}, f32[16,16,128]{2,1,0:T(8,128)S(1)}, f32[16,16,128]{2,1,0:T(8,128)S(1)}) custom-call(s32[408]{0:T(512)S(1)} %concatenate.3.refs_0_, ...), custom_call_target="tpu_custom_call", output_to_operand_aliasing={{0}: (3, {}), {1}: (4, {}), {2}: (5, {}), {3}: (6, {}), {4}... | custom-call | tf_op jit(solution)/shard_map/pallas_call | solution.py:336
  151.4 3.2 %all-to-all-done.6.refs_1_ = f32[16,2,16,128]{3,2,1,0:T(8,128)S(1)} async-done(((f32[16,2,16,128]{3,2,1,0:T(8,128)}), f32[16,2,16,128]{3,2,1,0:T(8,128)S(1)}, u32[]{:S(2)}, u32[]{:S(2)}) %all-to-all-start.6) | async-done | bytes 262176 | tf_op jit(solution)/shard_map/all_to_all | solution.py:351
  156.9 16.6 %all_to_all.75.refs_1_ = f32[16,1,16,128]{3,2,1,0:T(8,128)S(1)} all-to-all(f32[16,1,16,128]{3,2,1,0:T(8,128)S(1)} %bitcast.13), channel_id=1, replica_groups=mesh['prow'=16,'pcol'=16] {'pcol'}, dimensions={0} | all-to-all | bytes 262144 | tf_op jit(solution)/shard_map/all_to_all | solution.py:351
  174.7 3.5 %all-to-all-start.8 = ((f32[16,1,16,128]{3,2,1,0:T(8,128)}), f32[16,1,16,128]{3,2,1,0:T(8,128)S(1)}, u32[]{:S(2)}, u32[]{:S(2)}) async-start(f32[16,1,16,128]{3,2,1,0:T(8,128)} %shard_map.78), calls=%async_computation.8 | async-start | bytes 262144 | tf_op jit(solution)/shard_map/all_to_all | solution.py:351
  182.3 5.1 %all-to-all-done.8.refs_1_ = f32[16,1,16,128]{3,2,1,0:T(8,128)S(1)} async-done(((f32[16,1,16,128]{3,2,1,0:T(8,128)}), f32[16,1,16,128]{3,2,1,0:T(8,128)S(1)}, u32[]{:S(2)}, u32[]{:S(2)}) %all-to-all-start.8) | async-done | bytes 131104 | tf_op jit(solution)/shard_map/all_to_all | solution.py:351
  189.3 12.2 %all_to_all.76.refs_1_ = f32[16,1,16,128]{3,2,1,0:T(8,128)S(1)} all-to-all(f32[16,1,16,128]{3,2,1,0:T(8,128)S(1)} %bitcast.12), channel_id=1, replica_groups=mesh['prow'=16,'pcol'=16] {'pcol'}, dimensions={0} | all-to-all | bytes 262144 | tf_op jit(solution)/shard_map/all_to_all | solution.py:351
  202.7 3.5 %all-to-all-start.10 = ((f32[16,1,16,128]{3,2,1,0:T(8,128)}), f32[16,1,16,128]{3,2,1,0:T(8,128)S(1)}, u32[]{:S(2)}, u32[]{:S(2)}) async-start(f32[16,1,16,128]{3,2,1,0:T(8,128)} %shard_map.82), calls=%async_computation.10 | async-start | bytes 262144 | tf_op jit(solution)/shard_map/all_to_all | solution.py:351
  210.0 3.6 %all-to-all-done.10.refs_1_ = f32[16,1,16,128]{3,2,1,0:T(8,128)S(1)} async-done(((f32[16,1,16,128]{3,2,1,0:T(8,128)}), f32[16,1,16,128]{3,2,1,0:T(8,128)S(1)}, u32[]{:S(2)}, u32[]{:S(2)}) %all-to-all-start.10) | async-done | bytes 131104 | tf_op jit(solution)/shard_map/all_to_all | solution.py:351
  216.6 13.9 %all_to_all.77.refs_1_ = f32[16,8,256]{2,1,0:T(8,128)S(1)} all-to-all(f32[16,8,256]{2,1,0:T(8,128)S(1)} %shard_map.86), channel_id=1, replica_groups=mesh['prow'=16,'pcol'=16] {'pcol'}, dimensions={0} | all-to-all | bytes 262144 | tf_op jit(solution)/shard_map/all_to_all | solution.py:351
  231.1 10.0 %all_to_all.78.refs_1_ = f32[16,8,256]{2,1,0:T(8,128)S(1)} all-to-all(f32[16,8,256]{2,1,0:T(8,128)S(1)} %shard_map.87), channel_id=1, replica_groups=mesh['prow'=16,'pcol'=16] {'prow'}, dimensions={0} | all-to-all | bytes 262144 | tf_op jit(solution)/shard_map/all_to_all | solution.py:351
  241.1 4.3 %shard_map.89 = (f32[16,8,128]{2,1,0:T(8,128)S(1)}, f32[3,8,512]{2,1,0:T(8,128)S(1)}) custom-call(s32[408]{0:T(512)S(1)} %concatenate.3.refs_0_, f32[16,8,256]{2,1,0:T(8,128)S(1)} %all_to_all.78.refs_1_, f32[16,17,32,256]{3,2,1,0:T(8,128)} %bitcast.14), custom_call_target="tpu_custom_call" | custom-call | tf_op jit(solution)/shard_map/pallas_call | solution.py:336
  253.1 10.6 %all_to_all.79.refs_1_ = f32[16,8,128]{2,1,0:T(8,128)S(1)} all-to-all(f32[16,8,128]{2,1,0:T(8,128)S(1)} %shard_map.91), channel_id=1, replica_groups=mesh['prow'=16,'pcol'=16] {'pcol'}, dimensions={0} | all-to-all | bytes 131072 | tf_op jit(solution)/shard_map/all_to_all | solution.py:351
  (45 shorter events, 50.5 us)
Async XLA Ops:
  6.5 94.1 %all-gather.9.cloned.1.call-start = ((), (), s32[]{:S(2)}) async-start(), calls=%async_computation.15 | async-start | bytes 6684672 | tf_op jit(solution)/shard_map/all_gather | solution.py:384
  11.0 138.1 %all-gather.7.cloned.1.call-start = ((), (), s32[]{:S(2)}) async-start(), calls=%async_computation.14 | async-start | bytes 4456448 | tf_op jit(solution)/shard_map/all_gather | solution.py:437
  37.9 203.2 %all-gather.11.cloned.1.call-start = ((), (), s32[]{:S(2)}) async-start(), calls=%async_computation.16 | async-start | bytes 9469952 | tf_op jit(solution)/shard_map/all_gather | solution.py:459
  61.1 3.7 %collective-permute-start = (f32[32,16,128]{2,1,0:T(8,128)S(1)}, f32[32,16,128]{2,1,0:T(8,128)S(1)}, u32[]{:S(2)}, u32[]{:S(2)}) collective-permute-start(f32[32,16,128]{2,1,0:T(8,128)S(1)} %slice.8), channel_id=1, source_target_pairs={{0,1},{1,0},{2,3},{3,2},{4,5},{5,4},{6,7},{7,6},{8,9},{9,8},{10,11... | collective-permute-start | bytes 786440 | tf_op jit(solution)/shard_map/ppermute | solution.py:514
  103.1 19.8 %all-to-all-start.4 = ((f32[16,4,16,128]{3,2,1,0:T(8,128)}), f32[16,4,16,128]{3,2,1,0:T(8,128)S(1)}, u32[]{:S(2)}, u32[]{:S(2)}) async-start(f32[16,4,16,128]{3,2,1,0:T(8,128)} %get-tuple-element.53), calls=%async_computation.4 | async-start | bytes 1048576 | tf_op jit(solution)/shard_map/all_to_all | solution.py:351
  125.1 5.0 %collective-permute-start.1 = (f32[16,16,128]{2,1,0:T(8,128)S(1)}, f32[16,16,128]{2,1,0:T(8,128)S(1)}, u32[]{:S(2)}, u32[]{:S(2)}) collective-permute-start(f32[16,16,128]{2,1,0:T(8,128)S(1)} %slice.9), channel_id=1, source_target_pairs={{0,1},{1,0},{2,3},{3,2},{4,5},{5,4},{6,7},{7,6},{8,9},{9,8},{10,11... | collective-permute-start | bytes 393224 | tf_op jit(solution)/shard_map/ppermute | solution.py:514
  142.6 11.9 %all-to-all-start.6 = ((f32[16,2,16,128]{3,2,1,0:T(8,128)}), f32[16,2,16,128]{3,2,1,0:T(8,128)S(1)}, u32[]{:S(2)}, u32[]{:S(2)}) async-start(f32[16,2,16,128]{3,2,1,0:T(8,128)} %shard_map.74), calls=%async_computation.6 | async-start | bytes 524288 | tf_op jit(solution)/shard_map/all_to_all | solution.py:351
  174.7 12.7 %all-to-all-start.8 = ((f32[16,1,16,128]{3,2,1,0:T(8,128)}), f32[16,1,16,128]{3,2,1,0:T(8,128)S(1)}, u32[]{:S(2)}, u32[]{:S(2)}) async-start(f32[16,1,16,128]{3,2,1,0:T(8,128)} %shard_map.78), calls=%async_computation.8 | async-start | bytes 262144 | tf_op jit(solution)/shard_map/all_to_all | solution.py:351
  202.7 10.9 %all-to-all-start.10 = ((f32[16,1,16,128]{3,2,1,0:T(8,128)}), f32[16,1,16,128]{3,2,1,0:T(8,128)S(1)}, u32[]{:S(2)}, u32[]{:S(2)}) async-start(f32[16,1,16,128]{3,2,1,0:T(8,128)} %shard_map.82), calls=%async_computation.10 | async-start | bytes 262144 | tf_op jit(solution)/shard_map/all_to_all | solution.py:351
  245.4 1.8 collective-permute-start.2
  249.9 1.3 collective-permute-start.3
Sparse Core Ops, SparseCore 0:
  11.1 50.2 all-gather.8
  63.9 60.1 all-gather.6
  126.5 81.6 all-gather.10

commit v9 on v8

--- a/solution.py
+++ b/solution.py
@@ -203,6 +203,10 @@
     both[0, :512], both[0, 512:] = split(rows)
 
 
+def near_kernel(pos, parent, pattern, sizes, block, out):
+    out[0] = block[:, 0].reshape(512, 256)
+
+
 def join_kernel(pos, parent, pattern, sizes, here, there, out):
     out[...] = (here[...] + there[...]).reshape(out.shape)
 
@@ -296,7 +300,7 @@
 
 def middle_kernel(pos, parent, pattern, sizes, left, other, before, block, out, after):
     def matrix(i):
-        return block[:, i].reshape(512, 256)
+        return block[i]
 
     solved = [dot3(left[k] + other[k], matrix(2 * k), ((1,), (0,))) for k in range(2)]
     update = [dot3(solved[k], matrix(2 * k + 1), ((1,), (1,))) for k in range(2)]
@@ -307,7 +311,7 @@
 
 
 def root_kernel(pos, parent, pattern, sizes, left, other, before, block, out):
-    solved = dot3(left[...] + other[...], block[:, 0].reshape(512, 256), ((1,), (0,)))
+    solved = dot3(left[...] + other[...], block[0], ((1,), (0,)))
     out[...] = before[...]
     out[0] = place(before[0], solved, 2, pos)
 
@@ -326,10 +330,12 @@
     scalars = jnp.concatenate([pos, parent, pattern.reshape(-1), node_sizes.reshape(-1)])
     slot_counts = [max(1, n // 16) for n in NODES]
     bases = [sum(slot_counts[:h]) for h in range(LEVELS)]
+    near = []
+
     def call(kernel, scratch, grid, in_specs, out_specs, out_shape, aliases, *args):
         args = [
             pltpu.with_memory_space_constraint(a, pltpu.HBM)
-            if a is natural or (a.size > 1 << 18 and a.dtype == f32)
+            if a is natural or (a.size > 1 << 18 and a.dtype == f32 and not any(a is b for b in near))
             else a
             for a in args
         ]
@@ -549,9 +555,19 @@
     )
     total = call(sum_kernel, [], (1,), [sides], sides, sides_shape, {}, exchange(turned, "pcol"))
     gathered = exchange(total, "prow")
-    def halves_from(start, n):
-        return [pl.BlockSpec((16, n, 32, 256), lambda s, *_: (0, start // n + s, 0, 0))]
-
+    top, _ = lax.optimization_barrier((top, total))
+    upper = call(
+        near_kernel,
+        [],
+        (5,),
+        [pl.BlockSpec((16, 1, 32, 256), lambda s, *_: (0, 12 + s, 0, 0))],
+        pl.BlockSpec((1, 512, 256), lambda s, *_: (s, 0, 0)),
+        jax.ShapeDtypeStruct((5, 512, 256), f32),
+        {},
+        top,
+    )
+    gathered, upper = lax.optimization_barrier((gathered, upper))
+    near.append(upper)
     def whole_of(*shape):
         return pl.BlockSpec(shape, lambda *_: (0,) * len(shape)), jax.ShapeDtypeStruct(shape, f32)
 
@@ -565,7 +581,7 @@
         low_kernel,
         [pltpu.VMEM((4, 8, 512), f32)],
         (2,),
-        [sides] + halves_from(0, 6),
+        [sides, pl.BlockSpec((16, 6, 32, 256), lambda s, *_: (0, s, 0, 0))],
         [found, three],
         [found_shape, three_shape],
         {},
@@ -576,27 +592,27 @@
         middle_kernel,
         [],
         (1,),
-        [three, three, found] + halves_from(12, 4),
+        [three, three, found, pl.BlockSpec((4, 512, 256), lambda *_: (0, 0, 0))],
         [found, single],
         [found_shape, single_shape],
         {},
         left,
         other_core(left),
         solved,
-        top,
+        upper,
     )
     solved = call(
         root_kernel,
         [],
         (1,),
-        [single, single, found] + halves_from(16, 1),
+        [single, single, found, pl.BlockSpec((1, 512, 256), lambda *_: (4, 0, 0))],
         found,
         found_shape,
         {},
         left,
         other_core(left),
         solved,
-        top,
+        upper,
     )
     out = call(
         last_kernel,

time: 273 us -> 272 us (level)
  blocking collectives: 148 us -> 138 us
  starting transfers between devices: 22.2 us -> 25.7 us
  waiting for transfers between devices: 27.1 us -> 30.6 us
    all_to_all x8 -> x7, blocking collectives: 118 us -> 108 us  [exchange(): return lax.all_to_all(x, axis, 0, 0, tiled=True)]
    all_to_all x4 -> x5, starting transfers between devices: 14.1 us -> 17.7 us  [exchange(): return lax.all_to_all(x, axis, 0, 0, tiled=True)]
    all_to_all x4 -> x5, waiting for transfers between devices: 23.2 us -> 26.6 us  [exchange(): return lax.all_to_all(x, axis, 0, 0, tiled=True)]
    pallas_call x29 -> x30, Pallas kernels: 59.8 us -> 61.7 us  [call(): pl.pallas_call(functools.partial(with_parts, kernel), grid_spec=pltpu.Pre...]
  transfers between devices with their start and end apart: 11 -> 12, of which waited for: 8 -> 9; matrix products, arithmetic and copies ran while one was open for 0% -> 0% of each run, Pallas kernels for 17% -> 19%
where the time goes in v9:
time: 272 us; the launch traced here: 271 us
  blocking collectives  138 us (51%)
  Pallas kernels  61.7 us (23%)
  waiting for transfers between devices  30.6 us (11%)
  starting transfers between devices  25.7 us (9%)
  between operations  13.3 us (5%)
    all_to_all x7, blocking collectives, exchange(): return lax.all_to_all(x, axis, 0, 0, tiled=True)  108 us
    pallas_call x30, Pallas kernels, call(): pl.pallas_call(functools.partial(with_parts, kernel), grid_spec=pltpu.Pre...  61.7 us
    all_to_all x2, blocking collectives, on_device(): lax.all_to_all(joined, 'pcol', 0, 0, tiled=True, axis_index_groups=[[core...  29.6 us
    all_to_all x5, waiting for transfers between devices, exchange(): return lax.all_to_all(x, axis, 0, 0, tiled=True)  26.6 us
    all_to_all x5, starting transfers between devices, exchange(): return lax.all_to_all(x, axis, 0, 0, tiled=True)  17.7 us
    ppermute x2, starting transfers between devices, on_device(): lax.ppermute(results[0][8 * following:], 'pcol', [(i, i ^ 1) for i in ran...  6.6 us
  transfers between devices with their start and end apart: 12, of which 9 were waited for; matrix products, arithmetic and copies ran while one was open for 0% of the time, Pallas kernels for 19%

profile of v9, /device:TPU:1, one launch (start us, length us, event | category | flops | bytes accessed | tf_op | source)
XLA Modules:
  0.0 270.6 jit_solution(17861076284736163271)
XLA Ops:
  11.0 3.4 %shard_map.65 = f32[16,8,16,128]{3,2,1,0:T(8,128)S(1)} custom-call(s32[408]{0:T(512)S(1)} %concatenate.3.refs_0_, f32[19,16,128]{2,1,0:T(8,128)} %bitcast.23, f32[19,1,32,512]{3,2,1,0:T(8,128)} %refs_3_.6), custom_call_target="tpu_custom_call" | custom-call | tf_op jit(solution)/shard_map/pallas_call | solution.py:342
  14.4 23.5 %all_to_all.70.refs_1_ = f32[16,8,16,128]{3,2,1,0:T(8,128)S(1)} all-to-all(f32[16,8,16,128]{3,2,1,0:T(8,128)S(1)} %shard_map.65), channel_id=1, replica_groups=mesh['prow'=16,'pcol'=16] {'prow'}, dimensions={0} | all-to-all | bytes 2097152 | tf_op jit(solution)/shard_map/all_to_all | solution.py:357
  38.7 19.0 %all_to_all.71.refs_1_ = f32[16,8,16,128]{3,2,1,0:T(8,128)S(1)} all-to-all(f32[16,8,16,128]{3,2,1,0:T(8,128)S(1)} %get-tuple-element.55), channel_id=1, replica_groups=mesh['prow'=16,'pcol'=16] {'prow'}, dimensions={0} | all-to-all | bytes 2097152 | tf_op jit(solution)/shard_map/all_to_all | solution.py:357
  57.6 3.5 %shard_map.67.refs_1_ = f32[64,16,128]{2,1,0:T(8,128)S(1)} custom-call(s32[408]{0:T(512)S(1)} %concatenate.3.refs_0_, f32[16,8,16,128]{3,2,1,0:T(8,128)S(1)} %all_to_all.71.refs_1_, f32[19,1,7,32,512]{4,3,2,1,0:T(8,128)} %refs_3_.9), custom_call_target="tpu_custom_call" | custom-call | tf_op jit(solution)/shard_map/pallas_call | solution.py:342
  65.5 19.1 %all_to_all.72.refs_1_ = f32[8,4,16,128]{3,2,1,0:T(8,128)S(1)} all-to-all(f32[8,4,16,128]{3,2,1,0:T(8,128)S(1)} %shard_map.68), channel_id=1, replica_groups={{0,2,4,6,8,10,12,14},{1,3,5,7,9,11,13,15},{16,18,20,22,24,26,28,30},{17..., dimensions={0} | all-to-all | bytes 524288 | tf_op jit(solution)/shard_map/all_to_all | solution.py:532
  86.9 12.3 %all_to_all.73.refs_1_ = f32[16,4,16,128]{3,2,1,0:T(8,128)S(1)} all-to-all(f32[16,4,16,128]{3,2,1,0:T(8,128)S(1)} %shard_map.69), channel_id=1, replica_groups=mesh['prow'=16,'pcol'=16] {'prow'}, dimensions={0} | all-to-all | bytes 1048576 | tf_op jit(solution)/shard_map/all_to_all | solution.py:357
  103.1 3.6 %all-to-all-start.4 = ((f32[16,4,16,128]{3,2,1,0:T(8,128)}), f32[16,4,16,128]{3,2,1,0:T(8,128)S(1)}, u32[]{:S(2)}, u32[]{:S(2)}) async-start(f32[16,4,16,128]{3,2,1,0:T(8,128)} %get-tuple-element.56), calls=%async_computation.4 | async-start | bytes 1048576 | tf_op jit(solution)/shard_map/all_to_all | solution.py:357
  106.7 4.9 %shard_map.71 = (f32[32,16,128]{2,1,0:T(8,128)S(1)}, f32[16,16,128]{2,1,0:T(8,128)S(1)}, f32[16,16,128]{2,1,0:T(8,128)S(1)}, f32[16,16,128]{2,1,0:T(8,128)S(1)},...) custom-call(s32[408]{0:T(512)S(1)} %concatenate.3.refs_0_, f32[16,8,16,128]{3,2,1,0:T(8,128)S(1)} %all_to_all.71.refs_1_, ...), custom_call_target="tpu_custom_call" | custom-call | tf_op jit(solution)/shard_map/pallas_call | solution.py:342
  111.6 11.3 %all-to-all-done.4.refs_1_ = f32[16,4,16,128]{3,2,1,0:T(8,128)S(1)} async-done(((f32[16,4,16,128]{3,2,1,0:T(8,128)}), f32[16,4,16,128]{3,2,1,0:T(8,128)S(1)}, u32[]{:S(2)}, u32[]{:S(2)}) %all-to-all-start.4) | async-done | bytes 524320 | tf_op jit(solution)/shard_map/all_to_all | solution.py:357
  125.1 4.0 %collective-permute-start.1 = (f32[16,16,128]{2,1,0:T(8,128)S(1)}, f32[16,16,128]{2,1,0:T(8,128)S(1)}, u32[]{:S(2)}, u32[]{:S(2)}) collective-permute-start(f32[16,16,128]{2,1,0:T(8,128)S(1)} %slice.9), channel_id=1, source_target_pairs={{0,1},{1,0},{2,3},{3,2},{4,5},{5,4},{6,7},{7,6},{8,9},{9,8},{10,11... | collective-permute-start | bytes 393224 | tf_op jit(solution)/shard_map/ppermute | solution.py:520
  130.7 10.6 %all_to_all.74.refs_1_ = f32[8,2,16,128]{3,2,1,0:T(8,128)S(1)} all-to-all(f32[8,2,16,128]{3,2,1,0:T(8,128)S(1)} %shard_map.73), channel_id=1, replica_groups={{0,2,4,6,8,10,12,14},{1,3,5,7,9,11,13,15},{16,18,20,22,24,26,28,30},{17..., dimensions={0} | all-to-all | bytes 262144 | tf_op jit(solution)/shard_map/all_to_all | solution.py:532
  142.6 3.5 %all-to-all-start.6 = ((f32[16,2,16,128]{3,2,1,0:T(8,128)}), f32[16,2,16,128]{3,2,1,0:T(8,128)S(1)}, u32[]{:S(2)}, u32[]{:S(2)}) async-start(f32[16,2,16,128]{3,2,1,0:T(8,128)} %shard_map.74), calls=%async_computation.6 | async-start | bytes 524288 | tf_op jit(solution)/shard_map/all_to_all | solution.py:357
  156.9 16.6 %all_to_all.75.refs_1_ = f32[16,1,16,128]{3,2,1,0:T(8,128)S(1)} all-to-all(f32[16,1,16,128]{3,2,1,0:T(8,128)S(1)} %bitcast.13), channel_id=1, replica_groups=mesh['prow'=16,'pcol'=16] {'pcol'}, dimensions={0} | all-to-all | bytes 262144 | tf_op jit(solution)/shard_map/all_to_all | solution.py:357
  174.7 3.5 %all-to-all-start.8 = ((f32[16,1,16,128]{3,2,1,0:T(8,128)}), f32[16,1,16,128]{3,2,1,0:T(8,128)S(1)}, u32[]{:S(2)}, u32[]{:S(2)}) async-start(f32[16,1,16,128]{3,2,1,0:T(8,128)} %shard_map.78), calls=%async_computation.8 | async-start | bytes 262144 | tf_op jit(solution)/shard_map/all_to_all | solution.py:357
  182.3 5.0 %all-to-all-done.8.refs_1_ = f32[16,1,16,128]{3,2,1,0:T(8,128)S(1)} async-done(((f32[16,1,16,128]{3,2,1,0:T(8,128)}), f32[16,1,16,128]{3,2,1,0:T(8,128)S(1)}, u32[]{:S(2)}, u32[]{:S(2)}) %all-to-all-start.8) | async-done | bytes 131104 | tf_op jit(solution)/shard_map/all_to_all | solution.py:357
  189.3 12.2 %all_to_all.76.refs_1_ = f32[16,1,16,128]{3,2,1,0:T(8,128)S(1)} all-to-all(f32[16,1,16,128]{3,2,1,0:T(8,128)S(1)} %bitcast.12), channel_id=1, replica_groups=mesh['prow'=16,'pcol'=16] {'pcol'}, dimensions={0} | all-to-all | bytes 262144 | tf_op jit(solution)/shard_map/all_to_all | solution.py:357
  202.7 3.5 %all-to-all-start.10 = ((f32[16,1,16,128]{3,2,1,0:T(8,128)}), f32[16,1,16,128]{3,2,1,0:T(8,128)S(1)}, u32[]{:S(2)}, u32[]{:S(2)}) async-start(f32[16,1,16,128]{3,2,1,0:T(8,128)} %shard_map.82), calls=%async_computation.10 | async-start | bytes 262144 | tf_op jit(solution)/shard_map/all_to_all | solution.py:357
  210.0 3.6 %all-to-all-done.10.refs_1_ = f32[16,1,16,128]{3,2,1,0:T(8,128)S(1)} async-done(((f32[16,1,16,128]{3,2,1,0:T(8,128)}), f32[16,1,16,128]{3,2,1,0:T(8,128)S(1)}, u32[]{:S(2)}, u32[]{:S(2)}) %all-to-all-start.10) | async-done | bytes 131104 | tf_op jit(solution)/shard_map/all_to_all | solution.py:357
  216.6 13.9 %all_to_all.77.refs_1_ = f32[16,8,256]{2,1,0:T(8,128)S(1)} all-to-all(f32[16,8,256]{2,1,0:T(8,128)S(1)} %shard_map.86), channel_id=1, replica_groups=mesh['prow'=16,'pcol'=16] {'pcol'}, dimensions={0} | all-to-all | bytes 262144 | tf_op jit(solution)/shard_map/all_to_all | solution.py:357
  231.8 3.5 %all-to-all-start.12 = ((f32[16,8,256]{2,1,0:T(8,128)}), f32[16,8,256]{2,1,0:T(8,128)S(1)}, u32[]{:S(2)}, u32[]{:S(2)}) async-start(f32[16,8,256]{2,1,0:T(8,128)} %shard_map.87), calls=%async_computation.12 | async-start | bytes 262144 | tf_op jit(solution)/shard_map/all_to_all | solution.py:357
  235.3 3.9 %shard_map.89.refs_4_ = f32[5,512,256]{2,1,0:T(8,128)S(1)} custom-call(s32[408]{0:T(512)S(1)} %concatenate.3.refs_0_, f32[16,17,32,256]{3,2,1,0:T(8,128)} %bitcast.20), custom_call_target="tpu_custom_call" | custom-call | tf_op jit(solution)/shard_map/pallas_call | solution.py:342
  239.3 3.4 %all-to-all-done.12.refs_1_ = f32[16,8,256]{2,1,0:T(8,128)S(1)} async-done(((f32[16,8,256]{2,1,0:T(8,128)}), f32[16,8,256]{2,1,0:T(8,128)S(1)}, u32[]{:S(2)}, u32[]{:S(2)}) %all-to-all-start.12) | async-done | bytes 131104 | tf_op jit(solution)/shard_map/all_to_all | solution.py:357
  242.7 4.3 %shard_map.90 = (f32[16,8,128]{2,1,0:T(8,128)S(1)}, f32[3,8,512]{2,1,0:T(8,128)S(1)}) custom-call(s32[408]{0:T(512)S(1)} %concatenate.3.refs_0_, f32[16,8,256]{2,1,0:T(8,128)S(1)} %all-to-all-done.12.refs_1_, f32[16,17,32,256]{3,2,1,0:T(8,128)} %bitcast.21), custom_call_target="tpu_custom_call" | custom-call | tf_op jit(solution)/shard_map/pallas_call | solution.py:342
  252.0 10.6 %all_to_all.78.refs_1_ = f32[16,8,128]{2,1,0:T(8,128)S(1)} all-to-all(f32[16,8,128]{2,1,0:T(8,128)S(1)} %shard_map.92), channel_id=1, replica_groups=mesh['prow'=16,'pcol'=16] {'pcol'}, dimensions={0} | all-to-all | bytes 131072 | tf_op jit(solution)/shard_map/all_to_all | solution.py:357
  (47 shorter events, 54.5 us)
Async XLA Ops:
  6.5 94.1 %all-gather.9.cloned.1.call-start = ((), (), s32[]{:S(2)}) async-start(), calls=%async_computation.15 | async-start | bytes 6684672 | tf_op jit(solution)/shard_map/all_gather | solution.py:390
  11.0 138.1 %all-gather.7.cloned.1.call-start = ((), (), s32[]{:S(2)}) async-start(), calls=%async_computation.14 | async-start | bytes 4456448 | tf_op jit(solution)/shard_map/all_gather | solution.py:443
  37.9 197.4 %all-gather.11.cloned.1.call-start = ((), (), s32[]{:S(2)}) async-start(), calls=%async_computation.16 | async-start | bytes 9469952 | tf_op jit(solution)/shard_map/all_gather | solution.py:465
  61.1 3.7 %collective-permute-start = (f32[32,16,128]{2,1,0:T(8,128)S(1)}, f32[32,16,128]{2,1,0:T(8,128)S(1)}, u32[]{:S(2)}, u32[]{:S(2)}) collective-permute-start(f32[32,16,128]{2,1,0:T(8,128)S(1)} %slice.8), channel_id=1, source_target_pairs={{0,1},{1,0},{2,3},{3,2},{4,5},{5,4},{6,7},{7,6},{8,9},{9,8},{10,11... | collective-permute-start | bytes 786440 | tf_op jit(solution)/shard_map/ppermute | solution.py:520
  103.1 19.8 %all-to-all-start.4 = ((f32[16,4,16,128]{3,2,1,0:T(8,128)}), f32[16,4,16,128]{3,2,1,0:T(8,128)S(1)}, u32[]{:S(2)}, u32[]{:S(2)}) async-start(f32[16,4,16,128]{3,2,1,0:T(8,128)} %get-tuple-element.56), calls=%async_computation.4 | async-start | bytes 1048576 | tf_op jit(solution)/shard_map/all_to_all | solution.py:357
  125.1 5.0 %collective-permute-start.1 = (f32[16,16,128]{2,1,0:T(8,128)S(1)}, f32[16,16,128]{2,1,0:T(8,128)S(1)}, u32[]{:S(2)}, u32[]{:S(2)}) collective-permute-start(f32[16,16,128]{2,1,0:T(8,128)S(1)} %slice.9), channel_id=1, source_target_pairs={{0,1},{1,0},{2,3},{3,2},{4,5},{5,4},{6,7},{7,6},{8,9},{9,8},{10,11... | collective-permute-start | bytes 393224 | tf_op jit(solution)/shard_map/ppermute | solution.py:520
  142.6 11.9 %all-to-all-start.6 = ((f32[16,2,16,128]{3,2,1,0:T(8,128)}), f32[16,2,16,128]{3,2,1,0:T(8,128)S(1)}, u32[]{:S(2)}, u32[]{:S(2)}) async-start(f32[16,2,16,128]{3,2,1,0:T(8,128)} %shard_map.74), calls=%async_computation.6 | async-start | bytes 524288 | tf_op jit(solution)/shard_map/all_to_all | solution.py:357
  174.7 12.6 %all-to-all-start.8 = ((f32[16,1,16,128]{3,2,1,0:T(8,128)}), f32[16,1,16,128]{3,2,1,0:T(8,128)S(1)}, u32[]{:S(2)}, u32[]{:S(2)}) async-start(f32[16,1,16,128]{3,2,1,0:T(8,128)} %shard_map.78), calls=%async_computation.8 | async-start | bytes 262144 | tf_op jit(solution)/shard_map/all_to_all | solution.py:357
  202.7 10.9 %all-to-all-start.10 = ((f32[16,1,16,128]{3,2,1,0:T(8,128)}), f32[16,1,16,128]{3,2,1,0:T(8,128)S(1)}, u32[]{:S(2)}, u32[]{:S(2)}) async-start(f32[16,1,16,128]{3,2,1,0:T(8,128)} %shard_map.82), calls=%async_computation.10 | async-start | bytes 262144 | tf_op jit(solution)/shard_map/all_to_all | solution.py:357
  231.8 10.9 %all-to-all-start.12 = ((f32[16,8,256]{2,1,0:T(8,128)}), f32[16,8,256]{2,1,0:T(8,128)S(1)}, u32[]{:S(2)}, u32[]{:S(2)}) async-start(f32[16,8,256]{2,1,0:T(8,128)} %shard_map.87), calls=%async_computation.12 | async-start | bytes 262144 | tf_op jit(solution)/shard_map/all_to_all | solution.py:357
  247.0 1.8 collective-permute-start.2
  249.8 1.3 collective-permute-start.3
Sparse Core Ops, SparseCore 0:
  11.1 50.2 all-gather.8
  63.9 60.1 all-gather.6
  126.5 81.6 all-gather.10

commit v10 on v9

--- a/solution.py
+++ b/solution.py
@@ -234,6 +234,12 @@
     for c in range(2):
         out[12 + 2 * c : 14 + 2 * c] = middle[c]
     out[16:17] = high[0]
+
+
+def solved_and_choose_kernel(height, slots, slot_base, pos, parent, pattern, sizes, recv, *refs):
+    *blocks, out, sol, chosen = refs
+    solved_kernel(height, slots, slot_base, pos, parent, pattern, sizes, recv, out, sol)
+    choose_kernel(pos, parent, pattern, sizes, *blocks, chosen)
 
 
 def turn_kernel(pos, parent, pattern, sizes, p5, p6, p7, rhs, out, scratch):
@@ -441,28 +447,29 @@
             if height == 0:
                 wholes, parts = lax.optimization_barrier((wholes, parts))
                 inverses = [(lo, lax.all_gather(part, "prow", axis=0)) for lo, part in zip(cuts[:-1], wholes)]
-            y, sol = call(
-                functools.partial(solved_kernel, *info), [], (1,), [every], [every, every_own], [piece, own], {}, parts
-            )
+            if height == 1:
+                halves = [(4, 3, 0, 1), (2, 2, 0, 0), (1, 1, 0, 2)]
+                y, sol, chosen = call(
+                    functools.partial(solved_and_choose_kernel, *info),
+                    [],
+                    (1,),
+                    [every]
+                    + [
+                        pl.BlockSpec((m, n, 32, 256), lambda _, info, a=a, b=b: (a, b, 0, info[1] % 2))
+                        for m, n, a, b in halves
+                    ],
+                    [every, every_own, pl.BlockSpec((17, 32, 256), lambda *_: (0, 0, 0))],
+                    [piece, own, jax.ShapeDtypeStruct((17, 32, 256), f32)],
+                    {},
+                    parts,
+                    *[top] * 3,
+                )
+                top = lax.all_gather(chosen, "prow", axis=0)
+            else:
+                kernel = functools.partial(solved_kernel, *info)
+                y, sol = call(kernel, [], (1,), [every], [every, every_own], [piece, own], {}, parts)
             outputs.append(sol)
             gathered = exchange(y, "prow")
-        if height == 1:
-            chosen_from, _ = lax.optimization_barrier((top, y))
-            halves = [(4, 3, 0, 1), (2, 2, 0, 0), (1, 1, 0, 2)]
-            chosen = call(
-                choose_kernel,
-                [],
-                (1,),
-                [
-                    pl.BlockSpec((m, n, 32, 256), lambda _, info, a=a, b=b: (a, b, 0, info[1] % 2))
-                    for m, n, a, b in halves
-                ],
-                pl.BlockSpec((17, 32, 256), lambda *_: (0, 0, 0)),
-                jax.ShapeDtypeStruct((17, 32, 256), f32),
-                {},
-                *[chosen_from] * 3,
-            )
-            top = lax.all_gather(chosen, "prow", axis=0)
         steps = [(0, 1), (1, reach)] if height + 1 < TOP else [(0, reach)]
         updated = []
         given, source = gathered, "z" if whole else "y"

time: 272 us -> 271 us (level)
    pallas_call x30 -> x29, Pallas kernels: 61.7 us -> 60.6 us  [call(): pl.pallas_call(functools.partial(with_parts, kernel), grid_spec=pltpu.Pre...]
where the time goes in v10:
time: 271 us; the launch traced here: 269 us
  blocking collectives  136 us (50%)
  Pallas kernels  60.6 us (22%)
  waiting for transfers between devices  32.2 us (12%)
  starting transfers between devices  25.8 us (10%)
  between operations  13.3 us (5%)
    all_to_all x7, blocking collectives, exchange(): return lax.all_to_all(x, axis, 0, 0, tiled=True)  106 us
    pallas_call x29, Pallas kernels, call(): pl.pallas_call(functools.partial(with_parts, kernel), grid_spec=pltpu.Pre...  60.6 us
    all_to_all x2, blocking collectives, on_device(): lax.all_to_all(joined, 'pcol', 0, 0, tiled=True, axis_index_groups=[[core...  29.8 us
    all_to_all x5, waiting for transfers between devices, exchange(): return lax.all_to_all(x, axis, 0, 0, tiled=True)  28.3 us
    all_to_all x5, starting transfers between devices, exchange(): return lax.all_to_all(x, axis, 0, 0, tiled=True)  17.7 us
    ppermute x2, starting transfers between devices, on_device(): lax.ppermute(results[0][8 * following:], 'pcol', [(i, i ^ 1) for i in ran...  6.66 us
  transfers between devices with their start and end apart: 12, of which 9 were waited for; matrix products, arithmetic and copies ran while one was open for 0% of the time, Pallas kernels for 19%

profile of v10, /device:TPU:1, one launch (start us, length us, event | category | flops | bytes accessed | tf_op | source)
XLA Modules:
  0.0 269.4 jit_solution(18036199558746992998)
XLA Ops:
  14.4 23.5 %all_to_all.70.refs_1_ = f32[16,8,16,128]{3,2,1,0:T(8,128)S(1)} all-to-all(f32[16,8,16,128]{3,2,1,0:T(8,128)S(1)} %shard_map.65), channel_id=1, replica_groups=mesh['prow'=16,'pcol'=16] {'prow'}, dimensions={0} | all-to-all | bytes 2097152 | tf_op jit(solution)/shard_map/all_to_all | solution.py:363
  38.7 18.9 %all_to_all.71.refs_1_ = f32[16,8,16,128]{3,2,1,0:T(8,128)S(1)} all-to-all(f32[16,8,16,128]{3,2,1,0:T(8,128)S(1)} %get-tuple-element.55), channel_id=1, replica_groups=mesh['prow'=16,'pcol'=16] {'prow'}, dimensions={0} | all-to-all | bytes 2097152 | tf_op jit(solution)/shard_map/all_to_all | solution.py:363
  57.6 3.5 %shard_map.67.refs_1_ = f32[64,16,128]{2,1,0:T(8,128)S(1)} custom-call(s32[408]{0:T(512)S(1)} %concatenate.3.refs_0_, f32[16,8,16,128]{3,2,1,0:T(8,128)S(1)} %all_to_all.71.refs_1_, f32[19,1,7,32,512]{4,3,2,1,0:T(8,128)} %refs_3_.9), custom_call_target="tpu_custom_call" | custom-call | tf_op jit(solution)/shard_map/pallas_call | solution.py:348
  65.5 19.1 %all_to_all.72.refs_1_ = f32[8,4,16,128]{3,2,1,0:T(8,128)S(1)} all-to-all(f32[8,4,16,128]{3,2,1,0:T(8,128)S(1)} %shard_map.68), channel_id=1, replica_groups={{0,2,4,6,8,10,12,14},{1,3,5,7,9,11,13,15},{16,18,20,22,24,26,28,30},{17..., dimensions={0} | all-to-all | bytes 524288 | tf_op jit(solution)/shard_map/all_to_all | solution.py:539
  87.0 12.3 %all_to_all.73.refs_1_ = f32[16,4,16,128]{3,2,1,0:T(8,128)S(1)} all-to-all(f32[16,4,16,128]{3,2,1,0:T(8,128)S(1)} %shard_map.69), channel_id=1, replica_groups=mesh['prow'=16,'pcol'=16] {'prow'}, dimensions={0} | all-to-all | bytes 1048576 | tf_op jit(solution)/shard_map/all_to_all | solution.py:363
  102.0 3.6 %all-to-all-start.4 = ((f32[16,4,16,128]{3,2,1,0:T(8,128)}), f32[16,4,16,128]{3,2,1,0:T(8,128)S(1)}, u32[]{:S(2)}, u32[]{:S(2)}) async-start(f32[16,4,16,128]{3,2,1,0:T(8,128)} %get-tuple-element.57), calls=%async_computation.4 | async-start | bytes 1048576 | tf_op jit(solution)/shard_map/all_to_all | solution.py:363
  105.5 4.9 %shard_map.71 = (f32[32,16,128]{2,1,0:T(8,128)S(1)}, f32[16,16,128]{2,1,0:T(8,128)S(1)}, f32[16,16,128]{2,1,0:T(8,128)S(1)}, f32[16,16,128]{2,1,0:T(8,128)S(1)},...) custom-call(s32[408]{0:T(512)S(1)} %concatenate.3.refs_0_, f32[16,8,16,128]{3,2,1,0:T(8,128)S(1)} %all_to_all.71.refs_1_, ...), custom_call_target="tpu_custom_call" | custom-call | tf_op jit(solution)/shard_map/pallas_call | solution.py:348
  110.4 11.3 %all-to-all-done.4.refs_1_ = f32[16,4,16,128]{3,2,1,0:T(8,128)S(1)} async-done(((f32[16,4,16,128]{3,2,1,0:T(8,128)}), f32[16,4,16,128]{3,2,1,0:T(8,128)S(1)}, u32[]{:S(2)}, u32[]{:S(2)}) %all-to-all-start.4) | async-done | bytes 524320 | tf_op jit(solution)/shard_map/all_to_all | solution.py:363
  124.0 4.1 %collective-permute-start.1 = (f32[16,16,128]{2,1,0:T(8,128)S(1)}, f32[16,16,128]{2,1,0:T(8,128)S(1)}, u32[]{:S(2)}, u32[]{:S(2)}) collective-permute-start(f32[16,16,128]{2,1,0:T(8,128)S(1)} %slice.9), channel_id=1, source_target_pairs={{0,1},{1,0},{2,3},{3,2},{4,5},{5,4},{6,7},{7,6},{8,9},{9,8},{10,11... | collective-permute-start | bytes 393224 | tf_op jit(solution)/shard_map/ppermute | solution.py:527
  129.6 10.7 %all_to_all.74.refs_1_ = f32[8,2,16,128]{3,2,1,0:T(8,128)S(1)} all-to-all(f32[8,2,16,128]{3,2,1,0:T(8,128)S(1)} %shard_map.73), channel_id=1, replica_groups={{0,2,4,6,8,10,12,14},{1,3,5,7,9,11,13,15},{16,18,20,22,24,26,28,30},{17..., dimensions={0} | all-to-all | bytes 262144 | tf_op jit(solution)/shard_map/all_to_all | solution.py:539
  141.7 3.5 %all-to-all-start.6 = ((f32[16,2,16,128]{3,2,1,0:T(8,128)}), f32[16,2,16,128]{3,2,1,0:T(8,128)S(1)}, u32[]{:S(2)}, u32[]{:S(2)}) async-start(f32[16,2,16,128]{3,2,1,0:T(8,128)} %shard_map.74), calls=%async_computation.6 | async-start | bytes 524288 | tf_op jit(solution)/shard_map/all_to_all | solution.py:363
  150.4 4.8 %all-to-all-done.6.refs_1_ = f32[16,2,16,128]{3,2,1,0:T(8,128)S(1)} async-done(((f32[16,2,16,128]{3,2,1,0:T(8,128)}), f32[16,2,16,128]{3,2,1,0:T(8,128)S(1)}, u32[]{:S(2)}, u32[]{:S(2)}) %all-to-all-start.6) | async-done | bytes 262176 | tf_op jit(solution)/shard_map/all_to_all | solution.py:363
  157.6 14.7 %all_to_all.75.refs_1_ = f32[16,1,16,128]{3,2,1,0:T(8,128)S(1)} all-to-all(f32[16,1,16,128]{3,2,1,0:T(8,128)S(1)} %bitcast.13), channel_id=1, replica_groups=mesh['prow'=16,'pcol'=16] {'pcol'}, dimensions={0} | all-to-all | bytes 262144 | tf_op jit(solution)/shard_map/all_to_all | solution.py:363
  173.5 3.5 %all-to-all-start.8 = ((f32[16,1,16,128]{3,2,1,0:T(8,128)}), f32[16,1,16,128]{3,2,1,0:T(8,128)S(1)}, u32[]{:S(2)}, u32[]{:S(2)}) async-start(f32[16,1,16,128]{3,2,1,0:T(8,128)} %shard_map.78), calls=%async_computation.8 | async-start | bytes 262144 | tf_op jit(solution)/shard_map/all_to_all | solution.py:363
  181.1 5.1 %all-to-all-done.8.refs_1_ = f32[16,1,16,128]{3,2,1,0:T(8,128)S(1)} async-done(((f32[16,1,16,128]{3,2,1,0:T(8,128)}), f32[16,1,16,128]{3,2,1,0:T(8,128)S(1)}, u32[]{:S(2)}, u32[]{:S(2)}) %all-to-all-start.8) | async-done | bytes 131104 | tf_op jit(solution)/shard_map/all_to_all | solution.py:363
  188.1 12.2 %all_to_all.76.refs_1_ = f32[16,1,16,128]{3,2,1,0:T(8,128)S(1)} all-to-all(f32[16,1,16,128]{3,2,1,0:T(8,128)S(1)} %bitcast.12), channel_id=1, replica_groups=mesh['prow'=16,'pcol'=16] {'pcol'}, dimensions={0} | all-to-all | bytes 262144 | tf_op jit(solution)/shard_map/all_to_all | solution.py:363
  201.5 3.5 %all-to-all-start.10 = ((f32[16,1,16,128]{3,2,1,0:T(8,128)}), f32[16,1,16,128]{3,2,1,0:T(8,128)S(1)}, u32[]{:S(2)}, u32[]{:S(2)}) async-start(f32[16,1,16,128]{3,2,1,0:T(8,128)} %shard_map.82), calls=%async_computation.10 | async-start | bytes 262144 | tf_op jit(solution)/shard_map/all_to_all | solution.py:363
  208.8 3.6 %all-to-all-done.10.refs_1_ = f32[16,1,16,128]{3,2,1,0:T(8,128)S(1)} async-done(((f32[16,1,16,128]{3,2,1,0:T(8,128)}), f32[16,1,16,128]{3,2,1,0:T(8,128)S(1)}, u32[]{:S(2)}, u32[]{:S(2)}) %all-to-all-start.10) | async-done | bytes 131104 | tf_op jit(solution)/shard_map/all_to_all | solution.py:363
  215.4 13.9 %all_to_all.77.refs_1_ = f32[16,8,256]{2,1,0:T(8,128)S(1)} all-to-all(f32[16,8,256]{2,1,0:T(8,128)S(1)} %shard_map.86), channel_id=1, replica_groups=mesh['prow'=16,'pcol'=16] {'pcol'}, dimensions={0} | all-to-all | bytes 262144 | tf_op jit(solution)/shard_map/all_to_all | solution.py:363
  230.6 3.5 %all-to-all-start.12 = ((f32[16,8,256]{2,1,0:T(8,128)}), f32[16,8,256]{2,1,0:T(8,128)S(1)}, u32[]{:S(2)}, u32[]{:S(2)}) async-start(f32[16,8,256]{2,1,0:T(8,128)} %shard_map.87), calls=%async_computation.12 | async-start | bytes 262144 | tf_op jit(solution)/shard_map/all_to_all | solution.py:363
  234.2 3.9 %shard_map.88.refs_4_ = f32[5,512,256]{2,1,0:T(8,128)S(1)} custom-call(s32[408]{0:T(512)S(1)} %concatenate.3.refs_0_, f32[16,17,32,256]{3,2,1,0:T(8,128)} %bitcast.20), custom_call_target="tpu_custom_call" | custom-call | tf_op jit(solution)/shard_map/pallas_call | solution.py:348
  238.1 3.4 %all-to-all-done.12.refs_1_ = f32[16,8,256]{2,1,0:T(8,128)S(1)} async-done(((f32[16,8,256]{2,1,0:T(8,128)}), f32[16,8,256]{2,1,0:T(8,128)S(1)}, u32[]{:S(2)}, u32[]{:S(2)}) %all-to-all-start.12) | async-done | bytes 131104 | tf_op jit(solution)/shard_map/all_to_all | solution.py:363
  241.5 4.3 %shard_map.89 = (f32[16,8,128]{2,1,0:T(8,128)S(1)}, f32[3,8,512]{2,1,0:T(8,128)S(1)}) custom-call(s32[408]{0:T(512)S(1)} %concatenate.3.refs_0_, f32[16,8,256]{2,1,0:T(8,128)S(1)} %all-to-all-done.12.refs_1_, f32[16,17,32,256]{3,2,1,0:T(8,128)} %bitcast.21), custom_call_target="tpu_custom_call" | custom-call | tf_op jit(solution)/shard_map/pallas_call | solution.py:348
  250.8 10.6 %all_to_all.78.refs_1_ = f32[16,8,128]{2,1,0:T(8,128)S(1)} all-to-all(f32[16,8,128]{2,1,0:T(8,128)S(1)} %shard_map.91), channel_id=1, replica_groups=mesh['prow'=16,'pcol'=16] {'pcol'}, dimensions={0} | all-to-all | bytes 131072 | tf_op jit(solution)/shard_map/all_to_all | solution.py:363
  (46 shorter events, 53.6 us)
Async XLA Ops:
  6.5 92.7 %all-gather.7.cloned.1.call-start = ((), (), s32[]{:S(2)}) async-start(), calls=%async_computation.14 | async-start | bytes 6684672 | tf_op jit(solution)/shard_map/all_gather | solution.py:396
  11.0 137.1 %all-gather.9.cloned.1.call-start = ((), (), s32[]{:S(2)}) async-start(), calls=%async_computation.15 | async-start | bytes 4456448 | tf_op jit(solution)/shard_map/all_gather | solution.py:449
  37.9 196.2 %all-gather.11.cloned.1.call-start = ((), (), s32[]{:S(2)}) async-start(), calls=%async_computation.16 | async-start | bytes 9469952 | tf_op jit(solution)/shard_map/all_gather | solution.py:467
  61.1 3.7 %collective-permute-start = (f32[32,16,128]{2,1,0:T(8,128)S(1)}, f32[32,16,128]{2,1,0:T(8,128)S(1)}, u32[]{:S(2)}, u32[]{:S(2)}) collective-permute-start(f32[32,16,128]{2,1,0:T(8,128)S(1)} %slice.8), channel_id=1, source_target_pairs={{0,1},{1,0},{2,3},{3,2},{4,5},{5,4},{6,7},{7,6},{8,9},{9,8},{10,11... | collective-permute-start | bytes 786440 | tf_op jit(solution)/shard_map/ppermute | solution.py:527
  102.0 19.8 %all-to-all-start.4 = ((f32[16,4,16,128]{3,2,1,0:T(8,128)}), f32[16,4,16,128]{3,2,1,0:T(8,128)S(1)}, u32[]{:S(2)}, u32[]{:S(2)}) async-start(f32[16,4,16,128]{3,2,1,0:T(8,128)} %get-tuple-element.57), calls=%async_computation.4 | async-start | bytes 1048576 | tf_op jit(solution)/shard_map/all_to_all | solution.py:363
  124.0 5.1 %collective-permute-start.1 = (f32[16,16,128]{2,1,0:T(8,128)S(1)}, f32[16,16,128]{2,1,0:T(8,128)S(1)}, u32[]{:S(2)}, u32[]{:S(2)}) collective-permute-start(f32[16,16,128]{2,1,0:T(8,128)S(1)} %slice.9), channel_id=1, source_target_pairs={{0,1},{1,0},{2,3},{3,2},{4,5},{5,4},{6,7},{7,6},{8,9},{9,8},{10,11... | collective-permute-start | bytes 393224 | tf_op jit(solution)/shard_map/ppermute | solution.py:527
  141.7 13.6 %all-to-all-start.6 = ((f32[16,2,16,128]{3,2,1,0:T(8,128)}), f32[16,2,16,128]{3,2,1,0:T(8,128)S(1)}, u32[]{:S(2)}, u32[]{:S(2)}) async-start(f32[16,2,16,128]{3,2,1,0:T(8,128)} %shard_map.74), calls=%async_computation.6 | async-start | bytes 524288 | tf_op jit(solution)/shard_map/all_to_all | solution.py:363
  173.5 12.7 %all-to-all-start.8 = ((f32[16,1,16,128]{3,2,1,0:T(8,128)}), f32[16,1,16,128]{3,2,1,0:T(8,128)S(1)}, u32[]{:S(2)}, u32[]{:S(2)}) async-start(f32[16,1,16,128]{3,2,1,0:T(8,128)} %shard_map.78), calls=%async_computation.8 | async-start | bytes 262144 | tf_op jit(solution)/shard_map/all_to_all | solution.py:363
  201.5 10.9 %all-to-all-start.10 = ((f32[16,1,16,128]{3,2,1,0:T(8,128)}), f32[16,1,16,128]{3,2,1,0:T(8,128)S(1)}, u32[]{:S(2)}, u32[]{:S(2)}) async-start(f32[16,1,16,128]{3,2,1,0:T(8,128)} %shard_map.82), calls=%async_computation.10 | async-start | bytes 262144 | tf_op jit(solution)/shard_map/all_to_all | solution.py:363
  230.6 10.9 %all-to-all-start.12 = ((f32[16,8,256]{2,1,0:T(8,128)}), f32[16,8,256]{2,1,0:T(8,128)S(1)}, u32[]{:S(2)}, u32[]{:S(2)}) async-start(f32[16,8,256]{2,1,0:T(8,128)} %shard_map.87), calls=%async_computation.12 | async-start | bytes 262144 | tf_op jit(solution)/shard_map/all_to_all | solution.py:363
  245.8 1.8 collective-permute-start.2
  248.6 1.3 collective-permute-start.3
Sparse Core Ops, SparseCore 0:
  11.1 50.2 all-gather.6
  63.9 60.1 all-gather.8
  126.5 82.3 all-gather.10
